TPU v7x, 128 devices: a whole 4x4x4 slice. The times are simulated.
128 devices in a mesh: outer: 8 (over z, y_hi), inner: 16 (over x, y_lo, core).
Axes of the slice: x: 4, y: 4 (y_hi: 2, y_lo: 2; y = y_hi * 2 + y_lo), z: 4, core: 2. Of those that a mesh axis runs over, the one named last changes fastest.
Arguments:
- queries: bfloat16 [131072, 1024], P(('outer', 'inner')), may hold values from -180 to 180
- keys: bfloat16 [131072, 1024], P(('outer', 'inner')), may hold values from -6 to 6
- values: bfloat16 [131072, 1024], P(('outer', 'inner')), may hold values from -48 to 48
- out_grad: bfloat16 [131072, 1024], P(('outer', 'inner')), may hold values from -192 to 192
- middle_head_offsets: int32 [8], replicated, may hold values from 0 to 31
- distant_head_offsets: int32 [8], replicated, may hold values from 0 to 511
Outputs:
- attended: bfloat16 [131072, 1024], P(('outer', 'inner'))
- grad_q: bfloat16 [131072, 1024], P(('outer', 'inner'))
- grad_k: bfloat16 [131072, 1024], P(('outer', 'inner'))
- grad_v: bfloat16 [131072, 1024], P(('outer', 'inner'))
All inputs are finite; a program needn't handle non-finite values.
Results may differ from a plain program's by a relative error of at most 0.0075.
The roundings to bfloat16 on the way count: a program that leaves them out, or rounds other values in their place, can miss the bound.
Values may be sent and summed in bfloat16 or wider, within the bound.
No kernel may reach another device: no remote copies, remote signals or barrier semaphores. Data moves between devices by JAX's collectives and lax.ppermute only.
A program may use at most 192 MiB of HBM per device.

v0:
```python
import jax
import jax.numpy as jnp
from jax import lax
from jax.sharding import PartitionSpec as P

SEG1 = 512
DILATION_TWO = 32
DILATION_THREE = 512


def gather_rows(source, stride, offsets):
    number_of_heads = offsets.shape[0]
    shaped = source.reshape((source.shape[0] // stride, stride) + source.shape[1:])
    chosen = lax.broadcasted_iota(jnp.int32, (stride, number_of_heads), 0) == offsets[None, :]
    chosen = chosen.reshape((1, stride, number_of_heads) + (1,) * (source.ndim - 2))
    return jnp.sum(jnp.where(chosen, shaped, jnp.zeros((), source.dtype)), axis=1)


def insert_rows(source, stride, offsets):
    number_of_heads = offsets.shape[0]
    chosen = lax.broadcasted_iota(jnp.int32, (stride, number_of_heads), 0) == offsets[None, :]
    chosen = chosen.reshape((1, stride, number_of_heads) + (1,) * (source.ndim - 2))
    spread = jnp.where(chosen, source[:, None], jnp.zeros((), source.dtype))
    return spread.reshape((source.shape[0] * stride,) + source.shape[1:])


def coverage_count(number_of_rows, stride, offsets):
    position = lax.broadcasted_iota(jnp.int32, (number_of_rows, offsets.shape[0]), 0)
    return position % stride == offsets[None, :]


def attend(q_part, k_part, v_part):
    factor = q_part.shape[-1] ** (-0.5)
    scores = (
        jnp.einsum("gqhe,gkhe->ghqk", q_part, k_part, preferred_element_type=jnp.float32) * factor
    )
    highest = jnp.max(scores, axis=-1, keepdims=True)
    exponent = jnp.exp(scores - highest)
    denominator = jnp.sum(exponent, axis=-1)
    weights = exponent.astype(jnp.bfloat16)
    blended = jnp.einsum("ghqk,gkhe->gqhe", weights, v_part, preferred_element_type=jnp.float32)
    blended = blended / jnp.transpose(denominator, (0, 2, 1))[..., None]
    log_sum = jnp.transpose(highest[..., 0] + jnp.log(denominator), (0, 2, 1))
    return (blended, log_sum)


def gradients(q_part, k_part, v_part, g_part, combined_logsumexp, delta_per_row):
    factor = q_part.shape[-1] ** (-0.5)
    scores = (
        jnp.einsum("gqhe,gkhe->ghqk", q_part, k_part, preferred_element_type=jnp.float32) * factor
    )
    chances = jnp.exp(scores - jnp.transpose(combined_logsumexp, (0, 2, 1))[..., None])
    chance_low = chances.astype(jnp.bfloat16)
    grad_prob = jnp.einsum("gqhe,gkhe->ghqk", g_part, v_part, preferred_element_type=jnp.float32)
    dscore = (chances * (grad_prob - jnp.transpose(delta_per_row, (0, 2, 1))[..., None])).astype(
        jnp.bfloat16
    )
    grad_v = jnp.einsum("ghqk,gqhe->gkhe", chance_low, g_part, preferred_element_type=jnp.float32)
    grad_k = (
        jnp.einsum("ghqk,gqhe->gkhe", dscore, q_part, preferred_element_type=jnp.float32) * factor
    )
    grad_q = (
        jnp.einsum("ghqk,gkhe->gqhe", dscore, k_part, preferred_element_type=jnp.float32) * factor
    )
    return (grad_q, grad_k, grad_v)


def combine(lse_one, middle_logsumexp, middle_coverage, distant_logsumexp, distant_coverage):
    highest = jnp.maximum(
        lse_one,
        jnp.maximum(
            jnp.where(middle_coverage, middle_logsumexp, lse_one),
            jnp.where(distant_coverage, distant_logsumexp, lse_one),
        ),
    )
    summed = jnp.exp(lse_one - highest)
    summed = summed + jnp.where(
        middle_coverage, jnp.exp(jnp.where(middle_coverage, middle_logsumexp - highest, 0.0)), 0.0
    )
    summed = summed + jnp.where(
        distant_coverage,
        jnp.exp(jnp.where(distant_coverage, distant_logsumexp - highest, 0.0)),
        0.0,
    )
    return highest + jnp.log(summed)


def share(log_sum, cover, combined_logsumexp):
    return jnp.where(cover, jnp.exp(jnp.where(cover, log_sum - combined_logsumexp, 0.0)), 0.0)


def body(queries, keys, values, out_grad, middle_head_offsets, distant_head_offsets):
    number_of_rows = queries.shape[0]
    number_of_heads = middle_head_offsets.shape[0]
    per_head_width = queries.shape[1] // number_of_heads
    split_shape = (number_of_rows, number_of_heads, per_head_width)
    query_sections = queries.reshape(split_shape)
    key_sections = keys.reshape(split_shape)
    value_sections = values.reshape(split_shape)
    gradient_sections = out_grad.reshape(split_shape)
    block_shape = (number_of_rows // SEG1, SEG1, number_of_heads, per_head_width)
    stat_shape = (number_of_rows // SEG1, SEG1, number_of_heads)
    out_one, lse_one = attend(
        query_sections.reshape(block_shape),
        key_sections.reshape(block_shape),
        value_sections.reshape(block_shape),
    )
    out_one = out_one.reshape(split_shape)
    lse_one = lse_one.reshape(number_of_rows, number_of_heads)
    middle_query_rows = gather_rows(query_sections, DILATION_TWO, middle_head_offsets)
    middle_key_rows = gather_rows(key_sections, DILATION_TWO, middle_head_offsets)
    middle_value_rows = gather_rows(value_sections, DILATION_TWO, middle_head_offsets)
    distant_query_rows = gather_rows(query_sections, DILATION_THREE, distant_head_offsets)
    distant_key_rows = gather_rows(key_sections, DILATION_THREE, distant_head_offsets)
    distant_value_rows = gather_rows(value_sections, DILATION_THREE, distant_head_offsets)
    k_mid_all, v_mid_all = (
        lax.all_gather(middle_key_rows, "inner", axis=0, tiled=True),
        lax.all_gather(middle_value_rows, "inner", axis=0, tiled=True),
    )
    k_far_all, v_far_all = (
        lax.all_gather(distant_key_rows, ("outer", "inner"), axis=0, tiled=True),
        lax.all_gather(distant_value_rows, ("outer", "inner"), axis=0, tiled=True),
    )
    middle_output, middle_logsumexp = attend(
        middle_query_rows[None], k_mid_all[None], v_mid_all[None]
    )
    distant_output, distant_logsumexp = attend(
        distant_query_rows[None], k_far_all[None], v_far_all[None]
    )
    middle_output_full = insert_rows(middle_output[0], DILATION_TWO, middle_head_offsets)
    middle_logsumexp_full = insert_rows(middle_logsumexp[0], DILATION_TWO, middle_head_offsets)
    distant_output_full = insert_rows(distant_output[0], DILATION_THREE, distant_head_offsets)
    distant_logsumexp_full = insert_rows(distant_logsumexp[0], DILATION_THREE, distant_head_offsets)
    cover_one = coverage_count(number_of_rows, 1, jnp.zeros((number_of_heads,), jnp.int32))
    middle_coverage = coverage_count(number_of_rows, DILATION_TWO, middle_head_offsets)
    distant_coverage = coverage_count(number_of_rows, DILATION_THREE, distant_head_offsets)
    combined_logsumexp = combine(
        lse_one, middle_logsumexp_full, middle_coverage, distant_logsumexp_full, distant_coverage
    )
    blended = share(lse_one, cover_one, combined_logsumexp)[..., None] * out_one
    blended = (
        blended
        + share(middle_logsumexp_full, middle_coverage, combined_logsumexp)[..., None]
        * middle_output_full
    )
    blended = (
        blended
        + share(distant_logsumexp_full, distant_coverage, combined_logsumexp)[..., None]
        * distant_output_full
    )
    attended = blended.astype(jnp.bfloat16)
    delta_per_row = jnp.sum(
        gradient_sections.astype(jnp.float32) * attended.astype(jnp.float32), axis=-1
    )
    dq_one, dk_one, dv_one = gradients(
        query_sections.reshape(block_shape),
        key_sections.reshape(block_shape),
        value_sections.reshape(block_shape),
        gradient_sections.reshape(block_shape),
        combined_logsumexp.reshape(stat_shape),
        delta_per_row.reshape(stat_shape),
    )
    middle_output_gradient = gather_rows(gradient_sections, DILATION_TWO, middle_head_offsets)
    distant_output_gradient = gather_rows(gradient_sections, DILATION_THREE, distant_head_offsets)
    middle_total = gather_rows(combined_logsumexp, DILATION_TWO, middle_head_offsets)
    middle_delta = gather_rows(delta_per_row, DILATION_TWO, middle_head_offsets)
    distant_total = gather_rows(combined_logsumexp, DILATION_THREE, distant_head_offsets)
    distant_delta = gather_rows(delta_per_row, DILATION_THREE, distant_head_offsets)
    mid_results = gradients(
        middle_query_rows[None],
        k_mid_all[None],
        v_mid_all[None],
        middle_output_gradient[None],
        middle_total[None],
        middle_delta[None],
    )
    far_results = gradients(
        distant_query_rows[None],
        k_far_all[None],
        v_far_all[None],
        distant_output_gradient[None],
        distant_total[None],
        distant_delta[None],
    )
    dk_mid, dv_mid = (
        lax.psum_scatter(mid_results[1][0], "inner", scatter_dimension=0, tiled=True),
        lax.psum_scatter(mid_results[2][0], "inner", scatter_dimension=0, tiled=True),
    )
    dk_far, dv_far = (
        lax.psum_scatter(far_results[1][0], ("outer", "inner"), scatter_dimension=0, tiled=True),
        lax.psum_scatter(far_results[2][0], ("outer", "inner"), scatter_dimension=0, tiled=True),
    )

    def merge_three(one_part, middle_portion, distant_portion):
        complete_sequence = one_part.reshape(split_shape)
        complete_sequence = complete_sequence + insert_rows(
            middle_portion, DILATION_TWO, middle_head_offsets
        )
        complete_sequence = complete_sequence + insert_rows(
            distant_portion, DILATION_THREE, distant_head_offsets
        )
        return complete_sequence.astype(jnp.bfloat16).reshape(
            number_of_rows, number_of_heads * per_head_width
        )

    return (
        attended.reshape(number_of_rows, number_of_heads * per_head_width),
        merge_three(dq_one, mid_results[0][0], far_results[0][0]),
        merge_three(dk_one, dk_mid, dk_far),
        merge_three(dv_one, dv_mid, dv_far),
    )


def solution(mesh):
    in_specs = (
        P(("outer", "inner"), None),
        P(("outer", "inner"), None),
        P(("outer", "inner"), None),
        P(("outer", "inner"), None),
        P(),
        P(),
    )
    out_specs = (
        P(("outer", "inner"), None),
        P(("outer", "inner"), None),
        P(("outer", "inner"), None),
        P(("outer", "inner"), None),
    )
    return jax.shard_map(body, mesh=mesh, in_specs=in_specs, out_specs=out_specs, check_vma=False)
```

profile of v0, /device:TPU:1, one launch (start us, length us, event | category | flops | bytes accessed | tf_op | source)
XLA Modules:
  0.0 1930.3 jit_solution(14788931150368322517)
XLA Ops:
  7.2 3.7 copy.141
  15.6 5.6 fusion.35
  22.7 4.0 convert_bitcast_fusion
  27.6 5.2 select_reduce_fusion
  32.8 181.7 %all_gather.13 = bf16[256,8,128]{2,1,0:T(8,128)(2,1)S(1)} all-gather(bf16[2,8,128]{2,1,0:T(8,128)(2,1)S(1)} %get-tuple-element.5), channel_id=1, replica_groups=mesh['outer'=8,'inner'=16] {'outer','inner'}, dimensions={0}, use_global_device_ids=true | all-gather | bytes 528384 | tf_op jit(solution)/shard_map/all_gather | solution.py:121
  215.9 10.3 multiply_reduce_fusion
  226.3 8.6 fusion.1
  235.1 172.1 %all_gather.15 = bf16[256,8,128]{2,1,0:T(8,128)(2,1)S(1)} all-gather(bf16[2,8,128]{2,1,0:T(8,128)(2,1)S(1)} %get-tuple-element.6), channel_id=1, replica_groups=mesh['outer'=8,'inner'=16] {'outer','inner'}, dimensions={0}, use_global_device_ids=true | all-gather | bytes 528384 | tf_op jit(solution)/shard_map/all_gather | solution.py:122
  408.1 9.7 bitcast_divide_fusion
  417.8 4.4 copy.88
  422.7 5.2 copy.151
  443.5 8.3 fusion.27
  460.0 2.6 copy.125
  462.6 11.5 reduce-scatter.11.cloned.1.call-start
  475.5 2.5 copy.131
  481.6 2.9 copy.123
  486.4 2.9 copy.129
  489.3 8.9 multiply_convert_fusion
  498.2 4.6 multiply_bitcast_fusion.1
  502.8 6.7 copy.107
  511.9 4.4 copy.121
  516.9 7.5 fusion.32
  524.4 4.4 copy.127
  528.8 560.7 %reduce-scatter.7.cloned.1.call-done = f32[2,8,128]{2,1,0:T(8,128)} async-done(((f32[256,8,128]{2,1,0:T(8,128)}), f32[2,8,128]{2,1,0:T(8,128)}) %reduce-scatter.7.cloned.1.call-update) | async-done | bytes 8208 | tf_op jit(solution)/shard_map/reduce_scatter | solution.py:190
  1089.4 635.0 %reduce-scatter.11.cloned.1.call-done = f32[2,8,128]{2,1,0:T(8,128)} async-done(((f32[256,8,128]{2,1,0:T(8,128)}), f32[2,8,128]{2,1,0:T(8,128)}) %reduce-scatter.11.cloned.1.call-update) | async-done | bytes 8208 | tf_op jit(solution)/shard_map/reduce_scatter | solution.py:191
  1724.4 63.0 %reduce-scatter.5.cloned.1.call-done = f32[32,8,128]{2,1,0:T(8,128)} async-done(((f32[512,8,128]{2,1,0:T(8,128)}), f32[32,8,128]{2,1,0:T(8,128)}) %reduce-scatter.5.cloned.1.call-update) | async-done | bytes 131088 | tf_op jit(solution)/shard_map/reduce_scatter | solution.py:186
  1787.4 64.6 %reduce-scatter.9.cloned.1.call-done = f32[32,8,128]{2,1,0:T(8,128)} async-done(((f32[512,8,128]{2,1,0:T(8,128)}), f32[32,8,128]{2,1,0:T(8,128)}) %reduce-scatter.9.cloned.1.call-update) | async-done | bytes 131088 | tf_op jit(solution)/shard_map/reduce_scatter | solution.py:187
  1865.5 2.5 mul.133
  1870.5 2.7 mul.130
  1877.9 3.2 broadcast_in_dim.361
  1881.0 3.2 broadcast_in_dim.355
  1884.2 38.8 %fusion.12 = (bf16[1024,1024]{1,0:T(8,128)(2,1)}, bf16[1024,1024]{1,0:T(8,128)(2,1)}, bf16[1024,1024]{1,0:T(8,128)(2,1)}, bf16[1024,1024]{1,0:T(8,128)(2,1)}) fusion(f32[128,8,8,128]{3,2,1,0:T(8,128)} %bitcast.347, f32[128,8,8,128]{3,2,1,0:T(8,128)} %bitcast.346, f32[128,8,8,128]{3,2,1,0:T(8,128)} %bitcast.341, pred[128,8,8,128]{3,2,1,0:T(8,128)(4,1)S(1)} %bitcast.356, ...), kind=kLoop, calls=%fused_computation.15 | loop fusion | flops 24117248 | bytes 73400320 | tf_op jit(solution)/shard_map/convert_element_type | solution.py:202
  (185 shorter events, 64.0 us)
Async XLA Ops:
  7.2 426.2 %all-gather.3.cloned.1.call-start = ((), (), s32[]{:S(2)}) async-start(), calls=%async_computation.4 | async-start | bytes 1114112 | tf_op jit(solution)/shard_map/all_gather | solution.py:117
  7.2 5.7 copy-start.11
  15.5 219.3 %copy-start.40 = (pred[32,8]{0,1:T(8,128)(4,1)}, pred[32,8]{0,1:T(8,128)(4,1)S(1)}, u32[]{:S(2)}) copy-start(pred[32,8]{0,1:T(8,128)(4,1)S(1)} %iota_compare_fusion.1) | copy-start | bytes 772
  21.2 6.1 copy-start.39
  21.9 419.9 %all-gather.5.cloned.1.call-start = ((), (), s32[]{:S(2)}) async-start(), calls=%async_computation.5 | async-start | bytes 1114112 | tf_op jit(solution)/shard_map/all_gather | solution.py:118
  22.7 1066.8 %reduce-scatter.7.cloned.1.call-start = ((), (), s32[]{:S(2)}) async-start(), calls=%async_computation.7 | async-start | bytes 1056768 | tf_op jit(solution)/shard_map/reduce_scatter | solution.py:190
  27.4 402.1 %copy-start.25 = (pred[512,8]{0,1:T(8,128)(4,1)}, pred[512,8]{0,1:T(8,128)(4,1)S(1)}, u32[]{:S(2)}) copy-start(pred[512,8]{0,1:T(8,128)(4,1)S(1)} %iota_compare_fusion) | copy-start | bytes 12292
  32.8 193.5 %copy-start.36 = (bf16[2,8,128]{2,1,0:T(8,128)(2,1)}, bf16[2,8,128]{2,1,0:T(8,128)(2,1)S(1)}, u32[]{:S(2)}) copy-start(bf16[2,8,128]{2,1,0:T(8,128)(2,1)S(1)} %get-tuple-element.7) | copy-start | bytes 12292
  215.6 191.7 %copy-start.30 = (f32[8,2,256]{2,1,0:T(2,128)}, f32[8,2,256]{2,1,0:T(2,128)S(1)}, u32[]{:S(2)}) copy-start(f32[8,2,256]{2,1,0:T(2,128)S(1)} %get-tuple-element.29) | copy-start | bytes 49156
  235.0 202.1 %copy-start.38 = (f32[2,8]{1,0:T(2,128)}, f32[2,8]{1,0:T(2,128)S(1)}, u32[]{:S(2)}) copy-start(f32[2,8]{1,0:T(2,128)S(1)} %fusion.120) | copy-start | bytes 196
  422.5 21.0 %copy-start.12 = (pred[1024,8]{1,0:T(8,128)(4,1)}, pred[1024,8]{1,0:T(8,128)(4,1)S(1)}, u32[]{:S(2)}) copy-start(pred[1024,8]{1,0:T(8,128)(4,1)S(1)} %copy.94) | copy-start | bytes 24580
  427.9 15.5 copy-start.27
  439.0 12.8 copy-start.5
  443.5 8.4 copy-start.14
  443.5 8.4 copy-start.3
  451.9 5.5 copy-start.35
  451.9 6.8 copy-start.37
  454.7 19.4 %copy-start.31 = (f32[8,2,256]{2,1,0:T(2,128)S(1)}, f32[8,2,256]{2,1,0:T(2,128)}, u32[]{:S(2)}) copy-start(f32[8,2,256]{2,1,0:T(2,128)} %copy-done.30) | copy-start | bytes 49156
  458.7 19.3 %copy-start.43 = (bf16[8,2,256]{2,1,0:T(2,128)(2,1)}, bf16[8,2,256]{2,1,0:T(2,128)(2,1)S(1)}, u32[]{:S(2)}) copy-start(bf16[8,2,256]{2,1,0:T(2,128)(2,1)S(1)} %fusion.55) | copy-start | bytes 24580
  458.7 19.4 %copy-start.16 = (bf16[32,8,128]{2,1,0:T(8,128)(2,1)S(1)}, bf16[32,8,128]{2,1,0:T(8,128)(2,1)}, u32[]{:S(2)}) copy-start(bf16[32,8,128]{2,1,0:T(8,128)(2,1)} %get-tuple-element.8) | copy-start | bytes 196612
  462.6 1261.8 %reduce-scatter.11.cloned.1.call-start = ((), (), s32[]{:S(2)}) async-start(), calls=%async_computation.9 | async-start | bytes 1056768 | tf_op jit(solution)/shard_map/reduce_scatter | solution.py:191
  478.0 1309.3 %reduce-scatter.5.cloned.1.call-start = ((), (), s32[]{:S(2)}) async-start(), calls=%async_computation.6 | async-start | bytes 2228224 | tf_op jit(solution)/shard_map/reduce_scatter | solution.py:186
  484.5 4.8 copy-start.21
  484.5 1367.5 %reduce-scatter.9.cloned.1.call-start = ((), (), s32[]{:S(2)}) async-start(), calls=%async_computation.8 | async-start | bytes 2228224 | tf_op jit(solution)/shard_map/reduce_scatter | solution.py:187
  489.3 8.9 copy-start
  502.8 6.7 copy-start.2
  511.9 4.8 copy-start.18
  1787.4 66.9 %copy-start.22 = (f32[32,8,128]{2,1,0:T(8,128)S(1)}, f32[32,8,128]{2,1,0:T(8,128)}, u32[]{:S(2)}) copy-start(f32[32,8,128]{2,1,0:T(8,128)} %reduce-scatter.5.cloned.1.call-done) | copy-start | bytes 393220
  1865.5 5.1 copy-start.8
  1868.0 5.2 copy-start.28
  1870.5 4.9 copy-start.15
  1875.4 8.8 copy-start.1
  (20 other events, 63.3 us)
Sparse Core Ops, SparseCore 0:
  22.0 35.9 all-gather.2
  59.7 32.4 all-gather.4
  462.7 626.6 reduce-scatter.6
  1091.7 632.6 reduce-scatter.10
  1726.6 60.6 reduce-scatter.4
  1789.6 62.3 reduce-scatter.8
where the time goes:
time: 1940 us; the launch traced here: 1930 us
  waiting for transfers between devices  1320 us (68%)
  blocking collectives  354 us (18%)
  local copies, waits for them, and re-layouts  90.4 us (5%)
  other arithmetic  79.1 us (4%)
  matrix products  56.9 us (3%)
    reduce_scatter x1, waiting for transfers between devices, body(): lax.psum_scatter(far_results[2][0], ('outer', 'inner'), scatter_dimension...  635 us
    reduce_scatter x1, waiting for transfers between devices, body(): lax.psum_scatter(far_results[1][0], ('outer', 'inner'), scatter_dimension...  561 us
    all_gather x1, blocking collectives, body(): lax.all_gather(distant_key_rows, ('outer', 'inner'), axis=0, tiled=True)  182 us
    all_gather x1, blocking collectives, body(): lax.all_gather(distant_value_rows, ('outer', 'inner'), axis=0, tiled=True)  172 us
    reduce_scatter x1, waiting for transfers between devices, body(): lax.psum_scatter(mid_results[2][0], 'inner', scatter_dimension=0, tiled=T...  64.6 us
    reduce_scatter x1, waiting for transfers between devices, body(): lax.psum_scatter(mid_results[1][0], 'inner', scatter_dimension=0, tiled=T...  63 us
    convert_element_type x1, other arithmetic, merge_three(): complete_sequence.astype(jnp.bfloat16)  38.8 us
  transfers between devices with their start and end apart: 6, of which 4 were waited for; matrix products, arithmetic and copies ran while one was open for 6% of the time, Pallas kernels for 0%

commit v1 on v0

v1 whole, which is shorter than its diff:
```python
import math

import jax
import jax.numpy as jnp
from jax import lax
from jax.experimental import pallas as pl
from jax.experimental.pallas import tpu as pltpu
from jax.sharding import PartitionSpec as P

SEG1 = 512
DILATION_TWO = 32
DILATION_THREE = 512
HEADS = 8
WIDTH = 128
FACTOR = WIDTH ** (-0.5)
MID = SEG1 // DILATION_TWO
COV = 32
PACK = 128
KEPT = 7
EXTRACT_HEADS = 2
FINISH_HEADS = 2
VMEM = 60 * 2**20
NEG = -1e30
F32 = jnp.float32
BF16 = jnp.bfloat16


def dot_nn(a, b):
    return lax.dot_general(a, b, (((1,), (0,)), ((), ())), preferred_element_type=F32)


def dot_nt(a, b):
    return lax.dot_general(a, b, (((1,), (1,)), ((), ())), preferred_element_type=F32)


def dot_tn(a, b):
    return lax.dot_general(a, b, (((0,), (0,)), ((), ())), preferred_element_type=F32)


def iota(shape, dim):
    return lax.broadcasted_iota(jnp.int32, shape, dim)


def split3(x):
    high = x.astype(BF16).astype(F32)
    rest = x - high
    middle = rest.astype(BF16).astype(F32)
    return high, middle, (rest - middle).astype(BF16).astype(F32)


def lanes(columns, rows):
    lane = iota((rows, WIDTH), 1)
    out = jnp.zeros((rows, WIDTH), F32)
    for j, column in enumerate(columns):
        out = jnp.where(lane == j, column, out)
    return out


def join3(x, at):
    return x[:, at : at + 1] + x[:, at + 1 : at + 2] + x[:, at + 2 : at + 3]


def targets(shape, dim, off_two, off_three):
    j = iota(shape, dim)
    return jnp.where(j < MID, DILATION_TWO * j + off_two, jnp.where(j == MID, off_three, -1))


def far_rows_kernel(off3_ref, k_ref, v_ref, out_ref, slab, sems):
    copies = []
    for head in range(HEADS):
        start = pl.multiple_of((off3_ref[head] // 16) * 16, 16)
        for j in range(4):
            source = (k_ref, v_ref)[j // 2]
            copies.append(
                pltpu.make_async_copy(
                    source.at[pl.ds((j % 2) * SEG1 + start, 16), pl.ds(head * WIDTH, WIDTH)],
                    slab.at[4 * head + j],
                    sems.at[4 * head + j],
                )
            )
    for copy in copies:
        copy.start()
    for copy in copies:
        copy.wait()
    picked = []
    for head in range(HEADS):
        inside = iota((16, 1), 0) == off3_ref[head] % 16
        for j in range(4):
            picked.append(
                jnp.sum(jnp.where(inside, slab[4 * head + j].astype(F32), 0.0), axis=0, keepdims=True)
            )
    rows = jnp.concatenate(picked, 0).astype(BF16)
    for o in range(out_ref.shape[0]):
        out_ref[o] = rows


def far_rows(off3, k, v, copies):
    return pl.pallas_call(
        far_rows_kernel,
        in_specs=[pl.BlockSpec(memory_space=pltpu.SMEM)] + [pl.BlockSpec(memory_space=pl.ANY)] * 2,
        out_specs=pl.BlockSpec(memory_space=pltpu.VMEM),
        out_shape=jax.ShapeDtypeStruct((copies, 4 * HEADS, WIDTH), BF16),
        scratch_shapes=[
            pltpu.VMEM((4 * HEADS, 16, WIDTH), BF16),
            pltpu.SemaphoreType.DMA((4 * HEADS,)),
        ],
        compiler_params=pltpu.CompilerParams(vmem_limit_bytes=VMEM),
        cost_estimate=pl.CostEstimate(flops=2**18, bytes_accessed=2**18, transcendentals=0),
        name="far_rows",
    )(off3, k, v)


def extract_kernel(
    off2_ref, off3_ref, q_ref, k_ref, v_ref, g_ref, send_ref, cov_ref, left_ref
):
    cells = [(i, t) for i in range(EXTRACT_HEADS) for t in range(2)]

    def block(ref, cell):
        i, t = cell
        return ref[t * SEG1 : (t + 1) * SEG1, i * WIDTH : (i + 1) * WIDTH]

    selects, valids = [], []
    row = iota((COV, 1), 0)
    for i in range(EXTRACT_HEADS):
        head = pl.program_id(0) * EXTRACT_HEADS + i
        off_two, off_three = off2_ref[head], off3_ref[head]
        position = targets((COV, 1), 0, off_two, off_three)
        selects.append((iota((COV, SEG1), 1) == position).astype(BF16))
        twice = (off_three % DILATION_TWO) == off_two
        valids.append(((row < MID) | ((row == MID) & jnp.logical_not(twice))).astype(F32))
    picked = [
        dot_nn(selects[cell[0]], jnp.concatenate([block(r, cell) for r in (q_ref, k_ref, v_ref, g_ref)], 1))
        for cell in cells
    ]
    low = [x.astype(BF16) for x in picked]
    scores = [dot_nt(x[:, :WIDTH], block(k_ref, cell)) for x, cell in zip(low, cells)]
    grads = [dot_nt(x[:, 3 * WIDTH :], block(v_ref, cell)) for x, cell in zip(low, cells)]
    scores, grads = jnp.concatenate(scores, 0) * FACTOR, jnp.concatenate(grads, 0)
    top = jnp.max(scores, axis=1, keepdims=True)
    weight = jnp.exp(scores - top)
    total = jnp.sum(weight, axis=1, keepdims=True)
    weight_low = weight.astype(BF16)
    out = jnp.concatenate(
        [dot_nn(weight_low[n * COV : (n + 1) * COV], block(v_ref, cell)) for n, cell in enumerate(cells)], 0
    ) / total
    lse = top + jnp.log(total)
    g_cov = jnp.concatenate([x[:, 3 * WIDTH :] for x in picked], 0)
    delta = jnp.sum(g_cov * out, axis=1, keepdims=True)
    stats = lanes(split3(lse) + split3(delta), COV * len(cells))
    prob = weight * (jnp.concatenate([valids[i] for i, _ in cells], 0) / total)
    dscore = (prob * (grads - delta)).astype(BF16)
    prob = prob.astype(BF16)
    first = iota((MID, 1), 0) == 0
    shape = (COV, WIDTH)
    for n, (i, t) in enumerate(cells):
        rows = slice(n * COV, (n + 1) * COV)
        own = stats[rows]
        far_block = (
            picked[n][MID:, :WIDTH] + pltpu.roll(picked[n][MID:, 3 * WIDTH :], 1, 0)
            + pltpu.roll(jnp.where(first, own[MID:], 0.0), 2, 0)
        )
        for c in range(2):
            send_ref[2 * i + c, t * MID : (t + 1) * MID, :] = low[n][:MID, WIDTH : 2 * WIDTH]
            send_ref[2 * i + c, 2 * MID + t * MID : 2 * MID + (t + 1) * MID, :] = low[n][:MID, 2 * WIDTH : 3 * WIDTH]
        send_ref[2 * i + t, 4 * MID : 5 * MID, :] = low[n][:MID, :WIDTH]
        send_ref[2 * i + t, 5 * MID : 6 * MID, :] = low[n][:MID, 3 * WIDTH :]
        send_ref[2 * i + t, 6 * MID : 7 * MID, :] = own[:MID].astype(BF16)
        send_ref[2 * i + t, 7 * MID : 8 * MID, :] = far_block.astype(BF16)
        kept = (
            picked[n][:, :WIDTH], picked[n][:, 3 * WIDTH :], out[rows],
            jnp.broadcast_to(lse[rows], shape), jnp.broadcast_to(delta[rows], shape),
        )
        for at, x in enumerate(kept):
            cov_ref[at, i, t] = x
        keys = block(k_ref, (i, t))
        both = dot_nn(jnp.concatenate([dscore[rows], prob[rows]], 0), keys)
        cov_ref[5, i, t] = both[:COV]
        cov_ref[6, i, t] = both[COV:]
        chosen = selects[i] * valids[i].astype(BF16)
        left_ref[i, t] = jnp.concatenate([dscore[rows], prob[rows], chosen, chosen], 0).T


def extract(offsets, q, k, v, g, pack):
    n = EXTRACT_HEADS
    column = pl.BlockSpec((2 * SEG1, n * WIDTH), lambda h, *_: (0, h))
    return pl.pallas_call(
        extract_kernel,
        grid_spec=pltpu.PrefetchScalarGridSpec(
            num_scalar_prefetch=2,
            grid=(HEADS // n,),
            in_specs=[column] * 4,
            out_specs=[
                pl.BlockSpec((2 * n, PACK, WIDTH), lambda h, *_: (h, 0, 0)),
                pl.BlockSpec((KEPT, n, 2, COV, WIDTH), lambda h, *_: (0, h, 0, 0, 0)),
                pl.BlockSpec((n, 2, SEG1, 4 * COV), lambda h, *_: (h, 0, 0, 0)),
            ],
        ),
        out_shape=[
            jax.ShapeDtypeStruct((2 * HEADS, pack, WIDTH), BF16),
            jax.ShapeDtypeStruct((KEPT, HEADS, 2, COV, WIDTH), F32),
            jax.ShapeDtypeStruct((HEADS, 2, SEG1, 4 * COV), BF16),
        ],
        compiler_params=pltpu.CompilerParams(vmem_limit_bytes=VMEM),
        cost_estimate=pl.CostEstimate(flops=2**32, bytes_accessed=12 * 2**20, transcendentals=2**18),
        name="extract",
    )(*offsets, q, k, v, g)


def local_kernel(first, off2_ref, off3_ref, q_ref, k_ref, v_ref, g_ref, *rest):
    att_ref, dq_ref, dk_ref, dv_ref = rest[-4:]
    head = pl.program_id(0) + first
    position = iota((1, SEG1), 1)
    covered = ((position & (DILATION_TWO - 1)) == off2_ref[head]) | (position == off3_ref[head])
    for t in range(2):
        rows = slice(t * SEG1, (t + 1) * SEG1)
        q, k, v, g = (ref[rows, :] for ref in (q_ref, k_ref, v_ref, g_ref))
        scores = dot_nt(k, q) * (FACTOR * math.log2(math.e))
        grad = dot_nt(v, g)
        weight = jnp.exp2(scores - jnp.max(scores, axis=0, keepdims=True))
        inverse = 1.0 / jnp.sum(weight, axis=0, keepdims=True)
        att = (dot_nn(v.T, weight.astype(BF16)) * inverse).astype(BF16).astype(F32)
        delta = jnp.sum(g.T.astype(F32) * att, axis=0, keepdims=True)
        att_ref[rows, :] = jnp.where(covered, 0.0, att).astype(BF16).T
        prob = weight * jnp.where(covered, 0.0, inverse)
        dscore = (prob * (grad - delta)).astype(BF16)
        dq_ref[rows, :] = (dot_nn(k.T, dscore) * FACTOR).astype(BF16).T
        dk_ref[rows, :] = dot_nn(dscore, q)
        dv_ref[rows, :] = dot_nn(prob.astype(BF16), g)


def local(offsets, q, k, v, g, first, count, earlier):
    block = pl.BlockSpec((2 * SEG1, WIDTH), lambda h, *_: (0, h + first))
    kept = [pl.BlockSpec(memory_space=pl.ANY)] * len(earlier)
    share = count / HEADS
    return pl.pallas_call(
        lambda *refs: local_kernel(first, *refs),
        grid_spec=pltpu.PrefetchScalarGridSpec(
            num_scalar_prefetch=2,
            grid=(count,),
            in_specs=[block] * 4 + kept,
            out_specs=[block] * 4,
        ),
        out_shape=[jax.ShapeDtypeStruct(q.shape, d) for d in (BF16, BF16, F32, F32)],
        input_output_aliases={6 + i: i for i in range(len(earlier))},
        compiler_params=pltpu.CompilerParams(vmem_limit_bytes=VMEM),
        cost_estimate=pl.CostEstimate(
            flops=int(share * 12 * 2**30), bytes_accessed=int(share * 20 * 2**20), transcendentals=int(share * 2**22)
        ),
        name="local",
    )(*offsets, q, k, v, g, *earlier)


def merge_lse(parts):
    top = parts[0]
    for part in parts[1:]:
        top = jnp.maximum(top, part)
    total = jnp.exp(parts[0] - top)
    for part in parts[1:]:
        total = total + jnp.exp(part - top)
    return top + jnp.log(total)


def remote_kernel(off2_ref, off3_ref, in_ref, out_ref, far_out_ref):
    head = lax.axis_index("inner") // 2
    off_two, off_three = off2_ref[head], off3_ref[head]
    double = (off_three % DILATION_TWO) == off_two
    place = off_three // DILATION_TWO
    n = in_ref.shape[0]
    queries = n * MID

    def part(at, rows):
        return in_ref[:, at * MID : at * MID + rows, :].reshape(n * rows, WIDTH)

    k, v = part(0, 2 * MID), part(2, 2 * MID)
    q, g = part(4, MID), part(5, MID)
    stats = part(6, MID).astype(F32)
    packed = part(7, MID)
    row = iota((3 * n, queries), 0)
    pick = (iota((3 * n, queries), 1) == MID * (row % n) + row // n).astype(BF16)
    picked = dot_nn(pick, packed)
    qf, gf = picked[:n].astype(BF16), picked[n : 2 * n].astype(BF16)
    turn = (iota((8, WIDTH), 0) == iota((8, WIDTH), 1)).astype(BF16)
    figures = dot_nt(turn, picked[2 * n :].astype(BF16))
    lse1_far = figures[0:1] + figures[1:2] + figures[2:3]
    delta1_far = figures[3:4] + figures[4:5] + figures[5:6]
    scores = dot_nt(q, k) * FACTOR
    top = jnp.max(scores, axis=1, keepdims=True)
    weight = jnp.exp(scores - top)
    total = jnp.sum(weight, axis=1, keepdims=True)
    out = dot_nn(weight.astype(BF16), v) / total
    lse2 = top + jnp.log(total)
    delta2 = jnp.sum(g.astype(F32) * out, axis=1, keepdims=True)
    far = part(8, in_ref.shape[1] - PACK)
    held = far.shape[0]
    is_key = (iota((held, n), 0) & 3) < 2
    scores_far = jnp.where(is_key, dot_nt(far, qf) * FACTOR, NEG)
    top_far = jnp.max(scores_far, axis=0, keepdims=True)
    weight_far = jnp.where(is_key, jnp.exp(scores_far - top_far), 0.0)
    total_far = jnp.sum(weight_far, axis=0, keepdims=True)
    lse3 = top_far + jnp.log(total_far)
    share_far = weight_far / total_far
    out_far = dot_tn(pltpu.roll(share_far, 2, 0).astype(BF16), far)
    grad_far = pltpu.roll(dot_nt(far, gf), held - 2, 0)
    delta3 = jnp.sum(share_far * grad_far, axis=0, keepdims=True)
    same = (iota((queries, n), 0) == MID * iota((queries, n), 1) + place) & double
    lse3_mid = jnp.max(jnp.where(same, lse3, NEG), axis=1, keepdims=True)
    delta3_mid = jnp.sum(jnp.where(same, delta3, 0.0), axis=1, keepdims=True)
    lse2_far = jnp.max(jnp.where(same, lse2, NEG), axis=0, keepdims=True)
    delta2_far = jnp.sum(jnp.where(same, delta2, 0.0), axis=0, keepdims=True)
    lse1, delta1 = join3(stats, 0), join3(stats, 3)
    lse = merge_lse([lse1, lse2, lse3_mid])
    delta = (
        jnp.exp(lse1 - lse) * delta1 + jnp.exp(lse2 - lse) * delta2 + jnp.exp(lse3_mid - lse) * delta3_mid
    )
    lse_far = merge_lse([lse1_far, lse3, lse2_far])
    delta_far = (
        jnp.exp(lse1_far - lse_far) * delta1_far + jnp.exp(lse3 - lse_far) * delta3
        + jnp.exp(lse2_far - lse_far) * delta2_far
    )
    prob = jnp.exp(scores - lse)
    dscore = (prob * (dot_nt(g, v) - delta)).astype(BF16)
    dq = dot_nn(dscore, k)
    dk = dot_tn(dscore, q)
    dv = dot_tn(prob.astype(BF16), g)
    prob_far = jnp.where(is_key, jnp.exp(scores_far - lse_far), 0.0)
    dscore_far = (prob_far * (grad_far - delta_far)).astype(BF16)
    dq_far = dot_tn(dscore_far, far)
    far_out_ref[...] = (
        dot_nn(pltpu.roll(prob_far, 2, 0).astype(BF16), gf) + dot_nn(dscore_far, qf)
    ).astype(BF16)
    high, middle, low = split3(lse3)
    eight = iota((8, n), 0)
    figures = jnp.where(eight == 0, high, jnp.where(eight == 1, middle, jnp.where(eight == 2, low, 0.0)))
    stats_far = dot_tn(figures.astype(BF16), turn)
    unpick = (iota((queries, 3 * n), 0) == MID * (iota((queries, 3 * n), 1) % n) + iota((queries, 3 * n), 1) // n)
    packed = dot_nn(
        unpick.astype(BF16), jnp.concatenate([dq_far, out_far, stats_far], 0).astype(BF16)
    )

    def give(at, rows, value):
        out_ref[:, at * MID : at * MID + rows, :] = value.astype(BF16).reshape(n, rows, WIDTH)

    give(0, 2 * MID, dk)
    give(2, 2 * MID, dv)
    give(4, MID, dq)
    give(5, MID, out)
    give(6, MID, lanes(split3(lse2), queries))
    give(7, MID, packed)


def remote(offsets, received):
    vmem = pl.BlockSpec(memory_space=pltpu.VMEM)
    smem = pl.BlockSpec(memory_space=pltpu.SMEM)
    n, pack, _ = received.shape
    return pl.pallas_call(
        remote_kernel,
        in_specs=[smem, smem, vmem],
        out_specs=[vmem, vmem],
        out_shape=[
            jax.ShapeDtypeStruct((n, PACK, WIDTH), BF16),
            jax.ShapeDtypeStruct((n * (pack - PACK), WIDTH), BF16),
        ],
        compiler_params=pltpu.CompilerParams(vmem_limit_bytes=VMEM),
        cost_estimate=pl.CostEstimate(flops=2**31, bytes_accessed=2**21, transcendentals=2**19),
        name="remote",
    )(*offsets, received)


def prepare(off2_ref, off3_ref, cov_ref, back_ref, far_ref, right_ref):
    cells, rows = 2 * HEADS, 2 * HEADS * COV
    back = back_ref[...].astype(F32)

    def pad(x):
        return jnp.concatenate([x, jnp.zeros((cells, COV - MID, WIDTH), F32)], 1).reshape(rows, WIDTH)

    def own(at):
        return pad(back[:, at * MID : (at + 1) * MID])

    def both(at):
        x = back[:, at * MID : (at + 2) * MID].reshape(HEADS, 2, COV, WIDTH)
        return pad((x[:, 0] + x[:, 1]).reshape(cells, MID, WIDTH))

    def spread(x):
        return jnp.broadcast_to(x.reshape(cells, 1, WIDTH), (cells, COV, WIDTH)).reshape(rows, WIDTH)

    row = iota((COV, WIDTH), 0)
    is_far = []
    for head in range(HEADS):
        off_three = off3_ref[head]
        twice = (off_three % DILATION_TWO) == off2_ref[head]
        is_far += [(row == jnp.where(twice, off_three // DILATION_TWO, MID)).astype(F32)] * 2
    is_far = jnp.concatenate(is_far, 0) > 0.0
    is_mid = jnp.concatenate([row] * cells, 0) < MID
    ones = (iota((WIDTH, WIDTH), 0) < 3).astype(BF16)

    def joined(x):
        return dot_nn(x.astype(BF16), ones)

    q, g, out, lse1, delta1, dq_one, dq_two = (cov_ref[at].reshape(rows, WIDTH) for at in range(KEPT))
    packed = back[:, 7 * MID : 8 * MID]
    far = far_ref[...].astype(F32)
    far = (far[:, :4] + far[:, 4:]).reshape(HEADS, 2, 2, WIDTH)
    lse2 = jnp.where(is_mid, joined(own(6)), NEG)
    lse3 = jnp.where(is_far, joined(spread(packed[:, 2:3])), NEG)
    lse = merge_lse([lse1, lse2, lse3])
    share = jnp.exp(lse1 - lse)
    att = (
        share * out + jnp.exp(lse2 - lse) * own(5) + jnp.exp(lse3 - lse) * spread(packed[:, 1:2])
    ).astype(BF16)
    delta = jnp.sum(g * att.astype(F32), axis=1, keepdims=True)
    change = share * (delta - delta1)
    dq = share * dq_one - change * dq_two + own(4) + jnp.where(is_far, spread(packed[:, 0:1]), 0.0)
    dk = both(0) + jnp.where(is_far, spread(far[:, 0]), 0.0)
    dv = both(2) + jnp.where(is_far, spread(far[:, 1]), 0.0)

    def put(at, column, x):
        right_ref[:, at * COV : (at + 1) * COV, column * WIDTH : (column + 1) * WIDTH] = x.astype(BF16).reshape(
            cells, COV, WIDTH
        )

    def put_two(column, x):
        high = x.astype(BF16)
        put(2, column, high)
        put(3, column, x - high.astype(F32))

    right_ref[:, : 2 * COV, : 2 * WIDTH] = jnp.zeros((cells, 2 * COV, 2 * WIDTH), BF16)
    right_ref[:, :COV, 3 * WIDTH :] = jnp.zeros((cells, COV, WIDTH), BF16)
    right_ref[:, 3 * COV :, :WIDTH] = jnp.zeros((cells, COV, WIDTH), BF16)
    put(2, 0, att)
    put_two(1, dq)
    put(0, 2, share * q)
    put(1, 2, -change * q)
    put_two(2, dk)
    put(1, 3, share * g)
    put_two(3, dv)


def finish_kernel(
    off2_ref, off3_ref, cov_ref, back_ref, far_ref, left_ref,
    att_ref, dq_ref, dk_ref, dv_ref, att_out, dq_out, dk_out, dv_out, right_ref,
):
    head, t = pl.program_id(0) * FINISH_HEADS, pl.program_id(1)

    @pl.when((pl.program_id(0) == 0) & (t == 0))
    def _():
        prepare(off2_ref, off3_ref, cov_ref, back_ref, far_ref, right_ref)

    for i in range(FINISH_HEADS):
        c = slice(i * WIDTH, (i + 1) * WIDTH)
        x = dot_nn(left_ref[i, 0], right_ref[2 * (head + i) + t])
        att_out[:, c] = (att_ref[:, c].astype(F32) + x[:, :WIDTH]).astype(BF16)
        dq_out[:, c] = (dq_ref[:, c].astype(F32) + FACTOR * x[:, WIDTH : 2 * WIDTH]).astype(BF16)
        dk_out[:, c] = (FACTOR * (dk_ref[:, c] + x[:, 2 * WIDTH : 3 * WIDTH])).astype(BF16)
        dv_out[:, c] = (dv_ref[:, c] + x[:, 3 * WIDTH :]).astype(BF16)


def finish(offsets, cov, left, back, far, local_parts):
    n = FINISH_HEADS
    block = pl.BlockSpec((SEG1, n * WIDTH), lambda h, t, *_: (t, h))
    whole = [pl.BlockSpec(x.shape, lambda *_, r=x.ndim: (0,) * r, pipeline_mode=pl.Buffered(1)) for x in (cov, back, far)]
    return pl.pallas_call(
        finish_kernel,
        grid_spec=pltpu.PrefetchScalarGridSpec(
            num_scalar_prefetch=2,
            grid=(HEADS // n, 2),
            in_specs=whole
            + [pl.BlockSpec((n, 1, SEG1, 4 * COV), lambda h, t, *_: (h, t, 0, 0))]
            + [block] * 4,
            out_specs=[block] * 4,
            scratch_shapes=[pltpu.VMEM((2 * HEADS, 4 * COV, 4 * WIDTH), BF16)],
        ),
        out_shape=[jax.ShapeDtypeStruct(x.shape, BF16) for x in local_parts],
        compiler_params=pltpu.CompilerParams(vmem_limit_bytes=VMEM),
        cost_estimate=pl.CostEstimate(flops=2**30, bytes_accessed=28 * 2**20, transcendentals=2**18),
        name="finish",
    )(*offsets, cov, back, far, left, *local_parts)


def solution(mesh):
    outer, inner = mesh.shape["outer"], mesh.shape["inner"]
    split = P(("outer", "inner"), None)

    def body(queries, keys, values, out_grad, middle_head_offsets, distant_head_offsets):
        offsets = (middle_head_offsets, distant_head_offsets)
        arrays = (queries, keys, values, out_grad)
        far = far_rows(distant_head_offsets, keys, values, outer)
        far, *arrays = lax.optimization_barrier((far, *arrays))
        far = lax.all_to_all(far, "outer", 0, 0)
        send, cov, left = extract(offsets, *arrays, PACK + 4 * outer)
        far, send = lax.optimization_barrier((far, send))
        far = far.reshape(outer, HEADS, 4, WIDTH).transpose(1, 0, 2, 3).reshape(HEADS, 1, 4 * outer, WIDTH)
        far = jnp.broadcast_to(far, (HEADS, 2, 4 * outer, WIDTH)).reshape(inner, 4 * outer, WIDTH)
        send = lax.dynamic_update_slice(send, far, (0, PACK, 0))
        got = lax.all_to_all(send, "inner", 0, 0)
        parts = local(offsets, *arrays, 0, 4, ())
        got, *parts = lax.optimization_barrier((got, *parts))
        back, far = remote(offsets, got)
        back, far, *parts = lax.optimization_barrier((back, far, *parts))
        back = lax.all_to_all(back, "inner", 0, 0)
        far = far.reshape(inner, outer, 4, WIDTH).transpose(1, 0, 2, 3)
        far = lax.all_to_all(far.reshape(outer, inner * 4, WIDTH), "outer", 0, 0)
        parts = local(offsets, *arrays, 4, 2, parts)
        far, *parts = lax.optimization_barrier((far, *parts))
        far = jnp.sum(far.astype(F32), axis=0).astype(BF16).reshape(inner, 4, WIDTH)
        far = lax.all_to_all(far, "inner", 0, 0).reshape(HEADS, 8, WIDTH)
        parts = local(offsets, *arrays, 6, 2, parts)
        back, far, *parts = lax.optimization_barrier((back, far, *parts))
        return finish(offsets, cov, left, back, far, parts)

    return jax.shard_map(
        body, mesh=mesh, in_specs=(split,) * 4 + (P(), P()), out_specs=(split,) * 4, check_vma=False
    )
```

time: 1940 us -> 103 us (0.05)
  waiting for transfers between devices: 1320 us -> 1.62 us
  blocking collectives: 354 us -> 11.2 us
  local copies, waits for them, and re-layouts: 90.4 us -> 3.96 us
  other arithmetic: 79.1 us -> 0.03 us
  Pallas kernels: 0 us -> 58.6 us
  matrix products: 56.9 us -> 0 us
    reduce_scatter x4 -> x0, waiting for transfers between devices: 1320 us -> none  [the longest x1 635 us: body(): lax.psum_scatter(far_results[2][0], ('outer', 'inner'), scatter_dimension...]
    all_gather x2 -> x0, blocking collectives: 354 us -> none  [the longest x1 182 us: body(): lax.all_gather(distant_key_rows, ('outer', 'inner'), axis=0, tiled=True)]
    pallas_call x0 -> x7, Pallas kernels: none -> 58.6 us  [the longest x3 29.2 us: local(): pl.pallas_call(lambda *refs: local_kernel(first, *refs), grid_spec=pltpu....]
    dot_general x18 -> x0, matrix products: 56.9 us -> none  [the longest x3 12.4 us: attend(): jnp.einsum('gqhe,gkhe->ghqk', q_part, k_part, preferred_element_type=jnp....]
    convert_element_type x2 -> x0, other arithmetic: 47.1 us -> none  [the longest x1 38.8 us: merge_three(): complete_sequence.astype(jnp.bfloat16)]
    broadcast_in_dim x27 -> x2, local copies, waits for them, and re-layouts: 27.7 us -> 0.03 us  [body(): jnp.broadcast_to(far, (HEADS, 2, 4 * outer, WIDTH))]
    all_to_all x0 -> x4, starting transfers between devices: none -> 25.2 us  [the longest x1 8.51 us: body(): far = lax.all_to_all(far, 'outer', 0, 0)]
    reduce_sum x8 -> x1, other arithmetic: 23.3 us -> 0.03 us  [body(): far = jnp.sum(far.astype(F32), axis=0).astype(BF16).reshape(inner, 4, WIDTH)]
  transfers between devices with their start and end apart: 6 -> 4, of which waited for: 4 -> 1; matrix products, arithmetic and copies ran while one was open for 6% -> 0% of each run, Pallas kernels for 0% -> 38%
where the time goes in v1:
time: 103 us; the launch traced here: 101 us
  Pallas kernels  58.6 us (57%)
  starting transfers between devices  25.2 us (24%)
  blocking collectives  11.2 us (11%)
  local copies, waits for them, and re-layouts  3.96 us (4%)
  waiting for transfers between devices  1.62 us (2%)
    pallas_call x3, Pallas kernels, local(): pl.pallas_call(lambda *refs: local_kernel(first, *refs), grid_spec=pltpu....  29.2 us
    pallas_call x1, Pallas kernels, finish(): pl.pallas_call(finish_kernel, grid_spec=pltpu.PrefetchScalarGridSpec(num_...  13.8 us
    all_to_all x1, blocking collectives, body(): far = lax.all_to_all(far, 'inner', 0, 0).reshape(HEADS, 8, WIDTH)  11.2 us
    pallas_call x1, Pallas kernels, extract(): pl.pallas_call(extract_kernel, grid_spec=pltpu.PrefetchScalarGridSpec(num...  9.15 us
    all_to_all x1, starting transfers between devices, body(): far = lax.all_to_all(far, 'outer', 0, 0)  8.51 us
    all_to_all x1, starting transfers between devices, body(): far = lax.all_to_all(far.reshape(outer, inner * 4, WIDTH), 'outer', 0, 0)  7.55 us
    all_to_all x1, starting transfers between devices, body(): got = lax.all_to_all(send, 'inner', 0, 0)  5.39 us
    pallas_call x1, Pallas kernels, remote(): pl.pallas_call(remote_kernel, in_specs=[smem, smem, vmem], out_specs=[vme...  3.9 us
  transfers between devices with their start and end apart: 4, of which 1 were waited for; matrix products, arithmetic and copies ran while one was open for 0% of the time, Pallas kernels for 38%

profile of v1, /device:TPU:1, one launch (start us, length us, event | category | flops | bytes accessed | tf_op | source)
XLA Modules:
  0.0 101.4 jit_solution(7631786633475947976)
XLA Ops:
  0.6 2.6 %far_rows.1 = bf16[8,32,128]{2,1,0:T(8,128)(2,1)} custom-call(s32[8]{0:T(128)} %off3_ref.7, bf16[1024,1024]{1,0:T(8,128)(2,1)} %refs_3_.2, bf16[1024,1024]{1,0:T(8,128)(2,1)} %refs_4_.2), custom_call_target="tpu_custom_call" | custom-call | flops 262144 | bytes 262144 | tf_op jit(solution)/shard_map/far_rows/pallas_call | solution.py:98
  3.2 8.5 %all-to-all-start = ((bf16[8,32,128]{2,1,0:T(8,128)(2,1)}), bf16[8,32,128]{2,1,0:T(8,128)(2,1)S(1)}, u32[]{:S(2)}, u32[]{:S(2)}) async-start(bf16[8,32,128]{2,1,0:T(8,128)(2,1)} %far_rows.1), calls=%async_computation | async-start | bytes 131072 | tf_op jit(solution)/shard_map/all_to_all | solution.py:488
  11.7 9.1 %extract.1 = (bf16[16,160,128]{2,1,0:T(8,128)(2,1)}, f32[7,8,2,32,128]{4,3,2,1,0:T(8,128)}, bf16[8,2,512,128]{3,2,1,0:T(8,128)(2,1)}) custom-call(s32[8]{0:T(128)} %off2_ref.5, s32[8]{0:T(128)} %off3_ref.7, bf16[1024,1024]{1,0:T(8,128)(2,1)} %refs_2_.2, bf16[1024,1024]{1,0:T(8,128)(2,1)} %refs_3_.2, bf16[1024,1024]{1,0:T(8,128)(2,1)} %refs_4_.2, ...), custom_call_target="tpu_custom_call" | custom-call | flops 4294967296 | bytes 12582912 | tf_op jit(solution)/shard_map/extract/pallas_call | solution.py:186
  20.9 0.0 all-to-all-done
  20.9 0.7 constant_dynamic-update-slice_fusion
  21.6 5.4 %all-to-all-start.1 = ((bf16[16,160,128]{2,1,0:T(8,128)(2,1)}), bf16[16,160,128]{2,1,0:T(8,128)(2,1)S(1)}, u32[]{:S(2)}, u32[]{:S(2)}) async-start(bf16[16,160,128]{2,1,0:T(8,128)(2,1)} %constant_dynamic-update-slice_fusion), calls=%async_computation.1 | async-start | bytes 1310720 | tf_op jit(solution)/shard_map/all_to_all | solution.py:494
  27.0 13.1 %local.3 = (bf16[1024,1024]{1,0:T(8,128)(2,1)}, bf16[1024,1024]{1,0:T(8,128)(2,1)}, f32[1024,1024]{1,0:T(8,128)}, f32[1024,1024]{1,0:T(8,128)}) custom-call(s32[8]{0:T(128)} %off2_ref.5, s32[8]{0:T(128)} %off3_ref.7, bf16[1024,1024]{1,0:T(8,128)(2,1)} %refs_2_.2, bf16[1024,1024]{1,0:T(8,128)(2,1)} %refs_3_.2, bf16[1024,1024]{1,0:T(8,128)(2,1)} %refs_4_.2, ...), custom_call_target="tpu_custom_call" | custom-call | flops 6442450944 | bytes 10485760 | tf_op jit(solution)/shard_map/local/pallas_call | solution.py:235
  40.1 0.0 all-to-all-done.1.in_ref
  40.1 0.0 copy-start.1
  40.1 0.8 copy-done.1
  40.9 3.9 %remote.1 = (bf16[16,128,128]{2,1,0:T(8,128)(2,1)}, bf16[512,128]{1,0:T(8,128)(2,1)}) custom-call(s32[8]{0:T(128)} %off2_ref.5, s32[8]{0:T(128)} %off3_ref.7, bf16[16,160,128]{2,1,0:T(8,128)(2,1)} %copy-done.1), custom_call_target="tpu_custom_call" | custom-call | flops 2147483648 | bytes 2097152 | tf_op jit(solution)/shard_map/remote/pallas_call | solution.py:355
  44.8 0.9 copy.23
  45.8 0.7 copy.24
  46.5 7.6 %all-to-all-start.3 = ((bf16[8,64,128]{2,1,0:T(8,128)(2,1)}), bf16[8,64,128]{2,1,0:T(8,128)(2,1)S(1)}, u32[]{:S(2)}, u32[]{:S(2)}) async-start(bf16[8,64,128]{2,1,0:T(8,128)(2,1)} %copy.24), calls=%async_computation.3 | async-start | bytes 262144 | tf_op jit(solution)/shard_map/all_to_all | solution.py:501
  54.0 8.1 %local.4 = (bf16[1024,1024]{1,0:T(8,128)(2,1)}, bf16[1024,1024]{1,0:T(8,128)(2,1)}, f32[1024,1024]{1,0:T(8,128)}, f32[1024,1024]{1,0:T(8,128)}) custom-call(s32[8]{0:T(128)} %off2_ref.5, s32[8]{0:T(128)} %off3_ref.7, bf16[1024,1024]{1,0:T(8,128)(2,1)} %refs_2_.2, ...), custom_call_target="tpu_custom_call", output_to_operand_aliasing={{0}: (6, {}), {1}: (7, {}), {2}: (8, {}), {3}: (9, {})} | custom-call | flops 3221225472 | bytes 5242880 | tf_op jit(solution)/shard_map/local/pallas_call | solution.py:235
  62.1 0.0 all-to-all-done.3
  62.1 11.2 %all_to_all.25 = bf16[16,4,128]{2,1,0:T(4,128)(2,1)} all-to-all(bf16[16,4,128]{2,1,0:T(4,128)(2,1)S(1)} %bitcast.17), channel_id=1, replica_groups=mesh['outer'=8,'inner'=16] {'inner'}, dimensions={0} | all-to-all | bytes 32768 | tf_op jit(solution)/shard_map/all_to_all | solution.py:505
  73.3 3.8 %all-to-all-start.2 = ((bf16[16,128,128]{2,1,0:T(8,128)(2,1)}), bf16[16,128,128]{2,1,0:T(8,128)(2,1)S(1)}, u32[]{:S(2)}, u32[]{:S(2)}) async-start(bf16[16,128,128]{2,1,0:T(8,128)(2,1)} %get-tuple-element.70), calls=%async_computation.2 | async-start | bytes 1048576 | tf_op jit(solution)/shard_map/all_to_all | solution.py:499
  77.1 8.1 %local.5 = (bf16[1024,1024]{1,0:T(8,128)(2,1)}, bf16[1024,1024]{1,0:T(8,128)(2,1)}, f32[1024,1024]{1,0:T(8,128)}, f32[1024,1024]{1,0:T(8,128)}) custom-call(s32[8]{0:T(128)} %off2_ref.5, s32[8]{0:T(128)} %off3_ref.7, bf16[1024,1024]{1,0:T(8,128)(2,1)} %refs_2_.2, ...), custom_call_target="tpu_custom_call", output_to_operand_aliasing={{0}: (6, {}), {1}: (7, {}), {2}: (8, {}), {3}: (9, {})} | custom-call | flops 3221225472 | bytes 5242880 | tf_op jit(solution)/shard_map/local/pallas_call | solution.py:235
  85.1 1.6 %all-to-all-done.2.back_ref = bf16[16,128,128]{2,1,0:T(8,128)(2,1)S(1)} async-done(((bf16[16,128,128]{2,1,0:T(8,128)(2,1)}), bf16[16,128,128]{2,1,0:T(8,128)(2,1)S(1)}, u32[]{:S(2)}, u32[]{:S(2)}) %all-to-all-start.2) | async-done | bytes 524320 | tf_op jit(solution)/shard_map/all_to_all | solution.py:499
  86.7 0.0 copy-start
  86.7 0.8 copy-done
  87.5 13.8 %finish.1 = (bf16[1024,1024]{1,0:T(8,128)(2,1)}, bf16[1024,1024]{1,0:T(8,128)(2,1)}, bf16[1024,1024]{1,0:T(8,128)(2,1)}, bf16[1024,1024]{1,0:T(8,128)(2,1)}) custom-call(s32[8]{0:T(128)} %off2_ref.5, s32[8]{0:T(128)} %off3_ref.7, f32[7,8,2,32,128]{4,3,2,1,0:T(8,128)} %get-tuple-element.54.cov_ref, bf16[16,128,128]{2,1,0:T(8,128)(2,1)} %copy-done, ...), custom_call_target="tpu_custom_call" | custom-call | flops 1073741824 | bytes 29360128 | tf_op jit(solution)/shard_map/finish/pallas_call | solution.py:461
  (4 shorter events, 0.1 us)
Async XLA Ops:
  3.2 17.7 %all-to-all-start = ((bf16[8,32,128]{2,1,0:T(8,128)(2,1)}), bf16[8,32,128]{2,1,0:T(8,128)(2,1)S(1)}, u32[]{:S(2)}, u32[]{:S(2)}) async-start(bf16[8,32,128]{2,1,0:T(8,128)(2,1)} %far_rows.1), calls=%async_computation | async-start | bytes 131072 | tf_op jit(solution)/shard_map/all_to_all | solution.py:488
  21.6 18.5 %all-to-all-start.1 = ((bf16[16,160,128]{2,1,0:T(8,128)(2,1)}), bf16[16,160,128]{2,1,0:T(8,128)(2,1)S(1)}, u32[]{:S(2)}, u32[]{:S(2)}) async-start(bf16[16,160,128]{2,1,0:T(8,128)(2,1)} %constant_dynamic-update-slice_fusion), calls=%async_computation.1 | async-start | bytes 1310720 | tf_op jit(solution)/shard_map/all_to_all | solution.py:494
  40.1 0.8 copy-start.1
  46.5 15.6 %all-to-all-start.3 = ((bf16[8,64,128]{2,1,0:T(8,128)(2,1)}), bf16[8,64,128]{2,1,0:T(8,128)(2,1)S(1)}, u32[]{:S(2)}, u32[]{:S(2)}) async-start(bf16[8,64,128]{2,1,0:T(8,128)(2,1)} %copy.24), calls=%async_computation.3 | async-start | bytes 262144 | tf_op jit(solution)/shard_map/all_to_all | solution.py:501
  73.3 13.4 %all-to-all-start.2 = ((bf16[16,128,128]{2,1,0:T(8,128)(2,1)}), bf16[16,128,128]{2,1,0:T(8,128)(2,1)S(1)}, u32[]{:S(2)}, u32[]{:S(2)}) async-start(bf16[16,128,128]{2,1,0:T(8,128)(2,1)} %get-tuple-element.70), calls=%async_computation.2 | async-start | bytes 1048576 | tf_op jit(solution)/shard_map/all_to_all | solution.py:499
  86.7 0.8 copy-start

commit v2 on v1

--- a/solution.py
+++ b/solution.py
@@ -18,7 +18,7 @@
 PACK = 128
 KEPT = 7
 EXTRACT_HEADS = 2
-FINISH_HEADS = 2
+FINISH_HEADS = 4
 VMEM = 60 * 2**20
 NEG = -1e30
 F32 = jnp.float32
@@ -63,51 +63,6 @@
 def targets(shape, dim, off_two, off_three):
     j = iota(shape, dim)
     return jnp.where(j < MID, DILATION_TWO * j + off_two, jnp.where(j == MID, off_three, -1))
-
-
-def far_rows_kernel(off3_ref, k_ref, v_ref, out_ref, slab, sems):
-    copies = []
-    for head in range(HEADS):
-        start = pl.multiple_of((off3_ref[head] // 16) * 16, 16)
-        for j in range(4):
-            source = (k_ref, v_ref)[j // 2]
-            copies.append(
-                pltpu.make_async_copy(
-                    source.at[pl.ds((j % 2) * SEG1 + start, 16), pl.ds(head * WIDTH, WIDTH)],
-                    slab.at[4 * head + j],
-                    sems.at[4 * head + j],
-                )
-            )
-    for copy in copies:
-        copy.start()
-    for copy in copies:
-        copy.wait()
-    picked = []
-    for head in range(HEADS):
-        inside = iota((16, 1), 0) == off3_ref[head] % 16
-        for j in range(4):
-            picked.append(
-                jnp.sum(jnp.where(inside, slab[4 * head + j].astype(F32), 0.0), axis=0, keepdims=True)
-            )
-    rows = jnp.concatenate(picked, 0).astype(BF16)
-    for o in range(out_ref.shape[0]):
-        out_ref[o] = rows
-
-
-def far_rows(off3, k, v, copies):
-    return pl.pallas_call(
-        far_rows_kernel,
-        in_specs=[pl.BlockSpec(memory_space=pltpu.SMEM)] + [pl.BlockSpec(memory_space=pl.ANY)] * 2,
-        out_specs=pl.BlockSpec(memory_space=pltpu.VMEM),
-        out_shape=jax.ShapeDtypeStruct((copies, 4 * HEADS, WIDTH), BF16),
-        scratch_shapes=[
-            pltpu.VMEM((4 * HEADS, 16, WIDTH), BF16),
-            pltpu.SemaphoreType.DMA((4 * HEADS,)),
-        ],
-        compiler_params=pltpu.CompilerParams(vmem_limit_bytes=VMEM),
-        cost_estimate=pl.CostEstimate(flops=2**18, bytes_accessed=2**18, transcendentals=0),
-        name="far_rows",
-    )(off3, k, v)
 
 
 def extract_kernel(
@@ -155,17 +110,18 @@
     for n, (i, t) in enumerate(cells):
         rows = slice(n * COV, (n + 1) * COV)
         own = stats[rows]
-        far_block = (
-            picked[n][MID:, :WIDTH] + pltpu.roll(picked[n][MID:, 3 * WIDTH :], 1, 0)
-            + pltpu.roll(jnp.where(first, own[MID:], 0.0), 2, 0)
-        )
         for c in range(2):
             send_ref[2 * i + c, t * MID : (t + 1) * MID, :] = low[n][:MID, WIDTH : 2 * WIDTH]
             send_ref[2 * i + c, 2 * MID + t * MID : 2 * MID + (t + 1) * MID, :] = low[n][:MID, 2 * WIDTH : 3 * WIDTH]
         send_ref[2 * i + t, 4 * MID : 5 * MID, :] = low[n][:MID, :WIDTH]
         send_ref[2 * i + t, 5 * MID : 6 * MID, :] = low[n][:MID, 3 * WIDTH :]
         send_ref[2 * i + t, 6 * MID : 7 * MID, :] = own[:MID].astype(BF16)
-        send_ref[2 * i + t, 7 * MID : 8 * MID, :] = far_block.astype(BF16)
+        mine = (picked[n][MID:, :WIDTH], picked[n][MID:, 3 * WIDTH :], jnp.where(first, own[MID:], 0.0))
+        pair = [picked[n - t + u][MID:, at * WIDTH : (at + 1) * WIDTH] for at in (1, 2) for u in range(2)]
+        far_block = pair[0]
+        for at, x in enumerate((*pair[1:], *mine)):
+            far_block = far_block + pltpu.roll(x, at + 1, 0)
+        send_ref[2 * i + t, 7 * MID :, :] = far_block.astype(BF16)
         kept = (
             picked[n][:, :WIDTH], picked[n][:, 3 * WIDTH :], out[rows],
             jnp.broadcast_to(lse[rows], shape), jnp.broadcast_to(delta[rows], shape),
@@ -180,7 +136,7 @@
         left_ref[i, t] = jnp.concatenate([dscore[rows], prob[rows], chosen, chosen], 0).T
 
 
-def extract(offsets, q, k, v, g, pack):
+def extract(offsets, q, k, v, g):
     n = EXTRACT_HEADS
     column = pl.BlockSpec((2 * SEG1, n * WIDTH), lambda h, *_: (0, h))
     return pl.pallas_call(
@@ -196,7 +152,7 @@
             ],
         ),
         out_shape=[
-            jax.ShapeDtypeStruct((2 * HEADS, pack, WIDTH), BF16),
+            jax.ShapeDtypeStruct((2 * HEADS, PACK, WIDTH), BF16),
             jax.ShapeDtypeStruct((KEPT, HEADS, 2, COV, WIDTH), F32),
             jax.ShapeDtypeStruct((HEADS, 2, SEG1, 4 * COV), BF16),
         ],
@@ -260,113 +216,155 @@
     return top + jnp.log(total)
 
 
-def remote_kernel(off2_ref, off3_ref, in_ref, out_ref, far_out_ref):
+def part(ref, at, rows):
+    return ref[:, at * MID : at * MID + rows, :].reshape(ref.shape[0] * rows, WIDTH)
+
+
+def far_places(shape, dim, starts):
+    j = iota(shape, dim)
+    n = shape[dim] // 7
+    place = jnp.zeros(shape, jnp.int32)
+    for at, start in enumerate(starts):
+        if at < 2:
+            u = j - 2 * n * at
+            place = jnp.where((u >= 0) & (u < 2 * n), MID * (u // 2) + u % 2 + start, place)
+        else:
+            u = j - n * (at + 2)
+            place = jnp.where((u >= 0) & (u < n), MID * u + start, place)
+    return place
+
+
+def forward_kernel(off2_ref, off3_ref, in_ref, far_ref, out_ref, figures_ref):
     head = lax.axis_index("inner") // 2
-    off_two, off_three = off2_ref[head], off3_ref[head]
-    double = (off_three % DILATION_TWO) == off_two
-    place = off_three // DILATION_TWO
+    off_three = off3_ref[head]
     n = in_ref.shape[0]
+    k, v, q, g = part(in_ref, 0, 2 * MID), part(in_ref, 2, 2 * MID), part(in_ref, 4, MID), part(in_ref, 5, MID)
     queries = n * MID
-
-    def part(at, rows):
-        return in_ref[:, at * MID : at * MID + rows, :].reshape(n * rows, WIDTH)
-
-    k, v = part(0, 2 * MID), part(2, 2 * MID)
-    q, g = part(4, MID), part(5, MID)
-    stats = part(6, MID).astype(F32)
-    packed = part(7, MID)
-    row = iota((3 * n, queries), 0)
-    pick = (iota((3 * n, queries), 1) == MID * (row % n) + row // n).astype(BF16)
-    picked = dot_nn(pick, packed)
-    qf, gf = picked[:n].astype(BF16), picked[n : 2 * n].astype(BF16)
-    turn = (iota((8, WIDTH), 0) == iota((8, WIDTH), 1)).astype(BF16)
-    figures = dot_nt(turn, picked[2 * n :].astype(BF16))
-    lse1_far = figures[0:1] + figures[1:2] + figures[2:3]
-    delta1_far = figures[3:4] + figures[4:5] + figures[5:6]
     scores = dot_nt(q, k) * FACTOR
     top = jnp.max(scores, axis=1, keepdims=True)
     weight = jnp.exp(scores - top)
     total = jnp.sum(weight, axis=1, keepdims=True)
     out = dot_nn(weight.astype(BF16), v) / total
-    lse2 = top + jnp.log(total)
-    delta2 = jnp.sum(g.astype(F32) * out, axis=1, keepdims=True)
-    far = part(8, in_ref.shape[1] - PACK)
-    held = far.shape[0]
-    is_key = (iota((held, n), 0) & 3) < 2
-    scores_far = jnp.where(is_key, dot_nt(far, qf) * FACTOR, NEG)
-    top_far = jnp.max(scores_far, axis=0, keepdims=True)
-    weight_far = jnp.where(is_key, jnp.exp(scores_far - top_far), 0.0)
-    total_far = jnp.sum(weight_far, axis=0, keepdims=True)
-    lse3 = top_far + jnp.log(total_far)
-    share_far = weight_far / total_far
-    out_far = dot_tn(pltpu.roll(share_far, 2, 0).astype(BF16), far)
-    grad_far = pltpu.roll(dot_nt(far, gf), held - 2, 0)
-    delta3 = jnp.sum(share_far * grad_far, axis=0, keepdims=True)
-    same = (iota((queries, n), 0) == MID * iota((queries, n), 1) + place) & double
-    lse3_mid = jnp.max(jnp.where(same, lse3, NEG), axis=1, keepdims=True)
-    delta3_mid = jnp.sum(jnp.where(same, delta3, 0.0), axis=1, keepdims=True)
-    lse2_far = jnp.max(jnp.where(same, lse2, NEG), axis=0, keepdims=True)
-    delta2_far = jnp.sum(jnp.where(same, delta2, 0.0), axis=0, keepdims=True)
+    lse = jnp.broadcast_to(top + jnp.log(total), (queries, WIDTH))
+    delta = jnp.broadcast_to(jnp.sum(g.astype(F32) * out, axis=1, keepdims=True), (queries, WIDTH))
+    out_ref[...] = out
+    figures_ref[0] = lse
+    figures_ref[1] = delta
+    pick = (iota((7 * n, queries), 1) == far_places((7 * n, 1), 0, (0, 2, 4, 5, 6))).astype(BF16)
+    picked = dot_nn(pick, part(in_ref, 7, MID))
+    stats = picked[6 * n :]
+    same = ((off_three % DILATION_TWO) == off2_ref[head]) & (
+        iota((n, MID, WIDTH), 1) == off_three // DILATION_TWO
+    )
     lse1, delta1 = join3(stats, 0), join3(stats, 3)
-    lse = merge_lse([lse1, lse2, lse3_mid])
-    delta = (
-        jnp.exp(lse1 - lse) * delta1 + jnp.exp(lse2 - lse) * delta2 + jnp.exp(lse3_mid - lse) * delta3_mid
+    lse2 = jnp.max(jnp.where(same, lse.reshape(n, MID, WIDTH), NEG), axis=1)
+    delta2 = jnp.sum(jnp.where(same, delta.reshape(n, MID, WIDTH), 0.0), axis=1)
+    both = merge_lse([lse1, lse2])
+    delta = jnp.exp(lse1 - both) * delta1 + jnp.exp(lse2 - both) * delta2
+    rows = jnp.concatenate([picked[: 6 * n], lanes(split3(both) + split3(delta), n)], 0).astype(BF16)
+    for o in range(far_ref.shape[0]):
+        far_ref[o] = rows
+
+
+def backward_kernel(off2_ref, off3_ref, in_ref, far_ref, out2_ref, figures_ref, out_ref, key_ref, query_ref):
+    head, outer = lax.axis_index("inner") // 2, lax.axis_index("outer")
+    off_three = off3_ref[head]
+    n = in_ref.shape[0]
+    queries = n * MID
+    turn = (iota((8, WIDTH), 0) == iota((8, WIDTH), 1)).astype(BF16)
+    kf, vf = part(far_ref, 0, 2 * MID), part(far_ref, 2, 2 * MID)
+    qf, gf = part(far_ref, 4, MID), part(far_ref, 5, MID)
+    figures = dot_nt(turn, part(far_ref, 6, MID))
+    lse12 = figures[0:1] + figures[1:2] + figures[2:3]
+    delta12 = figures[3:4] + figures[4:5] + figures[5:6]
+    scores = dot_nt(kf, qf) * FACTOR
+    grads = dot_nt(vf, gf)
+    top = jnp.max(scores, axis=0, keepdims=True)
+    weight = jnp.exp(scores - top)
+    total = jnp.sum(weight, axis=0, keepdims=True)
+    lse3 = top + jnp.log(total)
+    share = weight / total
+    delta3 = jnp.sum(share * grads, axis=0, keepdims=True)
+    lse = merge_lse([lse12, lse3])
+    delta = jnp.exp(lse12 - lse) * delta12 + jnp.exp(lse3 - lse) * delta3
+    prob = jnp.exp(scores - lse)
+    dscore = (prob * (grads - delta)).astype(BF16)
+    key_ref[0] = dot_nn(dscore, qf)
+    key_ref[1] = dot_nn(prob.astype(BF16), gf)
+    query_ref[0] = dot_tn(dscore, kf)
+    query_ref[1] = dot_tn(share.astype(BF16), vf)
+    eight = iota((8, lse3.shape[1]), 0)
+    figures = jnp.zeros(eight.shape, F32)
+    for at, x in enumerate(split3(lse3) + split3(delta3)):
+        figures = jnp.where(eight == at, x, figures)
+    query_ref[2] = dot_tn(figures.astype(BF16), turn)
+    own_keys = pl.ds(pl.multiple_of(outer * 2 * n, 2 * n), 2 * n)
+    own_queries = pl.ds(pl.multiple_of(outer * n, n), n)
+    own = [key_ref[0, own_keys, :], key_ref[1, own_keys, :]] + [query_ref[at, own_queries, :] for at in range(3)]
+    unpick = (iota((queries, 7 * n), 0) == far_places((1, 7 * n), 1, (3, 5, 0, 1, 2))).astype(BF16)
+    packed = dot_nn(unpick, jnp.concatenate(own, 0).astype(BF16))
+    same = ((off_three % DILATION_TWO) == off2_ref[head]) & (
+        iota((n, MID, WIDTH), 1) == off_three // DILATION_TWO
     )
-    lse_far = merge_lse([lse1_far, lse3, lse2_far])
-    delta_far = (
-        jnp.exp(lse1_far - lse_far) * delta1_far + jnp.exp(lse3 - lse_far) * delta3
-        + jnp.exp(lse2_far - lse_far) * delta2_far
-    )
-    prob = jnp.exp(scores - lse)
-    dscore = (prob * (dot_nt(g, v) - delta)).astype(BF16)
-    dq = dot_nn(dscore, k)
-    dk = dot_tn(dscore, q)
-    dv = dot_tn(prob.astype(BF16), g)
-    prob_far = jnp.where(is_key, jnp.exp(scores_far - lse_far), 0.0)
-    dscore_far = (prob_far * (grad_far - delta_far)).astype(BF16)
-    dq_far = dot_tn(dscore_far, far)
-    far_out_ref[...] = (
-        dot_nn(pltpu.roll(prob_far, 2, 0).astype(BF16), gf) + dot_nn(dscore_far, qf)
-    ).astype(BF16)
-    high, middle, low = split3(lse3)
-    eight = iota((8, n), 0)
-    figures = jnp.where(eight == 0, high, jnp.where(eight == 1, middle, jnp.where(eight == 2, low, 0.0)))
-    stats_far = dot_tn(figures.astype(BF16), turn)
-    unpick = (iota((queries, 3 * n), 0) == MID * (iota((queries, 3 * n), 1) % n) + iota((queries, 3 * n), 1) // n)
-    packed = dot_nn(
-        unpick.astype(BF16), jnp.concatenate([dq_far, out_far, stats_far], 0).astype(BF16)
-    )
+
+    def expand(column, other):
+        wide = jnp.broadcast_to(jnp.broadcast_to(column, (n, WIDTH)).reshape(n, 1, WIDTH), (n, MID, WIDTH))
+        return jnp.where(same, wide, other).reshape(queries, WIDTH)
+
+    lse3, delta3 = expand(join3(own[4], 0), NEG), expand(join3(own[4], 3), 0.0)
+    stats = part(in_ref, 6, MID).astype(F32)
+    lse1, delta1 = join3(stats, 0), join3(stats, 3)
+    lse2, delta2 = figures_ref[0], figures_ref[1]
+    lse = merge_lse([lse1, lse2, lse3])
+    delta = jnp.exp(lse1 - lse) * delta1 + jnp.exp(lse2 - lse) * delta2 + jnp.exp(lse3 - lse) * delta3
+    k, v, q, g = part(in_ref, 0, 2 * MID), part(in_ref, 2, 2 * MID), part(in_ref, 4, MID), part(in_ref, 5, MID)
+    prob = jnp.exp(dot_nt(q, k) * FACTOR - lse[:, :1])
+    dscore = (prob * (dot_nt(g, v) - delta[:, :1])).astype(BF16)
 
     def give(at, rows, value):
         out_ref[:, at * MID : at * MID + rows, :] = value.astype(BF16).reshape(n, rows, WIDTH)
 
-    give(0, 2 * MID, dk)
-    give(2, 2 * MID, dv)
-    give(4, MID, dq)
-    give(5, MID, out)
+    give(0, 2 * MID, dot_tn(dscore, q))
+    give(2, 2 * MID, dot_tn(prob.astype(BF16), g))
+    give(4, MID, dot_nn(dscore, k))
+    give(5, MID, out2_ref[...])
     give(6, MID, lanes(split3(lse2), queries))
     give(7, MID, packed)
 
 
-def remote(offsets, received):
+def remote_call(kernel, offsets, arrays, shapes, scratch, name):
     vmem = pl.BlockSpec(memory_space=pltpu.VMEM)
     smem = pl.BlockSpec(memory_space=pltpu.SMEM)
-    n, pack, _ = received.shape
     return pl.pallas_call(
-        remote_kernel,
-        in_specs=[smem, smem, vmem],
-        out_specs=[vmem, vmem],
-        out_shape=[
-            jax.ShapeDtypeStruct((n, PACK, WIDTH), BF16),
-            jax.ShapeDtypeStruct((n * (pack - PACK), WIDTH), BF16),
-        ],
+        kernel,
+        in_specs=[smem, smem] + [vmem] * len(arrays),
+        out_specs=[vmem] * len(shapes),
+        out_shape=[jax.ShapeDtypeStruct(*x) for x in shapes],
+        scratch_shapes=[pltpu.VMEM(*x) for x in scratch],
         compiler_params=pltpu.CompilerParams(vmem_limit_bytes=VMEM),
         cost_estimate=pl.CostEstimate(flops=2**31, bytes_accessed=2**21, transcendentals=2**19),
-        name="remote",
-    )(*offsets, received)
-
-
-def prepare(off2_ref, off3_ref, cov_ref, back_ref, far_ref, right_ref):
+        name=name,
+    )(*offsets, *arrays)
+
+
+def remote_forward(offsets, received, outer):
+    n = received.shape[0]
+    rows = n * MID
+    return remote_call(
+        forward_kernel, offsets, (received,),
+        [((outer, 7 * n, WIDTH), BF16), ((rows, WIDTH), F32), ((2, rows, WIDTH), F32)], [], "remote_forward",
+    )
+
+
+def remote_backward(offsets, received, far, out, figures):
+    n, outer = received.shape[0], far.shape[0]
+    return remote_call(
+        backward_kernel, offsets, (received, far, out, figures), [(received.shape, BF16)],
+        [((2, outer * 2 * n, WIDTH), F32), ((3, outer * n, WIDTH), F32)], "remote_backward",
+    )[0]
+
+
+def prepare(off2_ref, off3_ref, cov_ref, back_ref, right_ref):
     cells, rows = 2 * HEADS, 2 * HEADS * COV
     back = back_ref[...].astype(F32)
 
@@ -398,8 +396,8 @@
 
     q, g, out, lse1, delta1, dq_one, dq_two = (cov_ref[at].reshape(rows, WIDTH) for at in range(KEPT))
     packed = back[:, 7 * MID : 8 * MID]
-    far = far_ref[...].astype(F32)
-    far = (far[:, :4] + far[:, 4:]).reshape(HEADS, 2, 2, WIDTH)
+    far = packed[:, 3:7].reshape(HEADS, 2, 4, WIDTH)
+    far = (far[:, 0] + far[:, 1]).reshape(HEADS, 2, 2, WIDTH)
     lse2 = jnp.where(is_mid, joined(own(6)), NEG)
     lse3 = jnp.where(is_far, joined(spread(packed[:, 2:3])), NEG)
     lse = merge_lse([lse1, lse2, lse3])
@@ -436,14 +434,14 @@
 
 
 def finish_kernel(
-    off2_ref, off3_ref, cov_ref, back_ref, far_ref, left_ref,
+    off2_ref, off3_ref, cov_ref, back_ref, left_ref,
     att_ref, dq_ref, dk_ref, dv_ref, att_out, dq_out, dk_out, dv_out, right_ref,
 ):
     head, t = pl.program_id(0) * FINISH_HEADS, pl.program_id(1)
 
     @pl.when((pl.program_id(0) == 0) & (t == 0))
     def _():
-        prepare(off2_ref, off3_ref, cov_ref, back_ref, far_ref, right_ref)
+        prepare(off2_ref, off3_ref, cov_ref, back_ref, right_ref)
 
     for i in range(FINISH_HEADS):
         c = slice(i * WIDTH, (i + 1) * WIDTH)
@@ -454,10 +452,10 @@
         dv_out[:, c] = (dv_ref[:, c] + x[:, 3 * WIDTH :]).astype(BF16)
 
 
-def finish(offsets, cov, left, back, far, local_parts):
+def finish(offsets, cov, left, back, local_parts):
     n = FINISH_HEADS
     block = pl.BlockSpec((SEG1, n * WIDTH), lambda h, t, *_: (t, h))
-    whole = [pl.BlockSpec(x.shape, lambda *_, r=x.ndim: (0,) * r, pipeline_mode=pl.Buffered(1)) for x in (cov, back, far)]
+    whole = [pl.BlockSpec(x.shape, lambda *_, r=x.ndim: (0,) * r, pipeline_mode=pl.Buffered(1)) for x in (cov, back)]
     return pl.pallas_call(
         finish_kernel,
         grid_spec=pltpu.PrefetchScalarGridSpec(
@@ -473,39 +471,31 @@
         compiler_params=pltpu.CompilerParams(vmem_limit_bytes=VMEM),
         cost_estimate=pl.CostEstimate(flops=2**30, bytes_accessed=28 * 2**20, transcendentals=2**18),
         name="finish",
-    )(*offsets, cov, back, far, left, *local_parts)
+    )(*offsets, cov, back, left, *local_parts)
 
 
 def solution(mesh):
-    outer, inner = mesh.shape["outer"], mesh.shape["inner"]
+    outer = mesh.shape["outer"]
     split = P(("outer", "inner"), None)
 
     def body(queries, keys, values, out_grad, middle_head_offsets, distant_head_offsets):
         offsets = (middle_head_offsets, distant_head_offsets)
         arrays = (queries, keys, values, out_grad)
-        far = far_rows(distant_head_offsets, keys, values, outer)
-        far, *arrays = lax.optimization_barrier((far, *arrays))
-        far = lax.all_to_all(far, "outer", 0, 0)
-        send, cov, left = extract(offsets, *arrays, PACK + 4 * outer)
-        far, send = lax.optimization_barrier((far, send))
-        far = far.reshape(outer, HEADS, 4, WIDTH).transpose(1, 0, 2, 3).reshape(HEADS, 1, 4 * outer, WIDTH)
-        far = jnp.broadcast_to(far, (HEADS, 2, 4 * outer, WIDTH)).reshape(inner, 4 * outer, WIDTH)
-        send = lax.dynamic_update_slice(send, far, (0, PACK, 0))
+        send, cov, left = extract(offsets, *arrays)
         got = lax.all_to_all(send, "inner", 0, 0)
         parts = local(offsets, *arrays, 0, 4, ())
         got, *parts = lax.optimization_barrier((got, *parts))
-        back, far = remote(offsets, got)
-        back, far, *parts = lax.optimization_barrier((back, far, *parts))
-        back = lax.all_to_all(back, "inner", 0, 0)
-        far = far.reshape(inner, outer, 4, WIDTH).transpose(1, 0, 2, 3)
-        far = lax.all_to_all(far.reshape(outer, inner * 4, WIDTH), "outer", 0, 0)
+        far, out, figures = remote_forward(offsets, got, outer)
+        far, *parts = lax.optimization_barrier((far, *parts))
+        far = lax.all_to_all(far, "outer", 0, 0)
         parts = local(offsets, *arrays, 4, 2, parts)
         far, *parts = lax.optimization_barrier((far, *parts))
-        far = jnp.sum(far.astype(F32), axis=0).astype(BF16).reshape(inner, 4, WIDTH)
-        far = lax.all_to_all(far, "inner", 0, 0).reshape(HEADS, 8, WIDTH)
+        back = remote_backward(offsets, got, far, out, figures)
+        back, *parts = lax.optimization_barrier((back, *parts))
+        back = lax.all_to_all(back, "inner", 0, 0)
         parts = local(offsets, *arrays, 6, 2, parts)
-        back, far, *parts = lax.optimization_barrier((back, far, *parts))
-        return finish(offsets, cov, left, back, far, parts)
+        back, *parts = lax.optimization_barrier((back, *parts))
+        return finish(offsets, cov, left, back, parts)
 
     return jax.shard_map(
         body, mesh=mesh, in_specs=(split,) * 4 + (P(), P()), out_specs=(split,) * 4, check_vma=False

time: 103 us -> 81.2 us (0.79)
  blocking collectives: 11.2 us -> 0 us
  starting transfers between devices: 25.2 us -> 20.3 us
  Pallas kernels: 58.6 us -> 55.7 us
  local copies, waits for them, and re-layouts: 3.96 us -> 2.25 us
    all_to_all x1 -> x0, blocking collectives: 11.2 us -> none  [body(): far = lax.all_to_all(far, 'inner', 0, 0).reshape(HEADS, 8, WIDTH)]
    all_to_all x1 -> x0, starting transfers between devices: 7.55 us -> none  [body(): far = lax.all_to_all(far.reshape(outer, inner * 4, WIDTH), 'outer', 0, 0)]
    all_to_all x1, starting transfers between devices: 3.76 us -> 6.09 us  [body(): back = lax.all_to_all(back, 'inner', 0, 0)]
    pallas_call x1, Pallas kernels: 13.8 us -> 11.6 us  [finish(): pl.pallas_call(finish_kernel, grid_spec=pltpu.PrefetchScalarGridSpec(num_...]
    reshape x3 -> x0, local copies, waits for them, and re-layouts: 1.61 us -> none  [the longest x1 0.92 us: body(): far = far.reshape(inner, outer, 4, WIDTH).transpose(1, 0, 2, 3)]
    all_to_all x1, starting transfers between devices: 5.39 us -> 6.83 us  [body(): got = lax.all_to_all(send, 'inner', 0, 0)]
    all_to_all x1, starting transfers between devices: 8.51 us -> 7.37 us  [body(): far = lax.all_to_all(far, 'outer', 0, 0)]
    unnamed x4 -> x6, local copies, waits for them, and re-layouts: 1.63 us -> 2.25 us
  transfers between devices with their start and end apart: 4 -> 3, of which waited for: 1 -> 1; matrix products, arithmetic and copies ran while one was open for 0% -> 0% of each run, Pallas kernels for 38% -> 36%
where the time goes in v2:
time: 81.2 us; the launch traced here: 80.5 us
  Pallas kernels  55.7 us (69%)
  starting transfers between devices  20.3 us (25%)
  local copies, waits for them, and re-layouts  2.25 us (3%)
  waiting for transfers between devices  1.55 us (2%)
    pallas_call x3, Pallas kernels, local(): pl.pallas_call(lambda *refs: local_kernel(first, *refs), grid_spec=pltpu....  29.2 us
    pallas_call x1, Pallas kernels, finish(): pl.pallas_call(finish_kernel, grid_spec=pltpu.PrefetchScalarGridSpec(num_...  11.6 us
    pallas_call x1, Pallas kernels, extract(): pl.pallas_call(extract_kernel, grid_spec=pltpu.PrefetchScalarGridSpec(num...  8.95 us
    all_to_all x1, starting transfers between devices, body(): far = lax.all_to_all(far, 'outer', 0, 0)  7.37 us
    all_to_all x1, starting transfers between devices, body(): got = lax.all_to_all(send, 'inner', 0, 0)  6.83 us
    all_to_all x1, starting transfers between devices, body(): back = lax.all_to_all(back, 'inner', 0, 0)  6.09 us
    pallas_call x2, Pallas kernels, remote_call(): pl.pallas_call(kernel, in_specs=[smem, smem] + [vmem] * len(arrays), out_...  5.94 us
    unnamed x6, local copies, waits for them, and re-layouts  2.25 us
  transfers between devices with their start and end apart: 3, of which 1 were waited for; matrix products, arithmetic and copies ran while one was open for 0% of the time, Pallas kernels for 36%

profile of v2, /device:TPU:1, one launch (start us, length us, event | category | flops | bytes accessed | tf_op | source)
XLA Modules:
  0.0 80.5 jit_solution(7319327767298641359)
XLA Ops:
  0.6 8.9 %extract.1 = (bf16[16,128,128]{2,1,0:T(8,128)(2,1)}, f32[7,8,2,32,128]{4,3,2,1,0:T(8,128)}, bf16[8,2,512,128]{3,2,1,0:T(8,128)(2,1)}) custom-call(s32[8]{0:T(128)} %off2_ref.7, s32[8]{0:T(128)} %off3_ref.7, bf16[1024,1024]{1,0:T(8,128)(2,1)} %refs_2_.5, bf16[1024,1024]{1,0:T(8,128)(2,1)} %refs_3_.5, bf16[1024,1024]{1,0:T(8,128)(2,1)} %refs_4_.5, ...), custom_call_target="tpu_custom_call" | custom-call | flops 4294967296 | bytes 12582912 | tf_op jit(solution)/shard_map/extract/pallas_call | solution.py:142
  9.6 6.8 %all-to-all-start = ((bf16[16,128,128]{2,1,0:T(8,128)(2,1)}), bf16[16,128,128]{2,1,0:T(8,128)(2,1)S(1)}, u32[]{:S(2)}, u32[]{:S(2)}) async-start(bf16[16,128,128]{2,1,0:T(8,128)(2,1)} %get-tuple-element.48), calls=%async_computation | async-start | bytes 1048576 | tf_op jit(solution)/shard_map/all_to_all | solution.py:485
  16.4 13.1 %local.3 = (bf16[1024,1024]{1,0:T(8,128)(2,1)}, bf16[1024,1024]{1,0:T(8,128)(2,1)}, f32[1024,1024]{1,0:T(8,128)}, f32[1024,1024]{1,0:T(8,128)}) custom-call(s32[8]{0:T(128)} %off2_ref.7, s32[8]{0:T(128)} %off3_ref.7, bf16[1024,1024]{1,0:T(8,128)(2,1)} %refs_2_.5, bf16[1024,1024]{1,0:T(8,128)(2,1)} %refs_3_.5, bf16[1024,1024]{1,0:T(8,128)(2,1)} %refs_4_.5, ...), custom_call_target="tpu_custom_call" | custom-call | flops 6442450944 | bytes 10485760 | tf_op jit(solution)/shard_map/local/pallas_call | solution.py:191
  29.5 0.0 all-to-all-done.in_ref
  29.5 0.0 copy-start.1
  29.5 0.8 copy-done.1
  30.3 2.5 %remote_forward.1 = (bf16[8,112,128]{2,1,0:T(8,128)(2,1)}, f32[256,128]{1,0:T(8,128)}, f32[2,256,128]{2,1,0:T(8,128)}) custom-call(s32[8]{0:T(128)} %off2_ref.7, s32[8]{0:T(128)} %off3_ref.7, bf16[16,128,128]{2,1,0:T(8,128)(2,1)} %copy-done.1), custom_call_target="tpu_custom_call" | custom-call | flops 2147483648 | bytes 2097152 | tf_op jit(solution)/shard_map/remote_forward/pallas_call | solution.py:338
  32.8 7.4 %all-to-all-start.1 = ((bf16[8,112,128]{2,1,0:T(8,128)(2,1)}), bf16[8,112,128]{2,1,0:T(8,128)(2,1)S(1)}, u32[]{:S(2)}, u32[]{:S(2)}) async-start(bf16[8,112,128]{2,1,0:T(8,128)(2,1)} %get-tuple-element.59), calls=%async_computation.1 | async-start | bytes 458752 | tf_op jit(solution)/shard_map/all_to_all | solution.py:490
  40.2 8.0 %local.4 = (bf16[1024,1024]{1,0:T(8,128)(2,1)}, bf16[1024,1024]{1,0:T(8,128)(2,1)}, f32[1024,1024]{1,0:T(8,128)}, f32[1024,1024]{1,0:T(8,128)}) custom-call(s32[8]{0:T(128)} %off2_ref.7, s32[8]{0:T(128)} %off3_ref.7, bf16[1024,1024]{1,0:T(8,128)(2,1)} %refs_2_.5, ...), custom_call_target="tpu_custom_call", output_to_operand_aliasing={{0}: (6, {}), {1}: (7, {}), {2}: (8, {}), {3}: (9, {})} | custom-call | flops 3221225472 | bytes 5242880 | tf_op jit(solution)/shard_map/local/pallas_call | solution.py:191
  48.2 0.0 all-to-all-done.1.far_ref
  48.2 0.0 copy-start.2
  48.2 0.7 copy-done.2
  48.9 3.4 %remote_backward.1 = bf16[16,128,128]{2,1,0:T(8,128)(2,1)} custom-call(s32[8]{0:T(128)} %off2_ref.7, s32[8]{0:T(128)} %off3_ref.7, bf16[16,128,128]{2,1,0:T(8,128)(2,1)} %copy-done.1, bf16[8,112,128]{2,1,0:T(8,128)(2,1)} %copy-done.2, f32[256,128]{1,0:T(8,128)} %get-tuple-element.69.out2_ref, f32[2,256,128]{2,1,0:T(8,128)} %get-tuple-element.70.figures_ref), custom_call_target="tpu_custom_call" | custom-call | flops 2147483648 | bytes 2097152 | tf_op jit(solution)/shard_map/remote_backward/pallas_call | solution.py:338
  52.3 6.1 %all-to-all-start.2 = ((bf16[16,128,128]{2,1,0:T(8,128)(2,1)}), bf16[16,128,128]{2,1,0:T(8,128)(2,1)S(1)}, u32[]{:S(2)}, u32[]{:S(2)}) async-start(bf16[16,128,128]{2,1,0:T(8,128)(2,1)} %remote_backward.1), calls=%async_computation.2 | async-start | bytes 1048576 | tf_op jit(solution)/shard_map/all_to_all | solution.py:495
  58.4 8.1 %local.5 = (bf16[1024,1024]{1,0:T(8,128)(2,1)}, bf16[1024,1024]{1,0:T(8,128)(2,1)}, f32[1024,1024]{1,0:T(8,128)}, f32[1024,1024]{1,0:T(8,128)}) custom-call(s32[8]{0:T(128)} %off2_ref.7, s32[8]{0:T(128)} %off3_ref.7, bf16[1024,1024]{1,0:T(8,128)(2,1)} %refs_2_.5, ...), custom_call_target="tpu_custom_call", output_to_operand_aliasing={{0}: (6, {}), {1}: (7, {}), {2}: (8, {}), {3}: (9, {})} | custom-call | flops 3221225472 | bytes 5242880 | tf_op jit(solution)/shard_map/local/pallas_call | solution.py:191
  66.5 1.5 %all-to-all-done.2.back_ref = bf16[16,128,128]{2,1,0:T(8,128)(2,1)S(1)} async-done(((bf16[16,128,128]{2,1,0:T(8,128)(2,1)}), bf16[16,128,128]{2,1,0:T(8,128)(2,1)S(1)}, u32[]{:S(2)}, u32[]{:S(2)}) %all-to-all-start.2) | async-done | bytes 524320 | tf_op jit(solution)/shard_map/all_to_all | solution.py:495
  68.1 0.0 copy-start
  68.1 0.8 copy-done
  68.8 11.6 %finish.1 = (bf16[1024,1024]{1,0:T(8,128)(2,1)}, bf16[1024,1024]{1,0:T(8,128)(2,1)}, bf16[1024,1024]{1,0:T(8,128)(2,1)}, bf16[1024,1024]{1,0:T(8,128)(2,1)}) custom-call(s32[8]{0:T(128)} %off2_ref.7, s32[8]{0:T(128)} %off3_ref.7, f32[7,8,2,32,128]{4,3,2,1,0:T(8,128)} %get-tuple-element.47.cov_ref, bf16[16,128,128]{2,1,0:T(8,128)(2,1)} %copy-done, ...), custom_call_target="tpu_custom_call" | custom-call | flops 1073741824 | bytes 29360128 | tf_op jit(solution)/shard_map/finish/pallas_call | solution.py:459
Async XLA Ops:
  9.6 19.9 %all-to-all-start = ((bf16[16,128,128]{2,1,0:T(8,128)(2,1)}), bf16[16,128,128]{2,1,0:T(8,128)(2,1)S(1)}, u32[]{:S(2)}, u32[]{:S(2)}) async-start(bf16[16,128,128]{2,1,0:T(8,128)(2,1)} %get-tuple-element.48), calls=%async_computation | async-start | bytes 1048576 | tf_op jit(solution)/shard_map/all_to_all | solution.py:485
  29.5 0.8 copy-start.1
  32.8 15.4 %all-to-all-start.1 = ((bf16[8,112,128]{2,1,0:T(8,128)(2,1)}), bf16[8,112,128]{2,1,0:T(8,128)(2,1)S(1)}, u32[]{:S(2)}, u32[]{:S(2)}) async-start(bf16[8,112,128]{2,1,0:T(8,128)(2,1)} %get-tuple-element.59), calls=%async_computation.1 | async-start | bytes 458752 | tf_op jit(solution)/shard_map/all_to_all | solution.py:490
  48.2 0.7 copy-start.2
  52.3 15.7 %all-to-all-start.2 = ((bf16[16,128,128]{2,1,0:T(8,128)(2,1)}), bf16[16,128,128]{2,1,0:T(8,128)(2,1)S(1)}, u32[]{:S(2)}, u32[]{:S(2)}) async-start(bf16[16,128,128]{2,1,0:T(8,128)(2,1)} %remote_backward.1), calls=%async_computation.2 | async-start | bytes 1048576 | tf_op jit(solution)/shard_map/all_to_all | solution.py:495
  68.1 0.8 copy-start

commit v3 on v2

--- a/solution.py
+++ b/solution.py
@@ -18,8 +18,9 @@
 PACK = 128
 KEPT = 7
 EXTRACT_HEADS = 2
-FINISH_HEADS = 4
-VMEM = 60 * 2**20
+SHARES = (3, 2, 3)
+VMEM = 63 * 2**20
+HALF = DILATION_TWO // 2
 NEG = -1e30
 F32 = jnp.float32
 BF16 = jnp.bfloat16
@@ -65,19 +66,61 @@
     return jnp.where(j < MID, DILATION_TWO * j + off_two, jnp.where(j == MID, off_three, -1))
 
 
+def columns(ref, head):
+    return ref.at[:, pl.ds(pl.multiple_of(head * WIDTH, WIDTH), WIDTH)]
+
+
 def extract_kernel(
-    off2_ref, off3_ref, q_ref, k_ref, v_ref, g_ref, send_ref, cov_ref, left_ref
+    off2_ref, off3_ref, q_hbm, k_hbm, v_hbm, g_hbm, send_hbm, cov_hbm, left_hbm,
+    q_all, k_all, v_all, g_all, send_ref, cov_ref, left_ref, sems, out_sems,
 ):
+    def load(at, head):
+        source, target = ((q_hbm, q_all), (k_hbm, k_all), (v_hbm, v_all), (g_hbm, g_all))[at]
+        return pltpu.make_async_copy(columns(source, head), target.at[head], sems.at[head, at])
+
+    def places(step):
+        heads = pl.ds(step * EXTRACT_HEADS, EXTRACT_HEADS)
+        return (pl.ds(step * 2 * EXTRACT_HEADS, 2 * EXTRACT_HEADS),), (slice(None), heads), (heads,)
+
+    def give(step):
+        pairs = zip((send_ref, cov_ref, left_ref), (send_hbm, cov_hbm, left_hbm), places(step))
+        return [
+            pltpu.make_async_copy(source.at[place], target.at[place], out_sems.at[step, at])
+            for at, (source, target, place) in enumerate(pairs)
+        ]
+
+    for head in range(HEADS):
+        for at in range(4):
+            load(at, head).start()
+
+    @pl.loop(0, HEADS // EXTRACT_HEADS)
+    def _(step):
+        first = step * EXTRACT_HEADS
+        for i in range(EXTRACT_HEADS):
+            for at in range(4):
+                load(at, first + i).wait()
+        here = [ref.at[pl.ds(first, EXTRACT_HEADS)] for ref in (q_all, k_all, v_all, g_all)]
+        out = [ref.at[place] for ref, place in zip((send_ref, cov_ref, left_ref), places(step))]
+        extract_heads(first, off2_ref, off3_ref, *here, *out)
+        for copy in give(step):
+            copy.start()
+
+    for step in range(HEADS // EXTRACT_HEADS):
+        for copy in give(step):
+            copy.wait()
+
+
+def extract_heads(first_head, off2_ref, off3_ref, q_ref, k_ref, v_ref, g_ref, send_ref, cov_ref, left_ref):
     cells = [(i, t) for i in range(EXTRACT_HEADS) for t in range(2)]
 
     def block(ref, cell):
         i, t = cell
-        return ref[t * SEG1 : (t + 1) * SEG1, i * WIDTH : (i + 1) * WIDTH]
+        return ref[i, t * SEG1 : (t + 1) * SEG1, :]
 
     selects, valids = [], []
     row = iota((COV, 1), 0)
     for i in range(EXTRACT_HEADS):
-        head = pl.program_id(0) * EXTRACT_HEADS + i
+        head = first_head + i
         off_two, off_three = off2_ref[head], off3_ref[head]
         position = targets((COV, 1), 0, off_two, off_three)
         selects.append((iota((COV, SEG1), 1) == position).astype(BF16))
@@ -137,73 +180,113 @@
 
 
 def extract(offsets, q, k, v, g):
-    n = EXTRACT_HEADS
-    column = pl.BlockSpec((2 * SEG1, n * WIDTH), lambda h, *_: (0, h))
+    smem, hbm = pl.BlockSpec(memory_space=pltpu.SMEM), pl.BlockSpec(memory_space=pl.ANY)
+    shapes = [
+        ((2 * HEADS, PACK, WIDTH), BF16),
+        ((KEPT, HEADS, 2, COV, WIDTH), F32),
+        ((HEADS, 2, SEG1, 4 * COV), BF16),
+    ]
     return pl.pallas_call(
         extract_kernel,
-        grid_spec=pltpu.PrefetchScalarGridSpec(
-            num_scalar_prefetch=2,
-            grid=(HEADS // n,),
-            in_specs=[column] * 4,
-            out_specs=[
-                pl.BlockSpec((2 * n, PACK, WIDTH), lambda h, *_: (h, 0, 0)),
-                pl.BlockSpec((KEPT, n, 2, COV, WIDTH), lambda h, *_: (0, h, 0, 0, 0)),
-                pl.BlockSpec((n, 2, SEG1, 4 * COV), lambda h, *_: (h, 0, 0, 0)),
-            ],
-        ),
-        out_shape=[
-            jax.ShapeDtypeStruct((2 * HEADS, PACK, WIDTH), BF16),
-            jax.ShapeDtypeStruct((KEPT, HEADS, 2, COV, WIDTH), F32),
-            jax.ShapeDtypeStruct((HEADS, 2, SEG1, 4 * COV), BF16),
-        ],
+        in_specs=[smem, smem] + [hbm] * 4,
+        out_specs=[hbm] * 3,
+        out_shape=[jax.ShapeDtypeStruct(*x) for x in shapes],
+        scratch_shapes=[pltpu.VMEM((HEADS, 2 * SEG1, WIDTH), BF16)] * 4
+        + [pltpu.VMEM(*x) for x in shapes]
+        + [pltpu.SemaphoreType.DMA((HEADS, 4)), pltpu.SemaphoreType.DMA((HEADS // EXTRACT_HEADS, 3))],
         compiler_params=pltpu.CompilerParams(vmem_limit_bytes=VMEM),
         cost_estimate=pl.CostEstimate(flops=2**32, bytes_accessed=12 * 2**20, transcendentals=2**18),
         name="extract",
     )(*offsets, q, k, v, g)
 
 
-def local_kernel(first, off2_ref, off3_ref, q_ref, k_ref, v_ref, g_ref, *rest):
-    att_ref, dq_ref, dk_ref, dv_ref = rest[-4:]
-    head = pl.program_id(0) + first
+def local_kernel(first, count, kept, off2_ref, off3_ref, *refs):
+    sources, outs = refs[:4], refs[4 + kept : 8 + kept]
+    held, done, (in_sems, out_sems) = refs[8 + kept : 12 + kept], refs[12 + kept : 16 + kept], refs[16 + kept :]
     position = iota((1, SEG1), 1)
-    covered = ((position & (DILATION_TWO - 1)) == off2_ref[head]) | (position == off3_ref[head])
-    for t in range(2):
-        rows = slice(t * SEG1, (t + 1) * SEG1)
-        q, k, v, g = (ref[rows, :] for ref in (q_ref, k_ref, v_ref, g_ref))
-        scores = dot_nt(k, q) * (FACTOR * math.log2(math.e))
-        grad = dot_nt(v, g)
-        weight = jnp.exp2(scores - jnp.max(scores, axis=0, keepdims=True))
-        inverse = 1.0 / jnp.sum(weight, axis=0, keepdims=True)
-        att = (dot_nn(v.T, weight.astype(BF16)) * inverse).astype(BF16).astype(F32)
-        delta = jnp.sum(g.T.astype(F32) * att, axis=0, keepdims=True)
-        att_ref[rows, :] = jnp.where(covered, 0.0, att).astype(BF16).T
-        prob = weight * jnp.where(covered, 0.0, inverse)
-        dscore = (prob * (grad - delta)).astype(BF16)
-        dq_ref[rows, :] = (dot_nn(k.T, dscore) * FACTOR).astype(BF16).T
-        dk_ref[rows, :] = dot_nn(dscore, q)
-        dv_ref[rows, :] = dot_nn(prob.astype(BF16), g)
-
-
-def local(offsets, q, k, v, g, first, count, earlier):
-    block = pl.BlockSpec((2 * SEG1, WIDTH), lambda h, *_: (0, h + first))
-    kept = [pl.BlockSpec(memory_space=pl.ANY)] * len(earlier)
+
+    def loads(i, t):
+        rows = pl.ds(t * SEG1, SEG1)
+        lane = pl.ds(pl.multiple_of((first + i) * WIDTH, WIDTH), WIDTH)
+        return [
+            pltpu.make_async_copy(sources[at].at[rows, lane], held[at].at[i, rows], in_sems.at[i, t, at])
+            for at in range(4)
+        ]
+
+    def stores(i, t):
+        lane = pl.ds(pl.multiple_of((first + i) * WIDTH, WIDTH), WIDTH)
+        rows = pl.ds(t * SEG1, SEG1)
+        return [
+            pltpu.make_async_copy(
+                done[at].at[i, t], outs[at].at[t, :, :, :, lane] if at < 2 else outs[at].at[first + i, rows],
+                out_sems.at[i, t, at],
+            )
+            for at in range(4)
+        ]
+
+    def start(i):
+        for t in range(2):
+            for copy in loads(i, t):
+                copy.start()
+
+    start(0)
+
+    @pl.loop(0, count)
+    def _(i):
+        @pl.when(i + 1 < count)
+        def _():
+            start(i + 1)
+
+        head = first + i
+        covered = ((position & (DILATION_TWO - 1)) == off2_ref[head]) | (position == off3_ref[head])
+        for t in range(2):
+            for copy in loads(i, t):
+                copy.wait()
+            rows = slice(t * SEG1, (t + 1) * SEG1)
+            q, k, v, g = (ref[i, rows, :] for ref in held)
+            scores = dot_nt(k, q) * (FACTOR * math.log2(math.e))
+            grad = dot_nt(v, g)
+            weight = jnp.exp2(scores - jnp.max(scores, axis=0, keepdims=True))
+            inverse = 1.0 / jnp.sum(weight, axis=0, keepdims=True)
+            att = (dot_nn(v.T, weight.astype(BF16)) * inverse).astype(BF16)
+            delta = jnp.sum(g.T.astype(F32) * att.astype(F32), axis=0, keepdims=True)
+            done[0][i, t] = att.T.reshape(MID, 2, HALF, WIDTH)
+            prob = weight * jnp.where(covered, 0.0, inverse)
+            dscore = (prob * (grad - delta)).astype(BF16)
+            done[1][i, t] = (dot_nn(k.T, dscore) * FACTOR).astype(BF16).T.reshape(MID, 2, HALF, WIDTH)
+            done[2][i, t] = dot_nn(dscore, q).astype(BF16)
+            done[3][i, t] = dot_nn(prob.astype(BF16), g).astype(BF16)
+            for copy in stores(i, t):
+                copy.start()
+
+    @pl.loop(0, count)
+    def _(i):
+        for t in range(2):
+            for copy in stores(i, t):
+                copy.wait()
+
+
+def local(offsets, arrays, first, count, earlier):
+    smem, hbm = pl.BlockSpec(memory_space=pltpu.SMEM), pl.BlockSpec(memory_space=pl.ANY)
     share = count / HEADS
+    period = (MID, 2, HALF)
     return pl.pallas_call(
-        lambda *refs: local_kernel(first, *refs),
-        grid_spec=pltpu.PrefetchScalarGridSpec(
-            num_scalar_prefetch=2,
-            grid=(count,),
-            in_specs=[block] * 4 + kept,
-            out_specs=[block] * 4,
-        ),
-        out_shape=[jax.ShapeDtypeStruct(q.shape, d) for d in (BF16, BF16, F32, F32)],
-        input_output_aliases={6 + i: i for i in range(len(earlier))},
+        lambda *refs: local_kernel(first, count, len(earlier), *refs),
+        in_specs=[smem, smem] + [hbm] * (4 + len(earlier)),
+        out_specs=[hbm] * 4,
+        out_shape=[jax.ShapeDtypeStruct((2, *period, HEADS * WIDTH), BF16)] * 2
+        + [jax.ShapeDtypeStruct((HEADS, 2 * SEG1, WIDTH), BF16)] * 2,
+        input_output_aliases={6 + at: at for at in range(len(earlier))},
+        scratch_shapes=[pltpu.VMEM((count, 2 * SEG1, WIDTH), BF16)] * 4
+        + [pltpu.VMEM((count, 2, *period, WIDTH), BF16)] * 2
+        + [pltpu.VMEM((count, 2, SEG1, WIDTH), BF16)] * 2
+        + [pltpu.SemaphoreType.DMA((count, 2, 4))] * 2,
         compiler_params=pltpu.CompilerParams(vmem_limit_bytes=VMEM),
         cost_estimate=pl.CostEstimate(
-            flops=int(share * 12 * 2**30), bytes_accessed=int(share * 20 * 2**20), transcendentals=int(share * 2**22)
+            flops=int(share * 12 * 2**30), bytes_accessed=int(share * 16 * 2**20), transcendentals=int(share * 2**22)
         ),
         name="local",
-    )(*offsets, q, k, v, g, *earlier)
+    )(*offsets, *arrays, *earlier)
 
 
 def merge_lse(parts):
@@ -247,9 +330,8 @@
     out = dot_nn(weight.astype(BF16), v) / total
     lse = jnp.broadcast_to(top + jnp.log(total), (queries, WIDTH))
     delta = jnp.broadcast_to(jnp.sum(g.astype(F32) * out, axis=1, keepdims=True), (queries, WIDTH))
-    out_ref[...] = out
-    figures_ref[0] = lse
-    figures_ref[1] = delta
+    out_ref[...] = out.astype(BF16)
+    figures_ref[...] = lanes([lse, delta], queries)
     pick = (iota((7 * n, queries), 1) == far_places((7 * n, 1), 0, (0, 2, 4, 5, 6))).astype(BF16)
     picked = dot_nn(pick, part(in_ref, 7, MID))
     stats = picked[6 * n :]
@@ -309,17 +391,17 @@
 
     def expand(column, other):
         wide = jnp.broadcast_to(jnp.broadcast_to(column, (n, WIDTH)).reshape(n, 1, WIDTH), (n, MID, WIDTH))
-        return jnp.where(same, wide, other).reshape(queries, WIDTH)
+        return jnp.where(same, wide, other).reshape(queries, WIDTH)[:, 0:1]
 
     lse3, delta3 = expand(join3(own[4], 0), NEG), expand(join3(own[4], 3), 0.0)
     stats = part(in_ref, 6, MID).astype(F32)
     lse1, delta1 = join3(stats, 0), join3(stats, 3)
-    lse2, delta2 = figures_ref[0], figures_ref[1]
+    lse2, delta2 = figures_ref[:, 0:1], figures_ref[:, 1:2]
     lse = merge_lse([lse1, lse2, lse3])
     delta = jnp.exp(lse1 - lse) * delta1 + jnp.exp(lse2 - lse) * delta2 + jnp.exp(lse3 - lse) * delta3
     k, v, q, g = part(in_ref, 0, 2 * MID), part(in_ref, 2, 2 * MID), part(in_ref, 4, MID), part(in_ref, 5, MID)
-    prob = jnp.exp(dot_nt(q, k) * FACTOR - lse[:, :1])
-    dscore = (prob * (dot_nt(g, v) - delta[:, :1])).astype(BF16)
+    prob = jnp.exp(dot_nt(q, k) * FACTOR - lse)
+    dscore = (prob * (dot_nt(g, v) - delta)).astype(BF16)
 
     def give(at, rows, value):
         out_ref[:, at * MID : at * MID + rows, :] = value.astype(BF16).reshape(n, rows, WIDTH)
@@ -333,13 +415,12 @@
 
 
 def remote_call(kernel, offsets, arrays, shapes, scratch, name):
-    vmem = pl.BlockSpec(memory_space=pltpu.VMEM)
-    smem = pl.BlockSpec(memory_space=pltpu.SMEM)
+    vmem, smem = pl.BlockSpec(memory_space=pltpu.VMEM), pl.BlockSpec(memory_space=pltpu.SMEM)
     return pl.pallas_call(
         kernel,
         in_specs=[smem, smem] + [vmem] * len(arrays),
         out_specs=[vmem] * len(shapes),
-        out_shape=[jax.ShapeDtypeStruct(*x) for x in shapes],
+        out_shape=shapes,
         scratch_shapes=[pltpu.VMEM(*x) for x in scratch],
         compiler_params=pltpu.CompilerParams(vmem_limit_bytes=VMEM),
         cost_estimate=pl.CostEstimate(flops=2**31, bytes_accessed=2**21, transcendentals=2**19),
@@ -352,19 +433,21 @@
     rows = n * MID
     return remote_call(
         forward_kernel, offsets, (received,),
-        [((outer, 7 * n, WIDTH), BF16), ((rows, WIDTH), F32), ((2, rows, WIDTH), F32)], [], "remote_forward",
+        [jax.ShapeDtypeStruct((outer, 7 * n, WIDTH), BF16), jax.ShapeDtypeStruct((rows, WIDTH), BF16),
+         jax.ShapeDtypeStruct((rows, WIDTH), F32)],
+        [], "remote_forward",
     )
 
 
 def remote_backward(offsets, received, far, out, figures):
     n, outer = received.shape[0], far.shape[0]
     return remote_call(
-        backward_kernel, offsets, (received, far, out, figures), [(received.shape, BF16)],
+        backward_kernel, offsets, (received, far, out, figures), [jax.ShapeDtypeStruct(received.shape, BF16)],
         [((2, outer * 2 * n, WIDTH), F32), ((3, outer * n, WIDTH), F32)], "remote_backward",
     )[0]
 
 
-def prepare(off2_ref, off3_ref, cov_ref, back_ref, right_ref):
+def prepare(off2_ref, off3_ref, cov_ref, back_ref, right_ref, rows_ref):
     cells, rows = 2 * HEADS, 2 * HEADS * COV
     back = back_ref[...].astype(F32)
 
@@ -421,57 +504,137 @@
         put(2, column, high)
         put(3, column, x - high.astype(F32))
 
-    right_ref[:, : 2 * COV, : 2 * WIDTH] = jnp.zeros((cells, 2 * COV, 2 * WIDTH), BF16)
-    right_ref[:, :COV, 3 * WIDTH :] = jnp.zeros((cells, COV, WIDTH), BF16)
-    right_ref[:, 3 * COV :, :WIDTH] = jnp.zeros((cells, COV, WIDTH), BF16)
-    put(2, 0, att)
-    put_two(1, dq)
-    put(0, 2, share * q)
-    put(1, 2, -change * q)
-    put_two(2, dk)
-    put(1, 3, share * g)
-    put_two(3, dv)
+    rows_ref[0] = att.astype(F32).reshape(HEADS, 2, COV, WIDTH)
+    rows_ref[1] = (FACTOR * dq).reshape(HEADS, 2, COV, WIDTH)
+    put(0, 0, share * q)
+    put(1, 0, -change * q)
+    put_two(0, dk)
+    put(0, 1, jnp.zeros((rows, WIDTH), F32))
+    put(1, 1, share * g)
+    put_two(1, dv)
+
+
+def patch(off_two, off_three, rows_ref, head, at, slab_ref, other_ref):
+    half = off_two // HALF
+    twice = (off_three % DILATION_TWO) == off_two
+    beside = ((off_three % DILATION_TWO) // HALF) == half
+    mid = rows_ref[at, head, :, :MID].reshape(2 * MID, 1, WIDTH)
+    far = rows_ref[at, head, :, MID : MID + 1]
+    shape = (2 * MID, HALF, WIDTH)
+    row = iota(shape, 1)
+    old = slab_ref[at, head].astype(F32).reshape(shape)
+    here = (row == off_three % HALF) & ((iota(shape, 0) & (MID - 1)) == off_three // DILATION_TWO)
+    here = here & beside & jnp.logical_not(twice)
+    wide = jnp.broadcast_to(far, (2, MID, WIDTH)).reshape(2 * MID, 1, WIDTH)
+    slab = jnp.where(here, wide, jnp.where(row == off_two % HALF, mid, old))
+    slab_ref[at, head] = slab.astype(BF16).reshape(2, MID, HALF, WIDTH)
+    there = (iota((2, HALF, WIDTH), 1) == off_three % HALF) & jnp.logical_not(beside)
+    other_ref[at, head] = jnp.where(there, far, other_ref[at, head].astype(F32)).astype(BF16)
 
 
 def finish_kernel(
-    off2_ref, off3_ref, cov_ref, back_ref, left_ref,
-    att_ref, dq_ref, dk_ref, dv_ref, att_out, dq_out, dk_out, dv_out, right_ref,
+    off2_ref, off3_ref, cov_hbm, back_hbm, left_hbm, att_hbm, dq_hbm, dk_hbm, dv_hbm,
+    att_out, dq_out, dk_out, dv_out,
+    cov_ref, back_ref, left_ref, right_ref, rows_ref, held, done_ref, slab_ref, other_ref,
+    first_sems, in_sems, out_sems, slab_in, slab_out,
 ):
-    head, t = pl.program_id(0) * FINISH_HEADS, pl.program_id(1)
-
-    @pl.when((pl.program_id(0) == 0) & (t == 0))
-    def _():
-        prepare(off2_ref, off3_ref, cov_ref, back_ref, right_ref)
-
-    for i in range(FINISH_HEADS):
-        c = slice(i * WIDTH, (i + 1) * WIDTH)
-        x = dot_nn(left_ref[i, 0], right_ref[2 * (head + i) + t])
-        att_out[:, c] = (att_ref[:, c].astype(F32) + x[:, :WIDTH]).astype(BF16)
-        dq_out[:, c] = (dq_ref[:, c].astype(F32) + FACTOR * x[:, WIDTH : 2 * WIDTH]).astype(BF16)
-        dk_out[:, c] = (FACTOR * (dk_ref[:, c] + x[:, 2 * WIDTH : 3 * WIDTH])).astype(BF16)
-        dv_out[:, c] = (dv_ref[:, c] + x[:, 3 * WIDTH :]).astype(BF16)
-
-
-def finish(offsets, cov, left, back, local_parts):
-    n = FINISH_HEADS
-    block = pl.BlockSpec((SEG1, n * WIDTH), lambda h, t, *_: (t, h))
-    whole = [pl.BlockSpec(x.shape, lambda *_, r=x.ndim: (0,) * r, pipeline_mode=pl.Buffered(1)) for x in (cov, back)]
-    return pl.pallas_call(
+    first = [
+        pltpu.make_async_copy(source, target, first_sems.at[at])
+        for at, (source, target) in enumerate(((back_hbm, back_ref), (cov_hbm, cov_ref)))
+    ]
+
+    def slabs(head, arrays):
+        half, period = off2_ref[head] // HALF, off3_ref[head] // DILATION_TWO
+        lane = pl.ds(pl.multiple_of(head * WIDTH, WIDTH), WIDTH)
+        pairs = []
+        for at, array in enumerate(arrays):
+            pairs.append((array.at[:, :, half, :, lane], slab_ref.at[at, head]))
+            pairs.append((array.at[:, period, 1 - half, :, lane], other_ref.at[at, head]))
+        return pairs
+
+    def loads(head):
+        pairs = slabs(head, (att_hbm, dq_hbm))
+        copies = [pltpu.make_async_copy(*pair, slab_in.at[head, at]) for at, pair in enumerate(pairs)]
+        pairs = [(dk_hbm.at[head], held.at[0, head]), (dv_hbm.at[head], held.at[1, head])]
+        pairs.append((left_hbm.at[head], left_ref.at[head]))
+        return copies + [pltpu.make_async_copy(*pair, in_sems.at[head, at]) for at, pair in enumerate(pairs)]
+
+    def slab_stores(head):
+        pairs = slabs(head, (att_out, dq_out))
+        return [
+            pltpu.make_async_copy(source, target, slab_out.at[head, at]) for at, (target, source) in enumerate(pairs)
+        ]
+
+    def stores(head):
+        lane = pl.ds(pl.multiple_of(head * WIDTH, WIDTH), WIDTH)
+        return [
+            pltpu.make_async_copy(done_ref.at[at, head], out.at[:, lane], out_sems.at[head, at])
+            for at, out in enumerate((dk_out, dv_out))
+        ]
+
+    for copy in first:
+        copy.start()
+
+    @pl.loop(0, HEADS)
+    def _(head):
+        for copy in loads(head):
+            copy.start()
+
+    for copy in first:
+        copy.wait()
+    prepare(off2_ref, off3_ref, cov_ref, back_ref, right_ref, rows_ref)
+
+    @pl.loop(0, HEADS)
+    def _(head):
+        for copy in loads(head):
+            copy.wait()
+        for at in range(2):
+            patch(off2_ref[head], off3_ref[head], rows_ref, head, at, slab_ref, other_ref)
+        for copy in slab_stores(head):
+            copy.start()
+        for t in range(2):
+            rows = slice(t * SEG1, (t + 1) * SEG1)
+            x = dot_nn(left_ref[head, t], right_ref[2 * head + t])
+            done_ref[0, head, rows, :] = (FACTOR * (held[0, head, rows, :].astype(F32) + x[:, :WIDTH])).astype(BF16)
+            done_ref[1, head, rows, :] = (held[1, head, rows, :].astype(F32) + x[:, WIDTH:]).astype(BF16)
+        for copy in stores(head):
+            copy.start()
+
+    @pl.loop(0, HEADS)
+    def _(head):
+        for copy in slab_stores(head) + stores(head):
+            copy.wait()
+
+
+def finish(offsets, cov, left, back, att, dq, dk, dv):
+    smem, hbm = pl.BlockSpec(memory_space=pltpu.SMEM), pl.BlockSpec(memory_space=pl.ANY)
+    kind = (2, HEADS, 2 * SEG1, WIDTH)
+    whole = (2 * SEG1, HEADS * WIDTH)
+    att, dq, dk, dv = pl.pallas_call(
         finish_kernel,
-        grid_spec=pltpu.PrefetchScalarGridSpec(
-            num_scalar_prefetch=2,
-            grid=(HEADS // n, 2),
-            in_specs=whole
-            + [pl.BlockSpec((n, 1, SEG1, 4 * COV), lambda h, t, *_: (h, t, 0, 0))]
-            + [block] * 4,
-            out_specs=[block] * 4,
-            scratch_shapes=[pltpu.VMEM((2 * HEADS, 4 * COV, 4 * WIDTH), BF16)],
-        ),
-        out_shape=[jax.ShapeDtypeStruct(x.shape, BF16) for x in local_parts],
+        in_specs=[smem, smem] + [hbm] * 7,
+        out_specs=[hbm] * 4,
+        out_shape=[jax.ShapeDtypeStruct(att.shape, BF16)] * 2 + [jax.ShapeDtypeStruct(whole, BF16)] * 2,
+        input_output_aliases={5: 0, 6: 1},
+        scratch_shapes=[pltpu.VMEM(x.shape, x.dtype) for x in (cov, back, left)]
+        + [
+            pltpu.VMEM((2 * HEADS, 4 * COV, 2 * WIDTH), BF16),
+            pltpu.VMEM((2, HEADS, 2, COV, WIDTH), F32),
+            pltpu.VMEM(kind, BF16),
+            pltpu.VMEM(kind, BF16),
+            pltpu.VMEM((2, HEADS, 2, MID, HALF, WIDTH), BF16),
+            pltpu.VMEM((2, HEADS, 2, HALF, WIDTH), BF16),
+            pltpu.SemaphoreType.DMA((2,)),
+            pltpu.SemaphoreType.DMA((HEADS, 3)),
+            pltpu.SemaphoreType.DMA((HEADS, 2)),
+            pltpu.SemaphoreType.DMA((HEADS, 4)),
+            pltpu.SemaphoreType.DMA((HEADS, 4)),
+        ],
         compiler_params=pltpu.CompilerParams(vmem_limit_bytes=VMEM),
-        cost_estimate=pl.CostEstimate(flops=2**30, bytes_accessed=28 * 2**20, transcendentals=2**18),
+        cost_estimate=pl.CostEstimate(flops=2**30, bytes_accessed=17 * 2**20, transcendentals=2**18),
         name="finish",
-    )(*offsets, cov, back, left, *local_parts)
+    )(*offsets, cov, back, left, att, dq, dk, dv)
+    return att.reshape(whole), dq.reshape(whole), dk, dv
 
 
 def solution(mesh):
@@ -483,19 +646,19 @@
         arrays = (queries, keys, values, out_grad)
         send, cov, left = extract(offsets, *arrays)
         got = lax.all_to_all(send, "inner", 0, 0)
-        parts = local(offsets, *arrays, 0, 4, ())
+        parts = local(offsets, arrays, 0, SHARES[0], ())
         got, *parts = lax.optimization_barrier((got, *parts))
         far, out, figures = remote_forward(offsets, got, outer)
         far, *parts = lax.optimization_barrier((far, *parts))
         far = lax.all_to_all(far, "outer", 0, 0)
-        parts = local(offsets, *arrays, 4, 2, parts)
+        parts = local(offsets, arrays, SHARES[0], SHARES[1], parts)
         far, *parts = lax.optimization_barrier((far, *parts))
         back = remote_backward(offsets, got, far, out, figures)
         back, *parts = lax.optimization_barrier((back, *parts))
         back = lax.all_to_all(back, "inner", 0, 0)
-        parts = local(offsets, *arrays, 6, 2, parts)
+        parts = local(offsets, arrays, SHARES[0] + SHARES[1], SHARES[2], parts)
         back, *parts = lax.optimization_barrier((back, *parts))
-        return finish(offsets, cov, left, back, parts)
+        return finish(offsets, cov, left, back, *parts)
 
     return jax.shard_map(
         body, mesh=mesh, in_specs=(split,) * 4 + (P(), P()), out_specs=(split,) * 4, check_vma=False

time: 81.2 us -> 76.6 us (0.943)
  Pallas kernels: 55.7 us -> 52.5 us
  waiting for transfers between devices: 1.55 us -> 0.01 us
    pallas_call x5, Pallas kernels: 49.8 us -> 46.7 us  [the longest x3 29.5 us: local(): pl.pallas_call(lambda *refs: local_kernel(first, count, len(earlier), *re...]
    all_to_all x1, waiting for transfers between devices: 1.54 us -> 0.01 us  [body(): back = lax.all_to_all(back, 'inner', 0, 0)]
  transfers between devices with their start and end apart: 3 -> 3, of which waited for: 1 -> 0; matrix products, arithmetic and copies ran while one was open for 0% -> 0% of each run, Pallas kernels for 36% -> 39%
where the time goes in v3:
time: 76.6 us; the launch traced here: 76.1 us
  Pallas kernels  52.5 us (69%)
  starting transfers between devices  20.3 us (27%)
  local copies, waits for them, and re-layouts  2.34 us (3%)
  between operations  0.87 us (1%)
    pallas_call x3, Pallas kernels, local(): pl.pallas_call(lambda *refs: local_kernel(first, count, len(earlier), *re...  29.5 us
    pallas_call x1, Pallas kernels, finish(): pl.pallas_call(finish_kernel, in_specs=[smem, smem] + [hbm] * 7, out_spec...  8.61 us
    pallas_call x1, Pallas kernels, extract(): pl.pallas_call(extract_kernel, in_specs=[smem, smem] + [hbm] * 4, out_spe...  8.58 us
    all_to_all x1, starting transfers between devices, body(): far = lax.all_to_all(far, 'outer', 0, 0)  7.37 us
    all_to_all x1, starting transfers between devices, body(): got = lax.all_to_all(send, 'inner', 0, 0)  6.84 us
    all_to_all x1, starting transfers between devices, body(): back = lax.all_to_all(back, 'inner', 0, 0)  6.14 us
    pallas_call x2, Pallas kernels, remote_call(): pl.pallas_call(kernel, in_specs=[smem, smem] + [vmem] * len(arrays), out_...  5.84 us
    unnamed x6, local copies, waits for them, and re-layouts  2.34 us
  transfers between devices with their start and end apart: 3, of which 0 were waited for; matrix products, arithmetic and copies ran while one was open for 0% of the time, Pallas kernels for 39%

profile of v3, /device:TPU:1, one launch (start us, length us, event | category | flops | bytes accessed | tf_op | source)
XLA Modules:
  0.0 76.1 jit_solution(9833623376540972212)
XLA Ops:
  0.6 8.6 %extract.1 = (bf16[16,128,128]{2,1,0:T(8,128)(2,1)}, f32[7,8,2,32,128]{4,3,2,1,0:T(8,128)}, bf16[8,2,512,128]{3,2,1,0:T(8,128)(2,1)}) custom-call(s32[8]{0:T(128)} %off2_ref.7, s32[8]{0:T(128)} %off3_ref.7, bf16[1024,1024]{1,0:T(8,128)(2,1)} %refs_2_.5, bf16[1024,1024]{1,0:T(8,128)(2,1)} %refs_3_.5, bf16[1024,1024]{1,0:T(8,128)(2,1)} %refs_4_.5, ...), custom_call_target="tpu_custom_call" | custom-call | flops 4294967296 | bytes 12582912 | tf_op jit(solution)/shard_map/extract/pallas_call | solution.py:189
  9.2 6.8 %all-to-all-start = ((bf16[16,128,128]{2,1,0:T(8,128)(2,1)}), bf16[16,128,128]{2,1,0:T(8,128)(2,1)S(1)}, u32[]{:S(2)}, u32[]{:S(2)}) async-start(bf16[16,128,128]{2,1,0:T(8,128)(2,1)} %get-tuple-element.52), calls=%async_computation | async-start | bytes 1048576 | tf_op jit(solution)/shard_map/all_to_all | solution.py:648
  16.1 10.7 %local.3 = (bf16[2,16,2,16,1024]{4,3,2,1,0:T(8,128)(2,1)}, bf16[2,16,2,16,1024]{4,3,2,1,0:T(8,128)(2,1)}, bf16[8,1024,128]{2,1,0:T(8,128)(2,1)}, bf16[8,1024,128]{2,1,0:T(8,128)(2,1)}) custom-call(s32[8]{0:T(128)} %off2_ref.7, s32[8]{0:T(128)} %off3_ref.7, bf16[1024,1024]{1,0:T(8,128)(2,1)} %refs_2_.5, bf16[1024,1024]{1,0:T(8,128)(2,1)} %refs_3_.5, ...), custom_call_target="tpu_custom_call" | custom-call | flops 4831838208 | bytes 6291456 | tf_op jit(solution)/shard_map/local/pallas_call | solution.py:273
  26.8 0.0 all-to-all-done.in_ref
  26.8 0.0 copy-start.1
  26.8 0.8 %copy-done.1 = bf16[16,128,128]{2,1,0:T(8,128)(2,1)} copy-done((bf16[16,128,128]{2,1,0:T(8,128)(2,1)}, bf16[16,128,128]{2,1,0:T(8,128)(2,1)S(1)}, u32[]{:S(2)}) %copy-start.1) | copy-done | bytes 524312
  27.6 2.4 %remote_forward.1 = (bf16[8,112,128]{2,1,0:T(8,128)(2,1)}, bf16[256,128]{1,0:T(8,128)(2,1)}, f32[256,128]{1,0:T(8,128)}) custom-call(s32[8]{0:T(128)} %off2_ref.7, s32[8]{0:T(128)} %off3_ref.7, bf16[16,128,128]{2,1,0:T(8,128)(2,1)} %copy-done.1), custom_call_target="tpu_custom_call" | custom-call | flops 2147483648 | bytes 2097152 | tf_op jit(solution)/shard_map/remote_forward/pallas_call | solution.py:419
  30.1 7.4 %all-to-all-start.1 = ((bf16[8,112,128]{2,1,0:T(8,128)(2,1)}), bf16[8,112,128]{2,1,0:T(8,128)(2,1)S(1)}, u32[]{:S(2)}, u32[]{:S(2)}) async-start(bf16[8,112,128]{2,1,0:T(8,128)(2,1)} %get-tuple-element.63), calls=%async_computation.1 | async-start | bytes 458752 | tf_op jit(solution)/shard_map/all_to_all | solution.py:653
  37.4 8.0 %local.4 = (bf16[2,16,2,16,1024]{4,3,2,1,0:T(8,128)(2,1)}, bf16[2,16,2,16,1024]{4,3,2,1,0:T(8,128)(2,1)}, bf16[8,1024,128]{2,1,0:T(8,128)(2,1)}, bf16[8,1024,128]{2,1,0:T(8,128)(2,1)}) custom-call(s32[8]{0:T(128)} %off2_ref.7, s32[8]{0:T(128)} %off3_ref.7, ...), custom_call_target="tpu_custom_call", output_to_operand_aliasing={{0}: (6, {}), {1}: (7, {}), {2}: (8, {}), {3}: (9, {})} | custom-call | flops 3221225472 | bytes 4194304 | tf_op jit(solution)/shard_map/local/pallas_call | solution.py:273
  45.4 0.0 all-to-all-done.1.far_ref
  45.4 0.0 copy-start.2
  45.4 0.7 copy-done.2
  46.1 3.4 %remote_backward.1 = bf16[16,128,128]{2,1,0:T(8,128)(2,1)} custom-call(s32[8]{0:T(128)} %off2_ref.7, s32[8]{0:T(128)} %off3_ref.7, bf16[16,128,128]{2,1,0:T(8,128)(2,1)} %copy-done.1, bf16[8,112,128]{2,1,0:T(8,128)(2,1)} %copy-done.2, bf16[256,128]{1,0:T(8,128)(2,1)} %get-tuple-element.73.out2_ref, f32[256,128]{1,0:T(8,128)} %get-tuple-element.74.figures_ref), custom_call_target="tpu_custom_call" | custom-call | flops 2147483648 | bytes 2097152 | tf_op jit(solution)/shard_map/remote_backward/pallas_call | solution.py:419
  49.5 6.1 %all-to-all-start.2 = ((bf16[16,128,128]{2,1,0:T(8,128)(2,1)}), bf16[16,128,128]{2,1,0:T(8,128)(2,1)S(1)}, u32[]{:S(2)}, u32[]{:S(2)}) async-start(bf16[16,128,128]{2,1,0:T(8,128)(2,1)} %remote_backward.1), calls=%async_computation.2 | async-start | bytes 1048576 | tf_op jit(solution)/shard_map/all_to_all | solution.py:658
  55.7 10.7 %local.5 = (bf16[2,16,2,16,1024]{4,3,2,1,0:T(8,128)(2,1)}, bf16[2,16,2,16,1024]{4,3,2,1,0:T(8,128)(2,1)}, bf16[8,1024,128]{2,1,0:T(8,128)(2,1)}, bf16[8,1024,128]{2,1,0:T(8,128)(2,1)}) custom-call(s32[8]{0:T(128)} %off2_ref.7, s32[8]{0:T(128)} %off3_ref.7, ...), custom_call_target="tpu_custom_call", output_to_operand_aliasing={{0}: (6, {}), {1}: (7, {}), {2}: (8, {}), {3}: (9, {})} | custom-call | flops 4831838208 | bytes 6291456 | tf_op jit(solution)/shard_map/local/pallas_call | solution.py:273
  66.4 0.0 all-to-all-done.2.back_hbm
  66.4 0.0 copy-start
  66.4 0.8 %copy-done = bf16[16,128,128]{2,1,0:T(8,128)(2,1)} copy-done((bf16[16,128,128]{2,1,0:T(8,128)(2,1)}, bf16[16,128,128]{2,1,0:T(8,128)(2,1)S(1)}, u32[]{:S(2)}) %copy-start) | copy-done | bytes 524312
  67.3 8.6 %finish.1 = (bf16[2,16,2,16,1024]{4,3,2,1,0:T(8,128)(2,1)}, bf16[2,16,2,16,1024]{4,3,2,1,0:T(8,128)(2,1)}, bf16[1024,1024]{1,0:T(8,128)(2,1)}, bf16[1024,1024]{1,0:T(8,128)(2,1)}) custom-call(s32[8]{0:T(128)} %off2_ref.7, s32[8]{0:T(128)} %off3_ref.7, f32[7,8,2,32,128]{4,3,2,1,0:T(8,128)} %get-tuple-element.51.cov_hbm, ...), custom_call_target="tpu_custom_call", output_to_operand_aliasing={{0}: (5, {}), {1}: (6, {})} | custom-call | flops 1073741824 | bytes 17825792 | tf_op jit(solution)/shard_map/finish/pallas_call | solution.py:613
Async XLA Ops:
  9.2 17.6 %all-to-all-start = ((bf16[16,128,128]{2,1,0:T(8,128)(2,1)}), bf16[16,128,128]{2,1,0:T(8,128)(2,1)S(1)}, u32[]{:S(2)}, u32[]{:S(2)}) async-start(bf16[16,128,128]{2,1,0:T(8,128)(2,1)} %get-tuple-element.52), calls=%async_computation | async-start | bytes 1048576 | tf_op jit(solution)/shard_map/all_to_all | solution.py:648
  26.8 0.8 %copy-start.1 = (bf16[16,128,128]{2,1,0:T(8,128)(2,1)}, bf16[16,128,128]{2,1,0:T(8,128)(2,1)S(1)}, u32[]{:S(2)}) copy-start(bf16[16,128,128]{2,1,0:T(8,128)(2,1)S(1)} %all-to-all-done.in_ref) | copy-start | bytes 1572868
  30.1 15.4 %all-to-all-start.1 = ((bf16[8,112,128]{2,1,0:T(8,128)(2,1)}), bf16[8,112,128]{2,1,0:T(8,128)(2,1)S(1)}, u32[]{:S(2)}, u32[]{:S(2)}) async-start(bf16[8,112,128]{2,1,0:T(8,128)(2,1)} %get-tuple-element.63), calls=%async_computation.1 | async-start | bytes 458752 | tf_op jit(solution)/shard_map/all_to_all | solution.py:653
  45.4 0.7 copy-start.2
  49.5 16.9 %all-to-all-start.2 = ((bf16[16,128,128]{2,1,0:T(8,128)(2,1)}), bf16[16,128,128]{2,1,0:T(8,128)(2,1)S(1)}, u32[]{:S(2)}, u32[]{:S(2)}) async-start(bf16[16,128,128]{2,1,0:T(8,128)(2,1)} %remote_backward.1), calls=%async_computation.2 | async-start | bytes 1048576 | tf_op jit(solution)/shard_map/all_to_all | solution.py:658
  66.4 0.9 %copy-start = (bf16[16,128,128]{2,1,0:T(8,128)(2,1)}, bf16[16,128,128]{2,1,0:T(8,128)(2,1)S(1)}, u32[]{:S(2)}) copy-start(bf16[16,128,128]{2,1,0:T(8,128)(2,1)S(1)} %all-to-all-done.2.back_hbm) | copy-start | bytes 1572868

commit v4 on v3

--- a/solution.py
+++ b/solution.py
@@ -16,10 +16,9 @@
 MID = SEG1 // DILATION_TWO
 COV = 32
 PACK = 128
-KEPT = 7
 EXTRACT_HEADS = 2
 SHARES = (3, 2, 3)
-VMEM = 63 * 2**20
+VMEM = 44 * 2**20
 HALF = DILATION_TWO // 2
 NEG = -1e30
 F32 = jnp.float32
@@ -62,74 +61,93 @@
 
 
 def targets(shape, dim, off_two, off_three):
-    j = iota(shape, dim)
+    j = iota(shape, dim) % COV
     return jnp.where(j < MID, DILATION_TWO * j + off_two, jnp.where(j == MID, off_three, -1))
 
 
-def columns(ref, head):
-    return ref.at[:, pl.ds(pl.multiple_of(head * WIDTH, WIDTH), WIDTH)]
+def in_hbm(arrays):
+    return [pltpu.with_memory_space_constraint(x, pltpu.HBM) for x in arrays]
 
 
 def extract_kernel(
-    off2_ref, off3_ref, q_hbm, k_hbm, v_hbm, g_hbm, send_hbm, cov_hbm, left_hbm,
-    q_all, k_all, v_all, g_all, send_ref, cov_ref, left_ref, sems, out_sems,
+    off2_ref, off3_ref, q_hbm, k_hbm, v_hbm, g_hbm, send_hbm, cov_hbm, low_hbm, left_hbm,
+    q_all, k_all, v_all, g_all, send_ref, cov_ref, low_ref, left_ref, sems, out_sems,
 ):
-    def load(at, head):
-        source, target = ((q_hbm, q_all), (k_hbm, k_all), (v_hbm, v_all), (g_hbm, g_all))[at]
-        return pltpu.make_async_copy(columns(source, head), target.at[head], sems.at[head, at])
+    n = EXTRACT_HEADS
+
+    def loads(step):
+        lane = pl.ds(pl.multiple_of(step * n * WIDTH, n * WIDTH), n * WIDTH)
+        pairs = ((q_hbm, q_all), (k_hbm, k_all), (v_hbm, v_all), (g_hbm, g_all))
+        return [
+            pltpu.make_async_copy(source.at[:, :, :, lane], target.at[step], sems.at[step, at])
+            for at, (source, target) in enumerate(pairs)
+        ]
 
     def places(step):
-        heads = pl.ds(step * EXTRACT_HEADS, EXTRACT_HEADS)
-        return (pl.ds(step * 2 * EXTRACT_HEADS, 2 * EXTRACT_HEADS),), (slice(None), heads), (heads,)
-
-    def give(step):
-        pairs = zip((send_ref, cov_ref, left_ref), (send_hbm, cov_hbm, left_hbm), places(step))
+        heads = pl.ds(step * n, n)
+        return (pl.ds(step * 2 * n, 2 * n),), (slice(None), heads), (slice(None), heads), (heads,)
+
+    scratch = (send_ref, cov_ref, low_ref, left_ref)
+
+    def stores(step):
+        pairs = zip(scratch, (send_hbm, cov_hbm, low_hbm, left_hbm), places(step))
         return [
             pltpu.make_async_copy(source.at[place], target.at[place], out_sems.at[step, at])
             for at, (source, target, place) in enumerate(pairs)
         ]
 
-    for head in range(HEADS):
-        for at in range(4):
-            load(at, head).start()
-
-    @pl.loop(0, HEADS // EXTRACT_HEADS)
+    @pl.loop(0, HEADS // n)
     def _(step):
-        first = step * EXTRACT_HEADS
-        for i in range(EXTRACT_HEADS):
-            for at in range(4):
-                load(at, first + i).wait()
-        here = [ref.at[pl.ds(first, EXTRACT_HEADS)] for ref in (q_all, k_all, v_all, g_all)]
-        out = [ref.at[place] for ref, place in zip((send_ref, cov_ref, left_ref), places(step))]
-        extract_heads(first, off2_ref, off3_ref, *here, *out)
-        for copy in give(step):
+        for copy in loads(step):
             copy.start()
 
-    for step in range(HEADS // EXTRACT_HEADS):
-        for copy in give(step):
+    @pl.loop(0, HEADS // n)
+    def _(step):
+        for copy in loads(step):
             copy.wait()
-
-
-def extract_heads(first_head, off2_ref, off3_ref, q_ref, k_ref, v_ref, g_ref, send_ref, cov_ref, left_ref):
+        here = [ref.at[step] for ref in (q_all, k_all, v_all, g_all)]
+        out = [ref.at[place] for ref, place in zip(scratch, places(step))]
+        extract_heads(step * n, off2_ref, off3_ref, *here, *out)
+        for copy in stores(step):
+            copy.start()
+
+    @pl.loop(0, HEADS // n)
+    def _(step):
+        for copy in stores(step):
+            copy.wait()
+
+
+def extract_heads(first_head, off2_ref, off3_ref, q_ref, k_ref, v_ref, g_ref, send_ref, cov_ref, low_ref, left_ref):
     cells = [(i, t) for i in range(EXTRACT_HEADS) for t in range(2)]
 
     def block(ref, cell):
         i, t = cell
-        return ref[i, t * SEG1 : (t + 1) * SEG1, :]
-
-    selects, valids = [], []
+        return ref[t * MID : (t + 1) * MID, :, :, i * WIDTH : (i + 1) * WIDTH].reshape(SEG1, WIDTH)
+
+    def pick(cell):
+        i, t = cell
+        off_two, off_three = off2_ref[first_head + i], off3_ref[first_head + i]
+        lane = slice(i * WIDTH, (i + 1) * WIDTH)
+        refs = (q_ref, k_ref, v_ref, g_ref)
+        slabs = [ref[t * MID : (t + 1) * MID, off_two // HALF, :, lane].reshape(MID * HALF, WIDTH) for ref in refs]
+        place = t * MID + off_three // DILATION_TWO
+        others = [ref[place, (off_three % DILATION_TWO) // HALF, :, lane] for ref in refs]
+        select = iota((MID, MID * HALF), 1) == HALF * iota((MID, 1), 0) + off_two % HALF
+        select_far = (iota((MID, HALF), 1) == off_three % HALF) & (iota((MID, HALF), 0) == 0)
+        return jnp.concatenate(
+            [
+                dot_nn(select.astype(BF16), jnp.concatenate(slabs, 1)),
+                dot_nn(select_far.astype(BF16), jnp.concatenate(others, 1)),
+            ],
+            0,
+        )
+
+    valids = []
     row = iota((COV, 1), 0)
     for i in range(EXTRACT_HEADS):
-        head = first_head + i
-        off_two, off_three = off2_ref[head], off3_ref[head]
-        position = targets((COV, 1), 0, off_two, off_three)
-        selects.append((iota((COV, SEG1), 1) == position).astype(BF16))
-        twice = (off_three % DILATION_TWO) == off_two
+        twice = (off3_ref[first_head + i] % DILATION_TWO) == off2_ref[first_head + i]
         valids.append(((row < MID) | ((row == MID) & jnp.logical_not(twice))).astype(F32))
-    picked = [
-        dot_nn(selects[cell[0]], jnp.concatenate([block(r, cell) for r in (q_ref, k_ref, v_ref, g_ref)], 1))
-        for cell in cells
-    ]
+    picked = [pick(cell) for cell in cells]
     low = [x.astype(BF16) for x in picked]
     scores = [dot_nt(x[:, :WIDTH], block(k_ref, cell)) for x, cell in zip(low, cells)]
     grads = [dot_nt(x[:, 3 * WIDTH :], block(v_ref, cell)) for x, cell in zip(low, cells)]
@@ -145,11 +163,11 @@
     g_cov = jnp.concatenate([x[:, 3 * WIDTH :] for x in picked], 0)
     delta = jnp.sum(g_cov * out, axis=1, keepdims=True)
     stats = lanes(split3(lse) + split3(delta), COV * len(cells))
+    shown = lanes([lse, delta], COV * len(cells))
     prob = weight * (jnp.concatenate([valids[i] for i, _ in cells], 0) / total)
     dscore = (prob * (grads - delta)).astype(BF16)
     prob = prob.astype(BF16)
     first = iota((MID, 1), 0) == 0
-    shape = (COV, WIDTH)
     for n, (i, t) in enumerate(cells):
         rows = slice(n * COV, (n + 1) * COV)
         own = stats[rows]
@@ -165,39 +183,38 @@
         for at, x in enumerate((*pair[1:], *mine)):
             far_block = far_block + pltpu.roll(x, at + 1, 0)
         send_ref[2 * i + t, 7 * MID :, :] = far_block.astype(BF16)
-        kept = (
-            picked[n][:, :WIDTH], picked[n][:, 3 * WIDTH :], out[rows],
-            jnp.broadcast_to(lse[rows], shape), jnp.broadcast_to(delta[rows], shape),
-        )
-        for at, x in enumerate(kept):
+        both = dot_nn(jnp.concatenate([dscore[rows], prob[rows]], 0), block(k_ref, (i, t)))
+        for at, x in enumerate((out[rows], both[:COV], both[COV:], shown[rows])):
             cov_ref[at, i, t] = x
-        keys = block(k_ref, (i, t))
-        both = dot_nn(jnp.concatenate([dscore[rows], prob[rows]], 0), keys)
-        cov_ref[5, i, t] = both[:COV]
-        cov_ref[6, i, t] = both[COV:]
-        chosen = selects[i] * valids[i].astype(BF16)
-        left_ref[i, t] = jnp.concatenate([dscore[rows], prob[rows], chosen, chosen], 0).T
+        low_ref[0, i, t] = low[n][:, :WIDTH]
+        low_ref[1, i, t] = low[n][:, 3 * WIDTH :]
+    for i in range(EXTRACT_HEADS):
+        parts = [x[n * COV : (n + 1) * COV] for n in (2 * i, 2 * i + 1) for x in (dscore, prob)]
+        left_ref[i] = jnp.concatenate(parts, 0).T
 
 
 def extract(offsets, q, k, v, g):
     smem, hbm = pl.BlockSpec(memory_space=pltpu.SMEM), pl.BlockSpec(memory_space=pl.ANY)
+    steps = HEADS // EXTRACT_HEADS
+    period = (2 * MID, 2, HALF)
     shapes = [
         ((2 * HEADS, PACK, WIDTH), BF16),
-        ((KEPT, HEADS, 2, COV, WIDTH), F32),
-        ((HEADS, 2, SEG1, 4 * COV), BF16),
+        ((4, HEADS, 2, COV, WIDTH), F32),
+        ((2, HEADS, 2, COV, WIDTH), BF16),
+        ((HEADS, SEG1, 4 * COV), BF16),
     ]
     return pl.pallas_call(
         extract_kernel,
         in_specs=[smem, smem] + [hbm] * 4,
-        out_specs=[hbm] * 3,
-        out_shape=[jax.ShapeDtypeStruct(*x) for x in shapes],
-        scratch_shapes=[pltpu.VMEM((HEADS, 2 * SEG1, WIDTH), BF16)] * 4
+        out_specs=[hbm] * 4,
+        out_shape=[pltpu.HBM(*x) for x in shapes],
+        scratch_shapes=[pltpu.VMEM((steps, *period, EXTRACT_HEADS * WIDTH), BF16)] * 4
         + [pltpu.VMEM(*x) for x in shapes]
-        + [pltpu.SemaphoreType.DMA((HEADS, 4)), pltpu.SemaphoreType.DMA((HEADS // EXTRACT_HEADS, 3))],
-        compiler_params=pltpu.CompilerParams(vmem_limit_bytes=VMEM),
+        + [pltpu.SemaphoreType.DMA((steps, 4))] * 2,
+        compiler_params=pltpu.CompilerParams(vmem_limit_bytes=63 * 2**20),
         cost_estimate=pl.CostEstimate(flops=2**32, bytes_accessed=12 * 2**20, transcendentals=2**18),
         name="extract",
-    )(*offsets, q, k, v, g)
+    )(*offsets, *in_hbm([x.reshape(*period, HEADS * WIDTH) for x in (q, k, v, g)]))
 
 
 def local_kernel(first, count, kept, off2_ref, off3_ref, *refs):
@@ -274,8 +291,7 @@
         lambda *refs: local_kernel(first, count, len(earlier), *refs),
         in_specs=[smem, smem] + [hbm] * (4 + len(earlier)),
         out_specs=[hbm] * 4,
-        out_shape=[jax.ShapeDtypeStruct((2, *period, HEADS * WIDTH), BF16)] * 2
-        + [jax.ShapeDtypeStruct((HEADS, 2 * SEG1, WIDTH), BF16)] * 2,
+        out_shape=[pltpu.HBM((2, *period, HEADS * WIDTH), BF16)] * 2 + [pltpu.HBM((HEADS, 2 * SEG1, WIDTH), BF16)] * 2,
         input_output_aliases={6 + at: at for at in range(len(earlier))},
         scratch_shapes=[pltpu.VMEM((count, 2 * SEG1, WIDTH), BF16)] * 4
         + [pltpu.VMEM((count, 2, *period, WIDTH), BF16)] * 2
@@ -286,7 +302,7 @@
             flops=int(share * 12 * 2**30), bytes_accessed=int(share * 16 * 2**20), transcendentals=int(share * 2**22)
         ),
         name="local",
-    )(*offsets, *arrays, *earlier)
+    )(*offsets, *in_hbm((*arrays, *earlier)))
 
 
 def merge_lse(parts):
@@ -447,7 +463,7 @@
     )[0]
 
 
-def prepare(off2_ref, off3_ref, cov_ref, back_ref, right_ref, rows_ref):
+def prepare(off2_ref, off3_ref, cov_ref, low_ref, back_ref, right_ref, rows_ref):
     cells, rows = 2 * HEADS, 2 * HEADS * COV
     back = back_ref[...].astype(F32)
 
@@ -477,7 +493,9 @@
     def joined(x):
         return dot_nn(x.astype(BF16), ones)
 
-    q, g, out, lse1, delta1, dq_one, dq_two = (cov_ref[at].reshape(rows, WIDTH) for at in range(KEPT))
+    q, g = (low_ref[at].reshape(rows, WIDTH).astype(F32) for at in range(2))
+    out, dq_one, dq_two, figures = (cov_ref[at].reshape(rows, WIDTH) for at in range(4))
+    lse1, delta1 = figures[:, 0:1], figures[:, 1:2]
     packed = back[:, 7 * MID : 8 * MID]
     far = packed[:, 3:7].reshape(HEADS, 2, 4, WIDTH)
     far = (far[:, 0] + far[:, 1]).reshape(HEADS, 2, 2, WIDTH)
@@ -494,24 +512,32 @@
     dk = both(0) + jnp.where(is_far, spread(far[:, 0]), 0.0)
     dv = both(2) + jnp.where(is_far, spread(far[:, 1]), 0.0)
 
-    def put(at, column, x):
-        right_ref[:, at * COV : (at + 1) * COV, column * WIDTH : (column + 1) * WIDTH] = x.astype(BF16).reshape(
-            cells, COV, WIDTH
-        )
-
-    def put_two(column, x):
+    def column(at):
+        return slice(at * WIDTH, (at + 1) * WIDTH)
+
+    def put(at, to, x):
+        x = x.astype(BF16).reshape(HEADS, 2, COV, WIDTH)
+        for t in range(2):
+            start = (2 * t + at) * COV
+            right_ref[:, t, start : start + COV, column(to)] = x[:, t]
+
+    def put_rows(to, x):
         high = x.astype(BF16)
-        put(2, column, high)
-        put(3, column, x - high.astype(F32))
+        for at, part_ in enumerate((high, (x - high.astype(F32)).astype(BF16))):
+            start = (4 + at) * COV
+            right_ref[:, :, start : start + COV, column(to)] = part_.reshape(HEADS, 2, COV, WIDTH)
 
     rows_ref[0] = att.astype(F32).reshape(HEADS, 2, COV, WIDTH)
     rows_ref[1] = (FACTOR * dq).reshape(HEADS, 2, COV, WIDTH)
+    nothing = jnp.zeros((HEADS, 2 * COV, 2 * WIDTH), BF16)
+    right_ref[:, 0, 2 * COV : 4 * COV, :] = nothing
+    right_ref[:, 1, : 2 * COV, :] = nothing
     put(0, 0, share * q)
     put(1, 0, -change * q)
-    put_two(0, dk)
+    put_rows(0, dk)
     put(0, 1, jnp.zeros((rows, WIDTH), F32))
     put(1, 1, share * g)
-    put_two(1, dv)
+    put_rows(1, dv)
 
 
 def patch(off_two, off_three, rows_ref, head, at, slab_ref, other_ref):
@@ -533,14 +559,14 @@
 
 
 def finish_kernel(
-    off2_ref, off3_ref, cov_hbm, back_hbm, left_hbm, att_hbm, dq_hbm, dk_hbm, dv_hbm,
+    off2_ref, off3_ref, cov_hbm, low_hbm, back_hbm, left_hbm, att_hbm, dq_hbm, dk_hbm, dv_hbm,
     att_out, dq_out, dk_out, dv_out,
-    cov_ref, back_ref, left_ref, right_ref, rows_ref, held, done_ref, slab_ref, other_ref,
+    cov_ref, low_ref, back_ref, left_ref, right_ref, rows_ref, held, done_ref, slab_ref, other_ref,
     first_sems, in_sems, out_sems, slab_in, slab_out,
 ):
     first = [
         pltpu.make_async_copy(source, target, first_sems.at[at])
-        for at, (source, target) in enumerate(((back_hbm, back_ref), (cov_hbm, cov_ref)))
+        for at, (source, target) in enumerate(((back_hbm, back_ref), (cov_hbm, cov_ref), (low_hbm, low_ref)))
     ]
 
     def slabs(head, arrays):
@@ -582,7 +608,7 @@
 
     for copy in first:
         copy.wait()
-    prepare(off2_ref, off3_ref, cov_ref, back_ref, right_ref, rows_ref)
+    prepare(off2_ref, off3_ref, cov_ref, low_ref, back_ref, right_ref, rows_ref)
 
     @pl.loop(0, HEADS)
     def _(head):
@@ -592,9 +618,15 @@
             patch(off2_ref[head], off3_ref[head], rows_ref, head, at, slab_ref, other_ref)
         for copy in slab_stores(head):
             copy.start()
+        off_two, off_three = off2_ref[head], off3_ref[head]
+        place = targets((1, 2 * COV), 1, off_two, off_three)
+        twice = (off_three % DILATION_TWO) == off_two
+        place = jnp.where(((iota((1, 2 * COV), 1) % COV) == MID) & twice, -1, place)
+        select = (iota((SEG1, 2 * COV), 0) == place).astype(BF16)
+        left = jnp.concatenate([left_ref[head], select], 1)
         for t in range(2):
             rows = slice(t * SEG1, (t + 1) * SEG1)
-            x = dot_nn(left_ref[head, t], right_ref[2 * head + t])
+            x = dot_nn(left, right_ref[head, t])
             done_ref[0, head, rows, :] = (FACTOR * (held[0, head, rows, :].astype(F32) + x[:, :WIDTH])).astype(BF16)
             done_ref[1, head, rows, :] = (held[1, head, rows, :].astype(F32) + x[:, WIDTH:]).astype(BF16)
         for copy in stores(head):
@@ -606,25 +638,25 @@
             copy.wait()
 
 
-def finish(offsets, cov, left, back, att, dq, dk, dv):
+def finish(offsets, cov, low, left, back, att, dq, dk, dv):
     smem, hbm = pl.BlockSpec(memory_space=pltpu.SMEM), pl.BlockSpec(memory_space=pl.ANY)
     kind = (2, HEADS, 2 * SEG1, WIDTH)
     whole = (2 * SEG1, HEADS * WIDTH)
     att, dq, dk, dv = pl.pallas_call(
         finish_kernel,
-        in_specs=[smem, smem] + [hbm] * 7,
+        in_specs=[smem, smem] + [hbm] * 8,
         out_specs=[hbm] * 4,
-        out_shape=[jax.ShapeDtypeStruct(att.shape, BF16)] * 2 + [jax.ShapeDtypeStruct(whole, BF16)] * 2,
-        input_output_aliases={5: 0, 6: 1},
-        scratch_shapes=[pltpu.VMEM(x.shape, x.dtype) for x in (cov, back, left)]
+        out_shape=[pltpu.HBM(att.shape, BF16)] * 2 + [pltpu.HBM(whole, BF16)] * 2,
+        input_output_aliases={6: 0, 7: 1},
+        scratch_shapes=[pltpu.VMEM(x.shape, x.dtype) for x in (cov, low, back, left)]
         + [
-            pltpu.VMEM((2 * HEADS, 4 * COV, 2 * WIDTH), BF16),
+            pltpu.VMEM((HEADS, 2, 6 * COV, 2 * WIDTH), BF16),
             pltpu.VMEM((2, HEADS, 2, COV, WIDTH), F32),
             pltpu.VMEM(kind, BF16),
             pltpu.VMEM(kind, BF16),
             pltpu.VMEM((2, HEADS, 2, MID, HALF, WIDTH), BF16),
             pltpu.VMEM((2, HEADS, 2, HALF, WIDTH), BF16),
-            pltpu.SemaphoreType.DMA((2,)),
+            pltpu.SemaphoreType.DMA((3,)),
             pltpu.SemaphoreType.DMA((HEADS, 3)),
             pltpu.SemaphoreType.DMA((HEADS, 2)),
             pltpu.SemaphoreType.DMA((HEADS, 4)),
@@ -633,7 +665,7 @@
         compiler_params=pltpu.CompilerParams(vmem_limit_bytes=VMEM),
         cost_estimate=pl.CostEstimate(flops=2**30, bytes_accessed=17 * 2**20, transcendentals=2**18),
         name="finish",
-    )(*offsets, cov, back, left, att, dq, dk, dv)
+    )(*offsets, *in_hbm((cov, low)), back, *in_hbm((left, att, dq, dk, dv)))
     return att.reshape(whole), dq.reshape(whole), dk, dv
 
 
@@ -644,7 +676,7 @@
     def body(queries, keys, values, out_grad, middle_head_offsets, distant_head_offsets):
         offsets = (middle_head_offsets, distant_head_offsets)
         arrays = (queries, keys, values, out_grad)
-        send, cov, left = extract(offsets, *arrays)
+        send, cov, low, left = extract(offsets, *arrays)
         got = lax.all_to_all(send, "inner", 0, 0)
         parts = local(offsets, arrays, 0, SHARES[0], ())
         got, *parts = lax.optimization_barrier((got, *parts))
@@ -658,7 +690,7 @@
         back = lax.all_to_all(back, "inner", 0, 0)
         parts = local(offsets, arrays, SHARES[0] + SHARES[1], SHARES[2], parts)
         back, *parts = lax.optimization_barrier((back, *parts))
-        return finish(offsets, cov, left, back, *parts)
+        return finish(offsets, cov, low, left, back, *parts)
 
     return jax.shard_map(
         body, mesh=mesh, in_specs=(split,) * 4 + (P(), P()), out_specs=(split,) * 4, check_vma=False

time: 76.6 us -> 71.6 us (0.935)
  Pallas kernels: 52.5 us -> 49.7 us
  local copies, waits for them, and re-layouts: 2.34 us -> 0.01 us
    unnamed x6 -> x4, local copies, waits for them, and re-layouts: 2.34 us -> 0.01 us
    pallas_call x2, Pallas kernels: 5.84 us -> 4.66 us  [remote_call(): pl.pallas_call(kernel, in_specs=[smem, smem] + [vmem] * len(arrays), out_...]
    pallas_call x1, Pallas kernels: 8.58 us -> 7.6 us  [extract(): pl.pallas_call(extract_kernel, in_specs=[smem, smem] + [hbm] * 4, out_spe...]
  transfers between devices with their start and end apart: 3 -> 3, of which waited for: 0 -> 0; matrix products, arithmetic and copies ran while one was open for 0% -> 0% of each run, Pallas kernels for 39% -> 41%
where the time goes in v4:
time: 71.6 us; the launch traced here: 71.1 us
  Pallas kernels  49.7 us (69%)
  starting transfers between devices  20.5 us (29%)
  between operations  0.88 us (1%)
    pallas_call x3, Pallas kernels, local(): pl.pallas_call(lambda *refs: local_kernel(first, count, len(earlier), *re...  29.2 us
    pallas_call x1, Pallas kernels, finish(): pl.pallas_call(finish_kernel, in_specs=[smem, smem] + [hbm] * 8, out_spec...  8.32 us
    pallas_call x1, Pallas kernels, extract(): pl.pallas_call(extract_kernel, in_specs=[smem, smem] + [hbm] * 4, out_spe...  7.6 us
    all_to_all x1, starting transfers between devices, body(): far = lax.all_to_all(far, 'outer', 0, 0)  7.38 us
    all_to_all x1, starting transfers between devices, body(): got = lax.all_to_all(send, 'inner', 0, 0)  6.84 us
    all_to_all x1, starting transfers between devices, body(): back = lax.all_to_all(back, 'inner', 0, 0)  6.25 us
    pallas_call x2, Pallas kernels, remote_call(): pl.pallas_call(kernel, in_specs=[smem, smem] + [vmem] * len(arrays), out_...  4.66 us
  transfers between devices with their start and end apart: 3, of which 0 were waited for; matrix products, arithmetic and copies ran while one was open for 0% of the time, Pallas kernels for 41%

profile of v4, /device:TPU:1, one launch (start us, length us, event | category | flops | bytes accessed | tf_op | source)
XLA Modules:
  0.0 71.1 jit_solution(5874651395113674913)
XLA Ops:
  0.6 0.0 copy-start
  0.6 0.0 copy-start.1
  0.7 7.6 %extract.1 = (bf16[16,128,128]{2,1,0:T(8,128)(2,1)}, f32[4,8,2,32,128]{4,3,2,1,0:T(8,128)}, bf16[2,8,2,32,128]{4,3,2,1,0:T(8,128)(2,1)}, bf16[8,512,128]{2,1,0:T(8,128)(2,1)}) custom-call(s32[8]{0:T(128)} %off2_ref.7, s32[8]{0:T(128)} %off3_ref.7, bf16[32,2,16,1024]{3,2,1,0:T(8,128)(2,1)} %bitcast.8, bf16[32,2,16,1024]{3,2,1,0:T(8,128)(2,1)} %bitcast.9, ...), custom_call_target="tpu_custom_call" | custom-call | flops 4294967296 | bytes 12582912 | tf_op jit(solution)/shard_map/extract/pallas_call | solution.py:206
  8.3 6.8 %all-to-all-start = ((bf16[16,128,128]{2,1,0:T(8,128)(2,1)}), bf16[16,128,128]{2,1,0:T(8,128)(2,1)S(1)}, u32[]{:S(2)}, u32[]{:S(2)}) async-start(bf16[16,128,128]{2,1,0:T(8,128)(2,1)} %get-tuple-element.54), calls=%async_computation | async-start | bytes 1048576 | tf_op jit(solution)/shard_map/all_to_all | solution.py:680
  15.1 0.0 copy-done
  15.1 0.0 copy-done.1
  15.1 10.7 %local.3 = (bf16[2,16,2,16,1024]{4,3,2,1,0:T(8,128)(2,1)}, bf16[2,16,2,16,1024]{4,3,2,1,0:T(8,128)(2,1)}, bf16[8,1024,128]{2,1,0:T(8,128)(2,1)}, bf16[8,1024,128]{2,1,0:T(8,128)(2,1)}) custom-call(s32[8]{0:T(128)S(1)} %copy-done, s32[8]{0:T(128)S(1)} %copy-done.1, bf16[1024,1024]{1,0:T(8,128)(2,1)} %refs_2_.5, bf16[1024,1024]{1,0:T(8,128)(2,1)} %refs_3_.5, ...), custom_call_target="tpu_custom_call" | custom-call | flops 4831838208 | bytes 6291456 | tf_op jit(solution)/shard_map/local/pallas_call | solution.py:290
  25.8 0.0 all-to-all-done.in_ref
  25.8 1.9 %remote_forward.1 = (bf16[8,112,128]{2,1,0:T(8,128)(2,1)}, bf16[256,128]{1,0:T(8,128)(2,1)S(1)}, f32[256,128]{1,0:T(8,128)S(1)}) custom-call(s32[8]{0:T(128)S(1)} %copy-done, s32[8]{0:T(128)S(1)} %copy-done.1, bf16[16,128,128]{2,1,0:T(8,128)(2,1)S(1)} %all-to-all-done.in_ref), custom_call_target="tpu_custom_call" | custom-call | flops 2147483648 | bytes 2097152 | tf_op jit(solution)/shard_map/remote_forward/pallas_call | solution.py:435
  27.7 7.4 %all-to-all-start.1 = ((bf16[8,112,128]{2,1,0:T(8,128)(2,1)}), bf16[8,112,128]{2,1,0:T(8,128)(2,1)S(1)}, u32[]{:S(2)}, u32[]{:S(2)}) async-start(bf16[8,112,128]{2,1,0:T(8,128)(2,1)} %get-tuple-element.65), calls=%async_computation.1 | async-start | bytes 458752 | tf_op jit(solution)/shard_map/all_to_all | solution.py:685
  35.1 7.9 %local.4 = (bf16[2,16,2,16,1024]{4,3,2,1,0:T(8,128)(2,1)}, bf16[2,16,2,16,1024]{4,3,2,1,0:T(8,128)(2,1)}, bf16[8,1024,128]{2,1,0:T(8,128)(2,1)}, bf16[8,1024,128]{2,1,0:T(8,128)(2,1)}) custom-call(s32[8]{0:T(128)S(1)} %copy-done, s32[8]{0:T(128)S(1)} %copy-done.1, ...), custom_call_target="tpu_custom_call", output_to_operand_aliasing={{0}: (6, {}), {1}: (7, {}), {2}: (8, {}), {3}: (9, {})} | custom-call | flops 3221225472 | bytes 4194304 | tf_op jit(solution)/shard_map/local/pallas_call | solution.py:290
  43.0 0.0 all-to-all-done.1.far_ref
  43.0 2.7 %remote_backward.1 = bf16[16,128,128]{2,1,0:T(8,128)(2,1)} custom-call(s32[8]{0:T(128)S(1)} %copy-done, s32[8]{0:T(128)S(1)} %copy-done.1, bf16[16,128,128]{2,1,0:T(8,128)(2,1)S(1)} %all-to-all-done.in_ref, bf16[8,112,128]{2,1,0:T(8,128)(2,1)S(1)} %all-to-all-done.1.far_ref, bf16[256,128]{1,0:T(8,128)(2,1)S(1)} %get-tuple-element.75.out2_ref, ...), custom_call_target="tpu_custom_call" | custom-call | flops 2147483648 | bytes 2097152 | tf_op jit(solution)/shard_map/remote_backward/pallas_call | solution.py:435
  45.7 6.2 %all-to-all-start.2 = ((bf16[16,128,128]{2,1,0:T(8,128)(2,1)}), bf16[16,128,128]{2,1,0:T(8,128)(2,1)S(1)}, u32[]{:S(2)}, u32[]{:S(2)}) async-start(bf16[16,128,128]{2,1,0:T(8,128)(2,1)} %remote_backward.1), calls=%async_computation.2 | async-start | bytes 1048576 | tf_op jit(solution)/shard_map/all_to_all | solution.py:690
  52.0 10.6 %local.5 = (bf16[2,16,2,16,1024]{4,3,2,1,0:T(8,128)(2,1)}, bf16[2,16,2,16,1024]{4,3,2,1,0:T(8,128)(2,1)}, bf16[8,1024,128]{2,1,0:T(8,128)(2,1)}, bf16[8,1024,128]{2,1,0:T(8,128)(2,1)}) custom-call(s32[8]{0:T(128)S(1)} %copy-done, s32[8]{0:T(128)S(1)} %copy-done.1, ...), custom_call_target="tpu_custom_call", output_to_operand_aliasing={{0}: (6, {}), {1}: (7, {}), {2}: (8, {}), {3}: (9, {})} | custom-call | flops 4831838208 | bytes 6291456 | tf_op jit(solution)/shard_map/local/pallas_call | solution.py:290
  62.6 0.0 all-to-all-done.2.back_hbm
  62.6 8.3 %finish.1 = (bf16[2,16,2,16,1024]{4,3,2,1,0:T(8,128)(2,1)}, bf16[2,16,2,16,1024]{4,3,2,1,0:T(8,128)(2,1)}, bf16[1024,1024]{1,0:T(8,128)(2,1)}, bf16[1024,1024]{1,0:T(8,128)(2,1)}) custom-call(s32[8]{0:T(128)S(1)} %copy-done, s32[8]{0:T(128)S(1)} %copy-done.1, ...), custom_call_target="tpu_custom_call", output_to_operand_aliasing={{0}: (6, {}), {1}: (7, {})} | custom-call | flops 1073741824 | bytes 17825792 | tf_op jit(solution)/shard_map/finish/pallas_call | solution.py:645
Async XLA Ops:
  0.6 14.5 %copy-start = (s32[8]{0:T(128)S(1)}, s32[8]{0:T(128)}, u32[]{:S(2)}) copy-start(s32[8]{0:T(128)} %off2_ref.7) | copy-start | bytes 100
  0.6 14.5 %copy-start.1 = (s32[8]{0:T(128)S(1)}, s32[8]{0:T(128)}, u32[]{:S(2)}) copy-start(s32[8]{0:T(128)} %off3_ref.7) | copy-start | bytes 100
  8.3 17.5 %all-to-all-start = ((bf16[16,128,128]{2,1,0:T(8,128)(2,1)}), bf16[16,128,128]{2,1,0:T(8,128)(2,1)S(1)}, u32[]{:S(2)}, u32[]{:S(2)}) async-start(bf16[16,128,128]{2,1,0:T(8,128)(2,1)} %get-tuple-element.54), calls=%async_computation | async-start | bytes 1048576 | tf_op jit(solution)/shard_map/all_to_all | solution.py:680
  27.7 15.2 %all-to-all-start.1 = ((bf16[8,112,128]{2,1,0:T(8,128)(2,1)}), bf16[8,112,128]{2,1,0:T(8,128)(2,1)S(1)}, u32[]{:S(2)}, u32[]{:S(2)}) async-start(bf16[8,112,128]{2,1,0:T(8,128)(2,1)} %get-tuple-element.65), calls=%async_computation.1 | async-start | bytes 458752 | tf_op jit(solution)/shard_map/all_to_all | solution.py:685
  45.7 16.9 %all-to-all-start.2 = ((bf16[16,128,128]{2,1,0:T(8,128)(2,1)}), bf16[16,128,128]{2,1,0:T(8,128)(2,1)S(1)}, u32[]{:S(2)}, u32[]{:S(2)}) async-start(bf16[16,128,128]{2,1,0:T(8,128)(2,1)} %remote_backward.1), calls=%async_computation.2 | async-start | bytes 1048576 | tf_op jit(solution)/shard_map/all_to_all | solution.py:690

commit v5 on v4

--- a/solution.py
+++ b/solution.py
@@ -17,7 +17,7 @@
 COV = 32
 PACK = 128
 EXTRACT_HEADS = 2
-SHARES = (3, 2, 3)
+SHARES = (5, 5, 6)
 VMEM = 44 * 2**20
 HALF = DILATION_TWO // 2
 NEG = -1e30
@@ -222,70 +222,70 @@
     held, done, (in_sems, out_sems) = refs[8 + kept : 12 + kept], refs[12 + kept : 16 + kept], refs[16 + kept :]
     position = iota((1, SEG1), 1)
 
-    def loads(i, t):
-        rows = pl.ds(t * SEG1, SEG1)
-        lane = pl.ds(pl.multiple_of((first + i) * WIDTH, WIDTH), WIDTH)
+    def place(c):
+        head, t = (first + c) // 2, (first + c) % 2
+        return head, t, pl.ds(pl.multiple_of(head * WIDTH, WIDTH), WIDTH), pl.ds(pl.multiple_of(t * SEG1, SEG1), SEG1)
+
+    def loads(c):
+        _, _, lane, rows = place(c)
         return [
-            pltpu.make_async_copy(sources[at].at[rows, lane], held[at].at[i, rows], in_sems.at[i, t, at])
-            for at in range(4)
+            pltpu.make_async_copy(sources[at].at[rows, lane], held[at].at[c], in_sems.at[c, at]) for at in range(4)
         ]
 
-    def stores(i, t):
-        lane = pl.ds(pl.multiple_of((first + i) * WIDTH, WIDTH), WIDTH)
-        rows = pl.ds(t * SEG1, SEG1)
+    def stores(c):
+        head, t, lane, rows = place(c)
         return [
             pltpu.make_async_copy(
-                done[at].at[i, t], outs[at].at[t, :, :, :, lane] if at < 2 else outs[at].at[first + i, rows],
-                out_sems.at[i, t, at],
+                done[at].at[c], outs[at].at[t, :, :, :, lane] if at < 2 else outs[at].at[head, rows], out_sems.at[c, at]
             )
             for at in range(4)
         ]
 
-    def start(i):
-        for t in range(2):
-            for copy in loads(i, t):
-                copy.start()
+    def start(c):
+        for copy in loads(c):
+            copy.start()
 
     start(0)
+    start(1)
 
     @pl.loop(0, count)
-    def _(i):
-        @pl.when(i + 1 < count)
+    def _(c):
+        @pl.when(c + 2 < count)
         def _():
-            start(i + 1)
-
-        head = first + i
+            start(c + 2)
+
+        head = (first + c) // 2
         covered = ((position & (DILATION_TWO - 1)) == off2_ref[head]) | (position == off3_ref[head])
-        for t in range(2):
-            for copy in loads(i, t):
-                copy.wait()
-            rows = slice(t * SEG1, (t + 1) * SEG1)
-            q, k, v, g = (ref[i, rows, :] for ref in held)
-            scores = dot_nt(k, q) * (FACTOR * math.log2(math.e))
-            grad = dot_nt(v, g)
-            weight = jnp.exp2(scores - jnp.max(scores, axis=0, keepdims=True))
-            inverse = 1.0 / jnp.sum(weight, axis=0, keepdims=True)
-            att = (dot_nn(v.T, weight.astype(BF16)) * inverse).astype(BF16)
-            delta = jnp.sum(g.T.astype(F32) * att.astype(F32), axis=0, keepdims=True)
-            done[0][i, t] = att.T.reshape(MID, 2, HALF, WIDTH)
-            prob = weight * jnp.where(covered, 0.0, inverse)
-            dscore = (prob * (grad - delta)).astype(BF16)
-            done[1][i, t] = (dot_nn(k.T, dscore) * FACTOR).astype(BF16).T.reshape(MID, 2, HALF, WIDTH)
-            done[2][i, t] = dot_nn(dscore, q).astype(BF16)
-            done[3][i, t] = dot_nn(prob.astype(BF16), g).astype(BF16)
-            for copy in stores(i, t):
-                copy.start()
+        for copy in loads(c):
+            copy.wait()
+        q, k, v, g = (ref[c] for ref in held)
+        scores = dot_nt(k, q) * (FACTOR * math.log2(math.e))
+        grad = dot_nt(v, g)
+        weight = jnp.exp2(scores - jnp.max(scores, axis=0, keepdims=True))
+        inverse = 1.0 / jnp.sum(weight, axis=0, keepdims=True)
+        att = (dot_nn(v.T, weight.astype(BF16)) * inverse).astype(BF16)
+        delta = jnp.sum(g.T.astype(F32) * att.astype(F32), axis=0, keepdims=True)
+        out = stores(c)
+        done[0][c] = att.T.reshape(MID, 2, HALF, WIDTH)
+        out[0].start()
+        prob = weight * jnp.where(covered, 0.0, inverse)
+        dscore = (prob * (grad - delta)).astype(BF16)
+        done[1][c] = (dot_nn(k.T, dscore) * FACTOR).astype(BF16).T.reshape(MID, 2, HALF, WIDTH)
+        out[1].start()
+        done[2][c] = dot_nn(dscore, q).astype(BF16)
+        out[2].start()
+        done[3][c] = dot_nn(prob.astype(BF16), g).astype(BF16)
+        out[3].start()
 
     @pl.loop(0, count)
-    def _(i):
-        for t in range(2):
-            for copy in stores(i, t):
-                copy.wait()
+    def _(c):
+        for copy in stores(c):
+            copy.wait()
 
 
 def local(offsets, arrays, first, count, earlier):
     smem, hbm = pl.BlockSpec(memory_space=pltpu.SMEM), pl.BlockSpec(memory_space=pl.ANY)
-    share = count / HEADS
+    share = count / (2 * HEADS)
     period = (MID, 2, HALF)
     return pl.pallas_call(
         lambda *refs: local_kernel(first, count, len(earlier), *refs),
@@ -293,10 +293,10 @@
         out_specs=[hbm] * 4,
         out_shape=[pltpu.HBM((2, *period, HEADS * WIDTH), BF16)] * 2 + [pltpu.HBM((HEADS, 2 * SEG1, WIDTH), BF16)] * 2,
         input_output_aliases={6 + at: at for at in range(len(earlier))},
-        scratch_shapes=[pltpu.VMEM((count, 2 * SEG1, WIDTH), BF16)] * 4
-        + [pltpu.VMEM((count, 2, *period, WIDTH), BF16)] * 2
-        + [pltpu.VMEM((count, 2, SEG1, WIDTH), BF16)] * 2
-        + [pltpu.SemaphoreType.DMA((count, 2, 4))] * 2,
+        scratch_shapes=[pltpu.VMEM((count, SEG1, WIDTH), BF16)] * 4
+        + [pltpu.VMEM((count, *period, WIDTH), BF16)] * 2
+        + [pltpu.VMEM((count, SEG1, WIDTH), BF16)] * 2
+        + [pltpu.SemaphoreType.DMA((count, 4))] * 2,
         compiler_params=pltpu.CompilerParams(vmem_limit_bytes=VMEM),
         cost_estimate=pl.CostEstimate(
             flops=int(share * 12 * 2**30), bytes_accessed=int(share * 16 * 2**20), transcendentals=int(share * 2**22)
@@ -540,33 +540,31 @@
     put_rows(1, dv)
 
 
-def patch(off_two, off_three, rows_ref, head, at, slab_ref, other_ref):
-    half = off_two // HALF
+def patch(off_two, off_three, rows_ref, head, at, slab_ref, other_ref, wide_ref):
+    size = 2 * MID * HALF
     twice = (off_three % DILATION_TWO) == off_two
-    beside = ((off_three % DILATION_TWO) // HALF) == half
-    mid = rows_ref[at, head, :, :MID].reshape(2 * MID, 1, WIDTH)
+    beside = ((off_three % DILATION_TWO) // HALF) == (off_two // HALF)
     far = rows_ref[at, head, :, MID : MID + 1]
-    shape = (2 * MID, HALF, WIDTH)
-    row = iota(shape, 1)
-    old = slab_ref[at, head].astype(F32).reshape(shape)
-    here = (row == off_three % HALF) & ((iota(shape, 0) & (MID - 1)) == off_three // DILATION_TWO)
-    here = here & beside & jnp.logical_not(twice)
-    wide = jnp.broadcast_to(far, (2, MID, WIDTH)).reshape(2 * MID, 1, WIDTH)
-    slab = jnp.where(here, wide, jnp.where(row == off_two % HALF, mid, old))
-    slab_ref[at, head] = slab.astype(BF16).reshape(2, MID, HALF, WIDTH)
+    wide_ref[at, :size, :] = slab_ref[at, head].astype(F32).reshape(size, WIDTH)
+    wide_ref[at, pl.ds(off_two % HALF, 2 * MID, stride=HALF), :] = rows_ref[at, head, :, :MID].reshape(2 * MID, WIDTH)
+    for t in range(2):
+        spot = (t * MID + off_three // DILATION_TWO) * HALF + off_three % HALF
+        spot = jnp.where(beside & jnp.logical_not(twice), spot, size)
+        wide_ref[at, pl.ds(spot, 1), :] = far[t]
+    slab_ref[at, head] = wide_ref[at, :size, :].astype(BF16).reshape(2, MID, HALF, WIDTH)
     there = (iota((2, HALF, WIDTH), 1) == off_three % HALF) & jnp.logical_not(beside)
     other_ref[at, head] = jnp.where(there, far, other_ref[at, head].astype(F32)).astype(BF16)
 
 
 def finish_kernel(
-    off2_ref, off3_ref, cov_hbm, low_hbm, back_hbm, left_hbm, att_hbm, dq_hbm, dk_hbm, dv_hbm,
+    off2_ref, off3_ref, cov_hbm, low_hbm, back_ref, left_hbm, att_hbm, dq_hbm, dk_hbm, dv_hbm,
     att_out, dq_out, dk_out, dv_out,
-    cov_ref, low_ref, back_ref, left_ref, right_ref, rows_ref, held, done_ref, slab_ref, other_ref,
+    cov_ref, low_ref, left_ref, right_ref, rows_ref, held, done_ref, slab_ref, other_ref, wide_ref,
     first_sems, in_sems, out_sems, slab_in, slab_out,
 ):
     first = [
         pltpu.make_async_copy(source, target, first_sems.at[at])
-        for at, (source, target) in enumerate(((back_hbm, back_ref), (cov_hbm, cov_ref), (low_hbm, low_ref)))
+        for at, (source, target) in enumerate(((cov_hbm, cov_ref), (low_hbm, low_ref)))
     ]
 
     def slabs(head, arrays):
@@ -615,7 +613,7 @@
         for copy in loads(head):
             copy.wait()
         for at in range(2):
-            patch(off2_ref[head], off3_ref[head], rows_ref, head, at, slab_ref, other_ref)
+            patch(off2_ref[head], off3_ref[head], rows_ref, head, at, slab_ref, other_ref, wide_ref)
         for copy in slab_stores(head):
             copy.start()
         off_two, off_three = off2_ref[head], off3_ref[head]
@@ -644,11 +642,11 @@
     whole = (2 * SEG1, HEADS * WIDTH)
     att, dq, dk, dv = pl.pallas_call(
         finish_kernel,
-        in_specs=[smem, smem] + [hbm] * 8,
+        in_specs=[smem, smem, hbm, hbm, pl.BlockSpec(memory_space=pltpu.VMEM)] + [hbm] * 5,
         out_specs=[hbm] * 4,
         out_shape=[pltpu.HBM(att.shape, BF16)] * 2 + [pltpu.HBM(whole, BF16)] * 2,
         input_output_aliases={6: 0, 7: 1},
-        scratch_shapes=[pltpu.VMEM(x.shape, x.dtype) for x in (cov, low, back, left)]
+        scratch_shapes=[pltpu.VMEM(x.shape, x.dtype) for x in (cov, low, left)]
         + [
             pltpu.VMEM((HEADS, 2, 6 * COV, 2 * WIDTH), BF16),
             pltpu.VMEM((2, HEADS, 2, COV, WIDTH), F32),
@@ -656,7 +654,8 @@
             pltpu.VMEM(kind, BF16),
             pltpu.VMEM((2, HEADS, 2, MID, HALF, WIDTH), BF16),
             pltpu.VMEM((2, HEADS, 2, HALF, WIDTH), BF16),
-            pltpu.SemaphoreType.DMA((3,)),
+            pltpu.VMEM((2, 2 * MID * HALF + 8, WIDTH), F32),
+            pltpu.SemaphoreType.DMA((2,)),
             pltpu.SemaphoreType.DMA((HEADS, 3)),
             pltpu.SemaphoreType.DMA((HEADS, 2)),
             pltpu.SemaphoreType.DMA((HEADS, 4)),

time: 71.6 us -> 70.5 us (0.985)
  starting transfers between devices: 20.5 us -> 19.3 us
    all_to_all x1, starting transfers between devices: 6.25 us -> 5.11 us  [body(): back = lax.all_to_all(back, 'inner', 0, 0)]
  transfers between devices with their start and end apart: 3 -> 3, of which waited for: 0 -> 1; matrix products, arithmetic and copies ran while one was open for 0% -> 0% of each run, Pallas kernels for 41% -> 42%
where the time goes in v5:
time: 70.5 us; the launch traced here: 69.5 us
  Pallas kernels  49.2 us (70%)
  starting transfers between devices  19.3 us (27%)
  between operations  0.71 us (1%)
    pallas_call x3, Pallas kernels, local(): pl.pallas_call(lambda *refs: local_kernel(first, count, len(earlier), *re...  29.3 us
    pallas_call x1, Pallas kernels, finish(): pl.pallas_call(finish_kernel, in_specs=[smem, smem, hbm, hbm, pl.BlockSpe...  7.62 us
    pallas_call x1, Pallas kernels, extract(): pl.pallas_call(extract_kernel, in_specs=[smem, smem] + [hbm] * 4, out_spe...  7.61 us
    all_to_all x1, starting transfers between devices, body(): far = lax.all_to_all(far, 'outer', 0, 0)  7.37 us
    all_to_all x1, starting transfers between devices, body(): got = lax.all_to_all(send, 'inner', 0, 0)  6.84 us
    all_to_all x1, starting transfers between devices, body(): back = lax.all_to_all(back, 'inner', 0, 0)  5.11 us
    pallas_call x2, Pallas kernels, remote_call(): pl.pallas_call(kernel, in_specs=[smem, smem] + [vmem] * len(arrays), out_...  4.66 us
  transfers between devices with their start and end apart: 3, of which 1 were waited for; matrix products, arithmetic and copies ran while one was open for 0% of the time, Pallas kernels for 42%

profile of v5, /device:TPU:1, one launch (start us, length us, event | category | flops | bytes accessed | tf_op | source)
XLA Modules:
  0.0 69.5 jit_solution(7373841414142528552)
XLA Ops:
  0.6 0.0 copy-start
  0.6 0.0 copy-start.1
  0.7 7.6 %extract.1 = (bf16[16,128,128]{2,1,0:T(8,128)(2,1)}, f32[4,8,2,32,128]{4,3,2,1,0:T(8,128)}, bf16[2,8,2,32,128]{4,3,2,1,0:T(8,128)(2,1)}, bf16[8,512,128]{2,1,0:T(8,128)(2,1)}) custom-call(s32[8]{0:T(128)} %off2_ref.7, s32[8]{0:T(128)} %off3_ref.7, bf16[32,2,16,1024]{3,2,1,0:T(8,128)(2,1)} %bitcast.8, bf16[32,2,16,1024]{3,2,1,0:T(8,128)(2,1)} %bitcast.9, ...), custom_call_target="tpu_custom_call" | custom-call | flops 4294967296 | bytes 12582912 | tf_op jit(solution)/shard_map/extract/pallas_call | solution.py:206
  8.3 6.8 %all-to-all-start = ((bf16[16,128,128]{2,1,0:T(8,128)(2,1)}), bf16[16,128,128]{2,1,0:T(8,128)(2,1)S(1)}, u32[]{:S(2)}, u32[]{:S(2)}) async-start(bf16[16,128,128]{2,1,0:T(8,128)(2,1)} %get-tuple-element.54), calls=%async_computation | async-start | bytes 1048576 | tf_op jit(solution)/shard_map/all_to_all | solution.py:679
  15.1 0.0 copy-done
  15.1 0.0 copy-done.1
  15.1 9.3 %local.3 = (bf16[2,16,2,16,1024]{4,3,2,1,0:T(8,128)(2,1)}, bf16[2,16,2,16,1024]{4,3,2,1,0:T(8,128)(2,1)}, bf16[8,1024,128]{2,1,0:T(8,128)(2,1)}, bf16[8,1024,128]{2,1,0:T(8,128)(2,1)}) custom-call(s32[8]{0:T(128)S(1)} %copy-done, s32[8]{0:T(128)S(1)} %copy-done.1, bf16[1024,1024]{1,0:T(8,128)(2,1)} %refs_2_.5, bf16[1024,1024]{1,0:T(8,128)(2,1)} %refs_3_.5, ...), custom_call_target="tpu_custom_call" | custom-call | flops 4026531840 | bytes 5242880 | tf_op jit(solution)/shard_map/local/pallas_call | solution.py:290
  24.4 0.3 all-to-all-done.in_ref
  24.7 1.9 %remote_forward.1 = (bf16[8,112,128]{2,1,0:T(8,128)(2,1)}, bf16[256,128]{1,0:T(8,128)(2,1)S(1)}, f32[256,128]{1,0:T(8,128)S(1)}) custom-call(s32[8]{0:T(128)S(1)} %copy-done, s32[8]{0:T(128)S(1)} %copy-done.1, bf16[16,128,128]{2,1,0:T(8,128)(2,1)S(1)} %all-to-all-done.in_ref), custom_call_target="tpu_custom_call" | custom-call | flops 2147483648 | bytes 2097152 | tf_op jit(solution)/shard_map/remote_forward/pallas_call | solution.py:435
  26.7 7.4 %all-to-all-start.1 = ((bf16[8,112,128]{2,1,0:T(8,128)(2,1)}), bf16[8,112,128]{2,1,0:T(8,128)(2,1)S(1)}, u32[]{:S(2)}, u32[]{:S(2)}) async-start(bf16[8,112,128]{2,1,0:T(8,128)(2,1)} %get-tuple-element.65), calls=%async_computation.1 | async-start | bytes 458752 | tf_op jit(solution)/shard_map/all_to_all | solution.py:684
  34.0 9.3 %local.4 = (bf16[2,16,2,16,1024]{4,3,2,1,0:T(8,128)(2,1)}, bf16[2,16,2,16,1024]{4,3,2,1,0:T(8,128)(2,1)}, bf16[8,1024,128]{2,1,0:T(8,128)(2,1)}, bf16[8,1024,128]{2,1,0:T(8,128)(2,1)}) custom-call(s32[8]{0:T(128)S(1)} %copy-done, s32[8]{0:T(128)S(1)} %copy-done.1, ...), custom_call_target="tpu_custom_call", output_to_operand_aliasing={{0}: (6, {}), {1}: (7, {}), {2}: (8, {}), {3}: (9, {})} | custom-call | flops 4026531840 | bytes 5242880 | tf_op jit(solution)/shard_map/local/pallas_call | solution.py:290
  43.3 0.0 all-to-all-done.1.far_ref
  43.3 2.7 %remote_backward.1 = bf16[16,128,128]{2,1,0:T(8,128)(2,1)} custom-call(s32[8]{0:T(128)S(1)} %copy-done, s32[8]{0:T(128)S(1)} %copy-done.1, bf16[16,128,128]{2,1,0:T(8,128)(2,1)S(1)} %all-to-all-done.in_ref, bf16[8,112,128]{2,1,0:T(8,128)(2,1)S(1)} %all-to-all-done.1.far_ref, bf16[256,128]{1,0:T(8,128)(2,1)S(1)} %get-tuple-element.75.out2_ref, ...), custom_call_target="tpu_custom_call" | custom-call | flops 2147483648 | bytes 2097152 | tf_op jit(solution)/shard_map/remote_backward/pallas_call | solution.py:435
  46.1 5.1 %all-to-all-start.2 = ((bf16[16,128,128]{2,1,0:T(8,128)(2,1)}), bf16[16,128,128]{2,1,0:T(8,128)(2,1)S(1)}, u32[]{:S(2)}, u32[]{:S(2)}) async-start(bf16[16,128,128]{2,1,0:T(8,128)(2,1)} %remote_backward.1), calls=%async_computation.2 | async-start | bytes 1048576 | tf_op jit(solution)/shard_map/all_to_all | solution.py:689
  51.2 10.7 %local.5 = (bf16[2,16,2,16,1024]{4,3,2,1,0:T(8,128)(2,1)}, bf16[2,16,2,16,1024]{4,3,2,1,0:T(8,128)(2,1)}, bf16[8,1024,128]{2,1,0:T(8,128)(2,1)}, bf16[8,1024,128]{2,1,0:T(8,128)(2,1)}) custom-call(s32[8]{0:T(128)S(1)} %copy-done, s32[8]{0:T(128)S(1)} %copy-done.1, ...), custom_call_target="tpu_custom_call", output_to_operand_aliasing={{0}: (6, {}), {1}: (7, {}), {2}: (8, {}), {3}: (9, {})} | custom-call | flops 4831838208 | bytes 6291456 | tf_op jit(solution)/shard_map/local/pallas_call | solution.py:290
  61.9 0.0 all-to-all-done.2.back_ref
  61.9 7.6 %finish.1 = (bf16[2,16,2,16,1024]{4,3,2,1,0:T(8,128)(2,1)}, bf16[2,16,2,16,1024]{4,3,2,1,0:T(8,128)(2,1)}, bf16[1024,1024]{1,0:T(8,128)(2,1)}, bf16[1024,1024]{1,0:T(8,128)(2,1)}) custom-call(s32[8]{0:T(128)S(1)} %copy-done, s32[8]{0:T(128)S(1)} %copy-done.1, ...), custom_call_target="tpu_custom_call", output_to_operand_aliasing={{0}: (6, {}), {1}: (7, {})} | custom-call | flops 1073741824 | bytes 17825792 | tf_op jit(solution)/shard_map/finish/pallas_call | solution.py:643
Async XLA Ops:
  0.6 14.5 %copy-start = (s32[8]{0:T(128)S(1)}, s32[8]{0:T(128)}, u32[]{:S(2)}) copy-start(s32[8]{0:T(128)} %off2_ref.7) | copy-start | bytes 100
  0.6 14.5 %copy-start.1 = (s32[8]{0:T(128)S(1)}, s32[8]{0:T(128)}, u32[]{:S(2)}) copy-start(s32[8]{0:T(128)} %off3_ref.7) | copy-start | bytes 100
  8.3 16.5 %all-to-all-start = ((bf16[16,128,128]{2,1,0:T(8,128)(2,1)}), bf16[16,128,128]{2,1,0:T(8,128)(2,1)S(1)}, u32[]{:S(2)}, u32[]{:S(2)}) async-start(bf16[16,128,128]{2,1,0:T(8,128)(2,1)} %get-tuple-element.54), calls=%async_computation | async-start | bytes 1048576 | tf_op jit(solution)/shard_map/all_to_all | solution.py:679
  26.7 16.7 %all-to-all-start.1 = ((bf16[8,112,128]{2,1,0:T(8,128)(2,1)}), bf16[8,112,128]{2,1,0:T(8,128)(2,1)S(1)}, u32[]{:S(2)}, u32[]{:S(2)}) async-start(bf16[8,112,128]{2,1,0:T(8,128)(2,1)} %get-tuple-element.65), calls=%async_computation.1 | async-start | bytes 458752 | tf_op jit(solution)/shard_map/all_to_all | solution.py:684
  46.1 15.8 %all-to-all-start.2 = ((bf16[16,128,128]{2,1,0:T(8,128)(2,1)}), bf16[16,128,128]{2,1,0:T(8,128)(2,1)S(1)}, u32[]{:S(2)}, u32[]{:S(2)}) async-start(bf16[16,128,128]{2,1,0:T(8,128)(2,1)} %remote_backward.1), calls=%async_computation.2 | async-start | bytes 1048576 | tf_op jit(solution)/shard_map/all_to_all | solution.py:689

commit v6 on v5

--- a/solution.py
+++ b/solution.py
@@ -654,7 +654,7 @@
             pltpu.VMEM(kind, BF16),
             pltpu.VMEM((2, HEADS, 2, MID, HALF, WIDTH), BF16),
             pltpu.VMEM((2, HEADS, 2, HALF, WIDTH), BF16),
-            pltpu.VMEM((2, 2 * MID * HALF + 8, WIDTH), F32),
+            pltpu.VMEM((2, 2 * MID * HALF + HALF, WIDTH), F32),
             pltpu.SemaphoreType.DMA((2,)),
             pltpu.SemaphoreType.DMA((HEADS, 3)),
             pltpu.SemaphoreType.DMA((HEADS, 2)),

time: 70.5 us -> 70.5 us (level)
  no operation moved by 1% of the time
where the time goes in v6:
time: 70.5 us; the launch traced here: 69.5 us
  Pallas kernels  49.2 us (70%)
  starting transfers between devices  19.3 us (27%)
  between operations  0.71 us (1%)
    pallas_call x3, Pallas kernels, local(): pl.pallas_call(lambda *refs: local_kernel(first, count, len(earlier), *re...  29.3 us
    pallas_call x1, Pallas kernels, extract(): pl.pallas_call(extract_kernel, in_specs=[smem, smem] + [hbm] * 4, out_spe...  7.61 us
    pallas_call x1, Pallas kernels, finish(): pl.pallas_call(finish_kernel, in_specs=[smem, smem, hbm, hbm, pl.BlockSpe...  7.6 us
    all_to_all x1, starting transfers between devices, body(): far = lax.all_to_all(far, 'outer', 0, 0)  7.37 us
    all_to_all x1, starting transfers between devices, body(): got = lax.all_to_all(send, 'inner', 0, 0)  6.84 us
    all_to_all x1, starting transfers between devices, body(): back = lax.all_to_all(back, 'inner', 0, 0)  5.11 us
    pallas_call x2, Pallas kernels, remote_call(): pl.pallas_call(kernel, in_specs=[smem, smem] + [vmem] * len(arrays), out_...  4.66 us
  transfers between devices with their start and end apart: 3, of which 1 were waited for; matrix products, arithmetic and copies ran while one was open for 0% of the time, Pallas kernels for 42%

profile of v6, /device:TPU:1, one launch (start us, length us, event | category | flops | bytes accessed | tf_op | source)
XLA Modules:
  0.0 69.5 jit_solution(18345345340305991654)
XLA Ops:
  0.6 0.0 copy-start
  0.6 0.0 copy-start.1
  0.7 7.6 %extract.1 = (bf16[16,128,128]{2,1,0:T(8,128)(2,1)}, f32[4,8,2,32,128]{4,3,2,1,0:T(8,128)}, bf16[2,8,2,32,128]{4,3,2,1,0:T(8,128)(2,1)}, bf16[8,512,128]{2,1,0:T(8,128)(2,1)}) custom-call(s32[8]{0:T(128)} %off2_ref.7, s32[8]{0:T(128)} %off3_ref.7, bf16[32,2,16,1024]{3,2,1,0:T(8,128)(2,1)} %bitcast.8, bf16[32,2,16,1024]{3,2,1,0:T(8,128)(2,1)} %bitcast.9, ...), custom_call_target="tpu_custom_call" | custom-call | flops 4294967296 | bytes 12582912 | tf_op jit(solution)/shard_map/extract/pallas_call | solution.py:206
  8.3 6.8 %all-to-all-start = ((bf16[16,128,128]{2,1,0:T(8,128)(2,1)}), bf16[16,128,128]{2,1,0:T(8,128)(2,1)S(1)}, u32[]{:S(2)}, u32[]{:S(2)}) async-start(bf16[16,128,128]{2,1,0:T(8,128)(2,1)} %get-tuple-element.54), calls=%async_computation | async-start | bytes 1048576 | tf_op jit(solution)/shard_map/all_to_all | solution.py:679
  15.1 0.0 copy-done
  15.1 0.0 copy-done.1
  15.1 9.3 %local.3 = (bf16[2,16,2,16,1024]{4,3,2,1,0:T(8,128)(2,1)}, bf16[2,16,2,16,1024]{4,3,2,1,0:T(8,128)(2,1)}, bf16[8,1024,128]{2,1,0:T(8,128)(2,1)}, bf16[8,1024,128]{2,1,0:T(8,128)(2,1)}) custom-call(s32[8]{0:T(128)S(1)} %copy-done, s32[8]{0:T(128)S(1)} %copy-done.1, bf16[1024,1024]{1,0:T(8,128)(2,1)} %refs_2_.5, bf16[1024,1024]{1,0:T(8,128)(2,1)} %refs_3_.5, ...), custom_call_target="tpu_custom_call" | custom-call | flops 4026531840 | bytes 5242880 | tf_op jit(solution)/shard_map/local/pallas_call | solution.py:290
  24.4 0.3 all-to-all-done.in_ref
  24.7 1.9 %remote_forward.1 = (bf16[8,112,128]{2,1,0:T(8,128)(2,1)}, bf16[256,128]{1,0:T(8,128)(2,1)S(1)}, f32[256,128]{1,0:T(8,128)S(1)}) custom-call(s32[8]{0:T(128)S(1)} %copy-done, s32[8]{0:T(128)S(1)} %copy-done.1, bf16[16,128,128]{2,1,0:T(8,128)(2,1)S(1)} %all-to-all-done.in_ref), custom_call_target="tpu_custom_call" | custom-call | flops 2147483648 | bytes 2097152 | tf_op jit(solution)/shard_map/remote_forward/pallas_call | solution.py:435
  26.7 7.4 %all-to-all-start.1 = ((bf16[8,112,128]{2,1,0:T(8,128)(2,1)}), bf16[8,112,128]{2,1,0:T(8,128)(2,1)S(1)}, u32[]{:S(2)}, u32[]{:S(2)}) async-start(bf16[8,112,128]{2,1,0:T(8,128)(2,1)} %get-tuple-element.65), calls=%async_computation.1 | async-start | bytes 458752 | tf_op jit(solution)/shard_map/all_to_all | solution.py:684
  34.0 9.3 %local.4 = (bf16[2,16,2,16,1024]{4,3,2,1,0:T(8,128)(2,1)}, bf16[2,16,2,16,1024]{4,3,2,1,0:T(8,128)(2,1)}, bf16[8,1024,128]{2,1,0:T(8,128)(2,1)}, bf16[8,1024,128]{2,1,0:T(8,128)(2,1)}) custom-call(s32[8]{0:T(128)S(1)} %copy-done, s32[8]{0:T(128)S(1)} %copy-done.1, ...), custom_call_target="tpu_custom_call", output_to_operand_aliasing={{0}: (6, {}), {1}: (7, {}), {2}: (8, {}), {3}: (9, {})} | custom-call | flops 4026531840 | bytes 5242880 | tf_op jit(solution)/shard_map/local/pallas_call | solution.py:290
  43.3 0.0 all-to-all-done.1.far_ref
  43.3 2.7 %remote_backward.1 = bf16[16,128,128]{2,1,0:T(8,128)(2,1)} custom-call(s32[8]{0:T(128)S(1)} %copy-done, s32[8]{0:T(128)S(1)} %copy-done.1, bf16[16,128,128]{2,1,0:T(8,128)(2,1)S(1)} %all-to-all-done.in_ref, bf16[8,112,128]{2,1,0:T(8,128)(2,1)S(1)} %all-to-all-done.1.far_ref, bf16[256,128]{1,0:T(8,128)(2,1)S(1)} %get-tuple-element.75.out2_ref, ...), custom_call_target="tpu_custom_call" | custom-call | flops 2147483648 | bytes 2097152 | tf_op jit(solution)/shard_map/remote_backward/pallas_call | solution.py:435
  46.1 5.1 %all-to-all-start.2 = ((bf16[16,128,128]{2,1,0:T(8,128)(2,1)}), bf16[16,128,128]{2,1,0:T(8,128)(2,1)S(1)}, u32[]{:S(2)}, u32[]{:S(2)}) async-start(bf16[16,128,128]{2,1,0:T(8,128)(2,1)} %remote_backward.1), calls=%async_computation.2 | async-start | bytes 1048576 | tf_op jit(solution)/shard_map/all_to_all | solution.py:689
  51.2 10.7 %local.5 = (bf16[2,16,2,16,1024]{4,3,2,1,0:T(8,128)(2,1)}, bf16[2,16,2,16,1024]{4,3,2,1,0:T(8,128)(2,1)}, bf16[8,1024,128]{2,1,0:T(8,128)(2,1)}, bf16[8,1024,128]{2,1,0:T(8,128)(2,1)}) custom-call(s32[8]{0:T(128)S(1)} %copy-done, s32[8]{0:T(128)S(1)} %copy-done.1, ...), custom_call_target="tpu_custom_call", output_to_operand_aliasing={{0}: (6, {}), {1}: (7, {}), {2}: (8, {}), {3}: (9, {})} | custom-call | flops 4831838208 | bytes 6291456 | tf_op jit(solution)/shard_map/local/pallas_call | solution.py:290
  61.9 0.0 all-to-all-done.2.back_ref
  61.9 7.6 %finish.1 = (bf16[2,16,2,16,1024]{4,3,2,1,0:T(8,128)(2,1)}, bf16[2,16,2,16,1024]{4,3,2,1,0:T(8,128)(2,1)}, bf16[1024,1024]{1,0:T(8,128)(2,1)}, bf16[1024,1024]{1,0:T(8,128)(2,1)}) custom-call(s32[8]{0:T(128)S(1)} %copy-done, s32[8]{0:T(128)S(1)} %copy-done.1, ...), custom_call_target="tpu_custom_call", output_to_operand_aliasing={{0}: (6, {}), {1}: (7, {})} | custom-call | flops 1073741824 | bytes 17825792 | tf_op jit(solution)/shard_map/finish/pallas_call | solution.py:643
Async XLA Ops:
  0.6 14.5 %copy-start = (s32[8]{0:T(128)S(1)}, s32[8]{0:T(128)}, u32[]{:S(2)}) copy-start(s32[8]{0:T(128)} %off2_ref.7) | copy-start | bytes 100
  0.6 14.5 %copy-start.1 = (s32[8]{0:T(128)S(1)}, s32[8]{0:T(128)}, u32[]{:S(2)}) copy-start(s32[8]{0:T(128)} %off3_ref.7) | copy-start | bytes 100
  8.3 16.5 %all-to-all-start = ((bf16[16,128,128]{2,1,0:T(8,128)(2,1)}), bf16[16,128,128]{2,1,0:T(8,128)(2,1)S(1)}, u32[]{:S(2)}, u32[]{:S(2)}) async-start(bf16[16,128,128]{2,1,0:T(8,128)(2,1)} %get-tuple-element.54), calls=%async_computation | async-start | bytes 1048576 | tf_op jit(solution)/shard_map/all_to_all | solution.py:679
  26.7 16.7 %all-to-all-start.1 = ((bf16[8,112,128]{2,1,0:T(8,128)(2,1)}), bf16[8,112,128]{2,1,0:T(8,128)(2,1)S(1)}, u32[]{:S(2)}, u32[]{:S(2)}) async-start(bf16[8,112,128]{2,1,0:T(8,128)(2,1)} %get-tuple-element.65), calls=%async_computation.1 | async-start | bytes 458752 | tf_op jit(solution)/shard_map/all_to_all | solution.py:684
  46.1 15.8 %all-to-all-start.2 = ((bf16[16,128,128]{2,1,0:T(8,128)(2,1)}), bf16[16,128,128]{2,1,0:T(8,128)(2,1)S(1)}, u32[]{:S(2)}, u32[]{:S(2)}) async-start(bf16[16,128,128]{2,1,0:T(8,128)(2,1)} %remote_backward.1), calls=%async_computation.2 | async-start | bytes 1048576 | tf_op jit(solution)/shard_map/all_to_all | solution.py:689
